TPU v7x, 128 devices: a whole 4x4x4 slice. The times are simulated.
128 devices in a mesh: dp: 32 (over x, z_hi, y), tensor: 4 (over z_lo, core).
Axes of the slice: x: 4, y: 4, z: 4 (z_hi: 2, z_lo: 2; z = z_hi * 2 + z_lo), core: 2. Of those that a mesh axis runs over, the one named last changes fastest.
Arguments:
- block_in: bfloat16 [16384, 1536], P(('dp', 'tensor')), may hold values from -6 to 6
- out_grad: bfloat16 [16384, 1536], P(('dp', 'tensor')), may hold values from -6 to 6
- condition: bfloat16 [96, 1024], P('dp'), may hold values from -6 to 6
- captions: bfloat16 [96, 256, 4096], P('dp'), may hold values from -6 to 6
- caption_len: int32 [96], P('dp'), may hold values from 64 to 256
- segment_ids: int32 [16384], P('dp'), may hold values from 0 to 2, as said below
- ada_weight: bfloat16 [1024, 6144], P(None, 'tensor'), may hold values from -0.1875 to 0.1875
- norm_gains: float32 [4, 1536], replicated, may hold values from 0.25 to 1.75
- query_weight: bfloat16 [1536, 1536], P(None, 'tensor'), may hold values from -0.15625 to 0.15625
- key_weight: bfloat16 [1536, 1536], P(None, 'tensor'), may hold values from -0.15625 to 0.15625
- value_weight: bfloat16 [1536, 1536], P(None, 'tensor'), may hold values from -0.15625 to 0.15625
- head_gains: float32 [3, 64], replicated, may hold values from 0.25 to 1.75
- textkey_weight: bfloat16 [4096, 1536], P(None, 'tensor'), may hold values from -0.09375 to 0.09375
- textvalue_weight: bfloat16 [4096, 1536], P(None, 'tensor'), may hold values from -0.09375 to 0.09375
- cross_gate: float32 [24], P('tensor'), may hold values from 0.3 to 1.5
- out_weight: bfloat16 [1536, 1536], P('tensor'), may hold values from -0.15625 to 0.15625
- gate_weight: bfloat16 [1536, 4096], P(None, 'tensor'), may hold values from -0.15625 to 0.15625
- up_weight: bfloat16 [1536, 4096], P(None, 'tensor'), may hold values from -0.15625 to 0.15625
- down_weight: bfloat16 [4096, 1536], P('tensor'), may hold values from -0.09375 to 0.09375
Outputs:
- block_out: bfloat16 [16384, 1536], P(('dp', 'tensor'))
- in_grad: bfloat16 [16384, 1536], P(('dp', 'tensor'))
- ada_grad: float32 [1024, 6144], P('dp', 'tensor')
- norm_grads: float32 [4, 1536], replicated
- query_grad: float32 [1536, 1536], P('dp', 'tensor')
- key_grad: float32 [1536, 1536], P('dp', 'tensor')
- value_grad: float32 [1536, 1536], P('dp', 'tensor')
- head_grads: float32 [3, 64], replicated
- textkey_grad: float32 [4096, 1536], P('dp', 'tensor')
- textvalue_grad: float32 [4096, 1536], P('dp', 'tensor')
- crossgate_grad: float32 [24], replicated
- outw_grad: float32 [1536, 1536], P('tensor', 'dp')
- gate_grad: float32 [1536, 4096], P('dp', 'tensor')
- up_grad: float32 [1536, 4096], P('dp', 'tensor')
- down_grad: float32 [4096, 1536], P('tensor', 'dp')
Inputs may be any that keep to these rules, and one draw needn't show every extreme that they name: `segment_ids`: within each sequence the ids never fall, every one of 0 to 2 holds one run of rows, and one segment is longer than 384.
All inputs are finite; a program needn't handle non-finite values.
Results may differ from a plain program's by a relative error of at most 0.025.
Values may be sent and summed in bfloat16 or wider, within the bound.
No kernel may reach another device: no remote copies, remote signals or barrier semaphores. Data moves between devices by JAX's collectives and lax.ppermute only.
A program may use at most 192 MiB of HBM per device.

v0:
```python
import functools
import math

import jax
import jax.numpy as jnp
from jax import lax
from jax.experimental import pallas as pl
from jax.experimental.pallas import tpu as pltpu
from jax.sharding import PartitionSpec as P

HEAD = 64
HEADS = 24
TXT = 256
SEGS = 3
EPS = 1e-06
LANES = 2 * HEAD
SHUT = 256.0
ROOT = HEAD ** (-0.5)
VMEM_LIMIT = 24 * 2**20
NO_COST = pl.CostEstimate(flops=0, bytes_accessed=0, transcendentals=0)


def cost_of(micros):
    return pl.CostEstimate(flops=int(micros * 1e9), bytes_accessed=0, transcendentals=0)


SUM_ROWS = 6
CROSS_MICROS = 10
BLOCK_IN_MICROS = 0
FFN_MICROS = 3
FFN_NEXT_MICROS = 8
MIDDLE_MICROS = 10
SELF_MICROS = 0
ATTN_MICROS = 7
TEXT_MICROS = 8
ATTN_FIRST_MICROS = 0

RING = 4
PAIR = 2
BLOCKS = RING * PAIR * RING
SLOTS = BLOCKS // RING
SEND_ORDER = (2, 1, 3, 0)
CORE_SWAP = [(0, 1), (1, 0), (2, 3), (3, 2)]
CHIP_SWAP = [(0, 2), (2, 0), (1, 3), (3, 1)]
ROW_ORDER = (0, 2, 1, 3)

def dp_index(x, z, y):
    return (x * PAIR + z) * RING + y


def dp_perm(axis, step):
    pairs = []
    for x in range(RING):
        for z in range(PAIR):
            for y in range(RING):
                for tensor in range(2 * PAIR):
                    way = axis
                    if axis in ("first", "second"):
                        way = "x" if (tensor % 2 == 0) == (axis == "first") else "y"
                    target = {
                        "x": ((x + step) % RING, z, y),
                        "y": (x, z, (y + step) % RING),
                        "z": (x, (z + step) % PAIR, y),
                    }[way]
                    pairs.append(
                        (
                            dp_index(x, z, y) * 2 * PAIR + tensor,
                            dp_index(*target) * 2 * PAIR + tensor,
                        )
                    )
    return pairs


def dp_permute(values, axis, step):
    return lax.ppermute(values, ("dp", "tensor"), dp_perm(axis, step))


def dp_spot(position):
    index = lax.axis_index("dp")
    x, z, y = index // (RING * PAIR), index // RING % PAIR, index % RING
    core = position % 2
    return jnp.stack([jnp.where(core == 0, x, y), z, jnp.where(core == 0, y, x), core])


def swap_core(values):
    return lax.ppermute(values, "tensor", CORE_SWAP)


def swap_chip(values):
    return lax.ppermute(values, "tensor", CHIP_SWAP)


def times_transpose(left, right):
    return lax.dot_general(
        left, right, (((1,), (1,)), ((), ())), preferred_element_type=jnp.float32
    )


def gather_tensor(block):
    far = swap_chip(block)
    near = swap_core(block)
    return [block, far, near, swap_core(far)]


def scatter_tensor(upper, lower):
    near = swap_core(lower)
    rows = upper.shape[0] // 2
    far = (upper[rows:].astype(jnp.float32) + near[rows:].astype(jnp.float32)).astype(near.dtype)
    return [upper, near, swap_chip(far)], far


def turn_kernel(source, target):
    target[...] = source[...].T


def turned(values, ties=()):
    tile = 512 if values.shape[1] % 512 == 0 else values.shape[1]
    return pl.pallas_call(
        lambda source, *rest: turn_kernel(source, rest[-1]),
        grid=(values.shape[1] // tile,),
        in_specs=[pl.BlockSpec((values.shape[0], tile), lambda step: (0, step))]
        + [pl.BlockSpec(memory_space=pl.ANY)] * len(ties),
        out_specs=pl.BlockSpec((tile, values.shape[0]), lambda step: (step, 0)),
        out_shape=jax.ShapeDtypeStruct(values.shape[::-1], values.dtype),
        compiler_params=pltpu.CompilerParams(vmem_limit_bytes=VMEM_LIMIT),
        cost_estimate=NO_COST,
    )(values, *ties)


def chunk_block(offset, slot, spot):
    first = (spot[0] + offset) % RING
    z, second = slot // RING, slot % RING
    x = jnp.where(spot[3] == 0, first, second)
    y = jnp.where(spot[3] == 0, second, first)
    return dp_index(x, z, y)


def offset_of_step(offsets, step):
    offset = offsets[-1]
    for place in range(len(offsets) - 1):
        offset = jnp.where(step == place, offsets[place], offset)
    return offset


def chunk_kernel(make, offsets, halves, extra, outs, held, sems):
    step = pl.program_id(0)
    first, second = halves

    def copies(place):
        slot = held.at[place % 2]
        if offsets[place] != 2:
            return [pltpu.make_async_copy(slot, outs[place], sems.at[place % 2, 0])]
        return [
            pltpu.make_async_copy(slot.at[half], out, sems.at[place % 2, way])
            for way, (half, out) in enumerate(zip((first, second), outs[place]))
        ]

    for place, offset in enumerate(offsets):

        @pl.when(step == place)
        def _(place=place, offset=offset):
            if place >= 2:
                for copy in copies(place - 2):
                    copy.wait()
            added = {1: (first, extra[0]), 3: (second, extra[1])}.get(offset) if extra else None
            make(held.at[place % 2], added, offset)
            for copy in copies(place):
                copy.start()
            if place == len(offsets) - 1:
                for last in range(max(place - 1, 0), place + 1):
                    for copy in copies(last):
                        copy.wait()


def chunk_call(make, operands, specs, offsets, halves, shape, spot, extra, ties, name, micros):
    count = len(operands)
    pieces = []
    for offset in offsets:
        if offset == 2:
            pieces += [tuple(len(range(*s.indices(d))) for s, d in zip(h, shape)) for h in halves]
        else:
            pieces.append(shape)

    def kernel(spot_ref, *refs):
        inputs, extras = refs[:count], refs[count : count + len(extra)]
        outs = list(refs[-len(pieces) - 2 : -2])
        grouped = []
        for offset in offsets:
            grouped.append((outs.pop(0), outs.pop(0)) if offset == 2 else outs.pop(0))
        chunk_kernel(
            functools.partial(make, inputs), offsets, halves, extras, grouped, refs[-2], refs[-1]
        )

    found = pl.pallas_call(
        kernel,
        grid_spec=pltpu.PrefetchScalarGridSpec(
            num_scalar_prefetch=1,
            grid=(len(offsets),),
            in_specs=list(specs)
            + [pl.BlockSpec(part.shape, lambda step, spot: (0, 0)) for part in extra]
            + [pl.BlockSpec(memory_space=pl.ANY)] * len(ties),
            out_specs=[pl.BlockSpec(memory_space=pl.ANY)] * len(pieces),
            scratch_shapes=[
                pltpu.VMEM((2,) + shape, jnp.bfloat16),
                pltpu.SemaphoreType.DMA((2, 2)),
            ],
        ),
        out_shape=[jax.ShapeDtypeStruct(piece, jnp.bfloat16) for piece in pieces],
        compiler_params=pltpu.CompilerParams(vmem_limit_bytes=VMEM_LIMIT),
        cost_estimate=cost_of(micros),
        name=name,
    )(spot, *operands, *extra, *ties)
    found = list(found)
    return [
        (found.pop(0), found.pop(0)) if offset == 2 else found.pop(0) for offset in offsets
    ]


def make_rows(groups, inputs, slot, added, offset):
    lefts, rights = inputs[: SLOTS * len(groups)], inputs[SLOTS * len(groups) :]
    size = SLOTS * lefts[0].shape[1]
    if len(rights) > sum(groups):
        riders = rights[-1][...]
        count, half = riders.shape[0], riders.shape[1] // 2
        first, second = slice(size, size + count), slice(size + count, size + 2 * count)
        if offset == 2:
            for side in (slice(0, half), slice(half, 2 * half)):
                slot[first, side] = riders[:, :half]
                slot[second, side] = riders[:, half:]
        else:
            slot[first, :] = riders
            if offset == 1:
                slot[second, :half] = added[1][first, :]
                slot[second, half:] = added[1][second, :]
            else:
                slot[second, :] = riders
    column = place = 0
    for group, count in enumerate(groups):
        rows = jnp.concatenate(
            [left[0] for left in lefts[SLOTS * group : SLOTS * (group + 1)]], axis=0
        )
        for right in rights[place : place + count]:
            wide = right.shape[1]
            product = dot(rows, right[...])
            low, high = column, column
            if added is not None:
                low = min(max(column, added[0][1].start), column + wide)
                high = min(max(column, added[0][1].stop), column + wide)
            for start, stop in ((column, low), (low, high), (high, column + wide)):
                if start < stop:
                    part = product[:, start - column : stop - column]
                    if (start, stop) == (low, high):
                        base = added[0][1].start
                        part = part + added[1][:size, start - base : stop - base].astype(jnp.float32)
                    slot[:size, start:stop] = part.astype(jnp.bfloat16)
            column += wide
        place += count


def row_chunks(pairs, offsets, spot, extra=(), ties=(), micros=0, riders=()):
    lefts = [left.reshape(BLOCKS, left.shape[0] // BLOCKS, left.shape[1]) for left, _ in pairs]
    rights = [right for _, group in pairs for right in group]
    total = sum(right.shape[1] for right in rights)
    specs, operands = [], []
    for left in lefts:
        for slot in range(SLOTS):
            specs.append(
                pl.BlockSpec(
                    (1,) + left.shape[1:],
                    lambda step, spot, slot=slot: (
                        chunk_block(offset_of_step(offsets, step), slot, spot),
                        0,
                        0,
                    ),
                )
            )
            operands.append(left)
    specs += [pl.BlockSpec(right.shape, lambda step, spot: (0, 0)) for right in rights]
    specs += [pl.BlockSpec(part.shape, lambda step, spot: (0, 0)) for part in riders]
    rows = SLOTS * lefts[0].shape[1] + sum(2 * part.shape[0] for part in riders)
    halves = [(slice(0, rows), slice(0, total // 2)), (slice(0, rows), slice(total // 2, total))]
    return chunk_call(
        functools.partial(make_rows, [len(group) for _, group in pairs]),
        operands + rights + list(riders),
        specs,
        offsets,
        halves,
        (rows, total),
        spot,
        extra,
        ties,
        "row_chunks",
        micros,
    )


def make_columns(lefts, inputs, slot, added, offset):
    whole = jnp.concatenate([right[...] for right in inputs[lefts:]], axis=1)
    row = 0
    for left in inputs[:lefts]:
        product = dot(left[...], whole)
        if added is not None and added[0][0].start == row:
            product = product + added[1][...].astype(jnp.float32)
        slot[row : row + left.shape[0], :] = product.astype(jnp.bfloat16)
        row += left.shape[0]


def column_chunks(lefts, right, offsets, spot, extra=(), ties=(), micros=0):
    rows = lefts[0].shape[0]
    depth, columns = right.shape
    specs = [pl.BlockSpec(left.shape, lambda step, spot: (0, 0)) for left in lefts]
    for slot in range(SLOTS):
        specs.append(
            pl.BlockSpec(
                (depth, columns // BLOCKS),
                lambda step, spot, slot=slot: (
                    0,
                    chunk_block(offset_of_step(offsets, step), slot, spot),
                ),
            )
        )
    lanes = columns // RING
    halves = [(slice(0, rows), slice(0, lanes)), (slice(rows, 2 * rows), slice(0, lanes))]
    return chunk_call(
        functools.partial(make_columns, len(lefts)),
        list(lefts) + [right] * SLOTS,
        specs,
        offsets,
        halves,
        (2 * rows, lanes),
        spot,
        extra,
        ties,
        "column_chunks",
        micros,
    )


def add_up(refs, index):
    total = refs[0][index].astype(jnp.float32)
    for ref in refs[1:]:
        total = total + ref[index].astype(jnp.float32)
    return total


def lane_slice(start, size):
    return (slice(None), pl.ds(pl.multiple_of(start * size, size), size))


def ffn_second_kernel(spot, *refs):
    parts, outs = refs[:-RING], refs[-RING:]
    for offset in range(RING):
        for z in range(PAIR):
            slot = z * RING + (spot[2] + offset) % RING
            outs[offset][z] = add_up(parts, slot).astype(jnp.bfloat16)


def ffn_third_kernel(spot, *refs):
    for out, z in ((refs[-2], spot[1]), (refs[-1], (spot[1] + 1) % PAIR)):
        out[...] = add_up(refs[:RING], z).astype(jnp.bfloat16)


def ffn_last_kernel(kept, got, gate_out, up_out, down_out):
    total = kept[...].astype(jnp.float32) + got[...].astype(jnp.float32)
    hidden = gate_out.shape[1]
    gate_out[...] = total[:, :hidden]
    up_out[...] = total[:, hidden : 2 * hidden]
    down_out[...] = total[:, 2 * hidden :].T


def text_second_kernel(spot, *refs):
    parts, outs = refs[:-RING], refs[-RING:]
    lanes = parts[0].shape[1] // SLOTS
    for offset in range(RING):
        for z in range(PAIR):
            slot = z * RING + (spot[2] + offset) % RING
            outs[offset][:, z * lanes : (z + 1) * lanes] = add_up(
                parts, lane_slice(slot, lanes)
            ).astype(jnp.bfloat16)


def text_third_kernel(spot, *refs):
    lanes = refs[-1].shape[1]
    for out, z in ((refs[-2], spot[1]), (refs[-1], (spot[1] + 1) % PAIR)):
        out[...] = add_up(refs[:RING], lane_slice(z, lanes)).astype(jnp.bfloat16)


def text_last_kernel(kept, got, textkey, textvalue):
    total = kept[...].astype(jnp.float32) + got[...].astype(jnp.float32)
    columns = textkey.shape[1]
    textkey[...] = total[:columns].T
    textvalue[...] = total[columns:].T


def attn_second_kernel(rows, spot, riders, *refs):
    parts, outs = refs[:-RING], refs[-RING:]
    size, count = SLOTS * rows, riders.shape[0]
    for offset in range(RING):
        for z in range(PAIR):
            slot = z * RING + (spot[2] + offset) % RING
            index = (pl.ds(pl.multiple_of(slot * rows, 16), rows), slice(None))
            outs[offset][z * rows : (z + 1) * rows, :] = add_up(parts, index).astype(jnp.bfloat16)
    ahead, behind = parts[1], parts[2]
    pairs = (
        (riders[...], ahead[size : size + count, :]),
        (behind[size : size + count, :], ahead[size + count : size + 2 * count, :]),
    )
    joined = [merge_rows(PAIR, first, second, rider_rows(2 * PAIR)) for first, second in pairs]
    joined = merge_rows(2 * PAIR, joined[0], joined[1], rider_rows(4 * PAIR))
    for out in outs:
        out[PAIR * rows :, :] = joined


def attn_third_kernel(spot, *refs):
    rows = refs[-1].shape[0]
    for out, z in ((refs[-2], spot[1]), (refs[-1], (spot[1] + 1) % PAIR)):
        index = (pl.ds(pl.multiple_of(z * rows, 16), rows), slice(None))
        out[...] = add_up(refs[:RING], index).astype(jnp.bfloat16)


def attn_last_kernel(kept, got, query, key, value, outw):
    total = kept[...].astype(jnp.float32) + got[...].astype(jnp.float32)
    columns = query.shape[1]
    for place, out in enumerate((query, key, value)):
        out[...] = total[:, place * columns : (place + 1) * columns]
    outw[...] = total[:, 3 * columns :].T


def whole_call(kernel, scalars, operands, outs, name, ties=(), scratch=(), micros=0):
    whole = pl.BlockSpec(memory_space=pltpu.VMEM)
    count = len(scalars) + len(operands)
    return pl.pallas_call(
        lambda *refs: kernel(*refs[:count], *refs[count + len(ties) :]),
        in_specs=[pl.BlockSpec(memory_space=pltpu.SMEM)] * len(scalars)
        + [whole] * len(operands)
        + [pl.BlockSpec(memory_space=pl.ANY)] * len(ties),
        out_specs=[whole] * len(outs),
        out_shape=[jax.ShapeDtypeStruct(shape, kind) for shape, kind in outs],
        scratch_shapes=list(scratch),
        compiler_params=pltpu.CompilerParams(vmem_limit_bytes=VMEM_LIMIT),
        cost_estimate=cost_of(micros),
        name=name,
    )(*scalars, *operands, *ties)


def tiled_call(kernel, scalars, operands, outs, name, axis, tiles, ties=(), micros=0, axes=None):
    def spec(shape, axis):
        block = list(shape)
        block[axis] //= tiles
        if axis == 0:
            return pl.BlockSpec(tuple(block), lambda step: (step,) + (0,) * (len(shape) - 1))
        return pl.BlockSpec(tuple(block), lambda step: (0,) * (len(shape) - 1) + (step,))

    count = len(scalars) + len(operands)
    return pl.pallas_call(
        lambda *refs: kernel(*refs[:count], *refs[count + len(ties) :]),
        grid=(tiles,),
        in_specs=[pl.BlockSpec(memory_space=pltpu.SMEM)] * len(scalars)
        + [spec(part.shape, way) for part, way in zip(operands, axes or [axis] * len(operands))]
        + [pl.BlockSpec(memory_space=pl.ANY)] * len(ties),
        out_specs=[spec(shape, axis) for shape, _ in outs],
        out_shape=[jax.ShapeDtypeStruct(shape, kind) for shape, kind in outs],
        compiler_params=pltpu.CompilerParams(vmem_limit_bytes=VMEM_LIMIT),
        cost_estimate=cost_of(micros),
        name=name,
    )(*scalars, *[pltpu.with_memory_space_constraint(part, pltpu.HBM) for part in operands], *ties)


def exchange(chunks, axis):
    return [chunks[0]] + [
        dp_permute(chunks[step], axis, step) for step in range(1, len(chunks))
    ]


def one_on(halves):
    return dp_permute(halves[0], "first", 1), dp_permute(halves[1], "first", RING - 1)


def to_neighbours(own, ahead, behind):
    return [own, dp_permute(ahead, "first", 1), dp_permute(behind, "first", RING - 1)]


def by_slots(chunk):
    return chunk.reshape(SLOTS, chunk.shape[0] // SLOTS, chunk.shape[1])


def lane_index(shape):
    return lax.broadcasted_iota(jnp.int32, shape, 1)


def head_lanes(shape, head):
    lane = lane_index(shape)
    return (lane < HEAD) if head == 0 else (lane >= HEAD)


def per_head(values, reduce):
    first = head_lanes(values.shape, 0)
    left = jnp.sum(jnp.where(first, values, 0.0), axis=1, keepdims=True)
    right = jnp.sum(jnp.where(first, 0.0, values), axis=1, keepdims=True)
    return jnp.where(first, left, right)


def head_units(raw):
    inverse = lax.rsqrt(per_head(raw * raw, None) * (1.0 / HEAD) + EPS)
    return raw * inverse, inverse


def partner(values):
    lane = lane_index(values.shape)
    return jnp.where(
        lane % HEAD < HEAD // 2,
        pltpu.roll(values, LANES - HEAD // 2, 1),
        pltpu.roll(values, HEAD // 2, 1),
    )


def dot(left, right):
    return jnp.dot(left, right, preferred_element_type=jnp.float32)


def dot_t(left, right):
    return lax.dot_general(left, right, (((1,), (1,)), ((), ())), preferred_element_type=jnp.float32)


def attend_kernel(
    raw_q, raw_k, value, raw_t, text_value, cosine, sine, gains, gate, gate_swapped, mark_q, mark_k, mark_t,
    query_out, key_out, text_out, mixed_out, self_out, cross_out, self_log, cross_log,
):
    cos, sin = cosine[...], sine[...]
    unit = head_units(raw_q[...])[0] * gains[0:1, :]
    query = ((unit * cos + partner(unit) * sin).astype(jnp.bfloat16) * ROOT).astype(jnp.bfloat16)
    unit = head_units(raw_k[...])[0] * gains[1:2, :]
    key = (unit * cos + partner(unit) * sin).astype(jnp.bfloat16)
    text = (head_units(raw_t[...])[0] * gains[2:3, :]).astype(jnp.bfloat16)
    query_out[...] = query
    key_out[...] = key
    text_out[...] = text

    def attention(keys, marks, values):
        outs, sums = [], []
        for head in range(2):
            own = head_lanes(query.shape, head)
            own_keys = head_lanes(keys.shape, head)
            probe = jnp.where(own, query, mark_q[...])
            scores = dot_t(probe, jnp.where(own_keys, keys, marks))
            weights = jnp.exp(scores).astype(jnp.bfloat16)
            both = dot(weights, jnp.where(own_keys, values, jnp.ones_like(values)))
            outs.append(both)
        first = head_lanes(outs[0].shape, 0)
        product = jnp.where(first, outs[0], outs[1])
        total = jnp.where(first, outs[1], outs[0])
        return product / pltpu.roll(total, HEAD, 1), jnp.log(total)

    out, log = attention(key, mark_k[...], value[...])
    self_out[...] = out
    self_log[...] = log
    cross, log = attention(text, mark_t[...], text_value[...])
    cross_out[...] = cross
    cross_log[...] = log - jnp.log(gate_swapped[...])
    mixed_out[...] = (out + gate[...] * cross).astype(jnp.bfloat16)


def attention_grads(query, keys, marks, values, grad, out, log, mark_q):
    rows = grad.astype(jnp.float32)
    delta = per_head(rows * out, None)
    delta = pltpu.roll(delta, HEAD, 1)
    lane = lane_index(query.shape) % HEAD
    log_high = log.astype(jnp.bfloat16)
    log_low = (log - log_high.astype(jnp.float32)).astype(jnp.bfloat16)
    delta_high = delta.astype(jnp.bfloat16)
    delta_low = (delta - delta_high.astype(jnp.float32)).astype(jnp.bfloat16)
    zero = jnp.zeros_like(query)
    code = jnp.where(lane == 4, -log_high, jnp.where(lane == 5, -log_low, mark_q))
    shift = jnp.where(lane == 4, -delta_high, jnp.where(lane == 5, -delta_low, zero))
    key_grads, value_grads, query_grads = [], [], []
    for head in range(2):
        own = head_lanes(query.shape, head)
        own_keys = head_lanes(keys.shape, head)
        probe = jnp.where(own, query, code)
        probs = jnp.exp(dot_t(jnp.where(own_keys, keys, marks), probe))
        slope = dot_t(jnp.where(own_keys, values, marks), jnp.where(own, grad, shift))
        score_grad = (probs * slope).astype(jnp.bfloat16)
        value_grads.append(dot(probs.astype(jnp.bfloat16), grad))
        key_grads.append(dot(score_grad, query))
        turned = keys[:, head * HEAD : (head + 1) * HEAD].T
        query_grads.append(dot(turned, score_grad))
    first = head_lanes(keys.shape, 0)
    return (
        jnp.concatenate(query_grads, axis=0),
        jnp.where(first, key_grads[0], key_grads[1]),
        jnp.where(first, value_grads[0], value_grads[1]),
    )


def norm_back(weighted, unit, inverse):
    return inverse * (weighted - unit * (per_head(weighted * unit, None) * (1.0 / HEAD)))


def cross_back_kernel(
    query, text, text_value, raw_t, grad, out, log, gains, mark_q, mark_t,
    query_grad, raw_grad, value_grad, gain_sum, gate_sum,
):
    grad_q, grad_t, grad_v = attention_grads(
        query[...], text[...], mark_t[...], text_value[...], grad[...], out[...], log[...], mark_q[...]
    )
    query_grad[...] = grad_q.T
    value_grad[...] = grad_v.astype(jnp.bfloat16).T
    grad_t = grad_t.astype(jnp.bfloat16).astype(jnp.float32)
    unit, inverse = head_units(raw_t[...])
    gain_sum[...] = jnp.sum(grad_t * unit, axis=0, keepdims=True)
    raw_grad[...] = norm_back(grad_t * gains[2:3, :], unit, inverse).astype(jnp.bfloat16).T
    gate_sum[...] = jnp.sum(grad[...].astype(jnp.float32) * out[...], axis=0, keepdims=True)


def self_back_kernel(
    query, key, value, raw_q, raw_k, grad, out, log, cross_grad, cosine, sine, gains, mark_q, mark_k,
    query_grad, key_grad, value_grad, gain_sum,
):
    grad_q, grad_k, grad_v = attention_grads(
        query[...], key[...], mark_k[...], value[...], grad[...], out[...], log[...], mark_q[...]
    )
    value_grad[...] = grad_v.astype(jnp.bfloat16)
    cos, sin = cosine[...], sine[...]
    grad_q = (grad_q.T + cross_grad[...]) * ROOT
    for turn, raw, row, target in ((grad_q, raw_q, 0, query_grad), (grad_k, raw_k, 1, key_grad)):
        turn = turn.astype(jnp.bfloat16).astype(jnp.float32)
        turn = turn * cos - partner(turn) * sin
        unit, inverse = head_units(raw[...])
        gain_sum[row : row + 1, :] = jnp.sum(turn * unit, axis=0, keepdims=True)
        target[...] = norm_back(turn * gains[row : row + 1, :], unit, inverse).astype(jnp.bfloat16)


def pair_call(kernel, operands, outs, name, ties=(), micros=0):
    def spec(shape, cut):
        if cut is None:
            return pl.BlockSpec(shape, lambda pair: (0, 0))
        if cut == 1:
            return pl.BlockSpec((shape[0], LANES), lambda pair: (0, pair))
        return pl.BlockSpec((LANES, shape[1]), lambda pair: (pair, 0))

    width = outs[0][0][0] if outs[0][2] == 0 else outs[0][0][1]
    return pl.pallas_call(
        lambda *refs: kernel(*refs[: len(operands)], *refs[len(operands) + len(ties) :]),
        grid=(width // LANES,),
        in_specs=[spec(part.shape, cut) for part, cut in operands]
        + [pl.BlockSpec(memory_space=pl.ANY)] * len(ties),
        out_specs=[spec(shape, cut) for shape, _, cut in outs],
        out_shape=[jax.ShapeDtypeStruct(shape, kind) for shape, kind, _ in outs],
        compiler_params=pltpu.CompilerParams(vmem_limit_bytes=VMEM_LIMIT),
        cost_estimate=cost_of(micros),
        name=name,
    )(*[part for part, _ in operands], *ties)
def inverse_rms(values):
    return lax.rsqrt(jnp.mean(values * values, axis=-1, keepdims=True) + EPS)


def row_norm_back(weighted, unit, inverse):
    return inverse * (weighted - unit * jnp.mean(weighted * unit, axis=-1, keepdims=True))


def per_row(table, segment):
    return jnp.where(segment == 0.0, table[0:1], jnp.where(segment == 1.0, table[1:2], table[2:3]))


def total_of(parts):
    upper, near, far = parts
    rows = far.shape[0]
    return (
        upper[:rows].astype(jnp.float32) + near[:rows].astype(jnp.float32) + far[...].astype(jnp.float32)
    )


def segment_sums(member, values):
    high = values.astype(jnp.bfloat16)
    low = (values - high.astype(jnp.float32)).astype(jnp.bfloat16)
    return dot(member, high) + dot(member, low)


def tables_kernel(here, lens, gate, segments, head_gains, cosine, sine, mark_q, mark_k, mark_t,
                  segment, member, gate_lanes, gate_swapped, gains):
    heads = gains.shape[1] // HEAD
    lane = lane_index(gate_lanes.shape) // HEAD
    line = jnp.zeros(gate_lanes.shape, jnp.float32)
    swapped = line
    for head in range(heads):
        line = jnp.where(lane == head, gate[head], line)
        swapped = jnp.where(lane == head ^ 1, gate[head], swapped)
    gate_lanes[...] = jnp.tanh(line)
    gate_swapped[...] = jnp.tanh(swapped)
    gains[...] = jnp.concatenate([head_gains[...]] * heads, axis=1)
    rows = segments.shape[1]
    ids = segments[...]
    first = jnp.sum((ids < 1).astype(jnp.float32))
    second = jnp.sum((ids < 2).astype(jnp.float32))
    lane = lane_index((rows, LANES))
    half = HEAD // 2
    rate = jnp.exp((lane % half).astype(jnp.float32) * (-2.0 * math.log(10000.0) / HEAD))
    within = lane % HEAD
    for block, code in enumerate(ROW_ORDER):
        source = here[0] ^ code
        line = segments[pl.ds(source, 1), :].astype(jnp.float32)
        label = jnp.broadcast_to(line, (rows, rows)).T
        start = jnp.where(label == 0.0, 0.0, jnp.where(label == 1.0, first, second))
        token = (lax.broadcasted_iota(jnp.int32, (rows, LANES), 0) + source * rows).astype(jnp.float32)
        angle = (token - start) * rate
        index = slice(block * rows, (block + 1) * rows)
        cosine[index, :] = jnp.cos(angle)
        sine[index, :] = jnp.where(within < half, -1.0, 1.0) * jnp.sin(angle)
        same = ((label == within.astype(jnp.float32)) & (within < SEGS)).astype(jnp.float32)
        shut = (within == SEGS).astype(jnp.float32)
        ones = ((within >= SEGS) & (within < SEGS + 3)).astype(jnp.float32)
        mark_q[index, :] = (SHUT * same - SHUT * shut).astype(jnp.bfloat16)
        mark_k[index, :] = (same + ones).astype(jnp.bfloat16)
        if block == 0:
            segment[...] = label
            member[...] = (
                lax.broadcasted_iota(jnp.int32, (8, rows), 0).astype(jnp.float32) == line
            ).astype(jnp.bfloat16)
    for group in range(SEGS):
        lane = lane_index((TXT, LANES)) % HEAD
        row = lax.broadcasted_iota(jnp.int32, (TXT, LANES), 0)
        inside = ((lane == group) & (row < lens[group])).astype(jnp.float32)
        ones = ((lane >= SEGS) & (lane < SEGS + 3)).astype(jnp.float32)
        mark_t[group * TXT : (group + 1) * TXT, :] = (inside + ones).astype(jnp.bfloat16)


def text_kernel(captions, key_weight, value_weight, raw_out, value_out, raw_sum, value_sum):
    step = pl.program_id(0)

    @pl.when(step == 0)
    def _():
        raw_sum[...] = dot(captions[...], key_weight[...])
        value_sum[...] = dot(captions[...], value_weight[...])

    @pl.when(step > 0)
    def _():
        raw_sum[...] += dot(captions[...], key_weight[...])
        value_sum[...] += dot(captions[...], value_weight[...])

    @pl.when(step == pl.num_programs(0) - 1)
    def _():
        raw_out[...] = raw_sum[...]
        value_out[...] = value_sum[...].astype(jnp.bfloat16)


def text_call(captions, key_weight, value_weight):
    rows, depth = captions.shape
    columns = key_weight.shape[1]
    tile = depth // 4
    return pl.pallas_call(
        text_kernel,
        grid=(depth // tile,),
        in_specs=[
            pl.BlockSpec((rows, tile), lambda step: (0, step)),
            pl.BlockSpec((tile, columns), lambda step: (step, 0)),
            pl.BlockSpec((tile, columns), lambda step: (step, 0)),
        ],
        out_specs=[pl.BlockSpec((rows, columns), lambda step: (0, 0))] * 2,
        out_shape=[
            jax.ShapeDtypeStruct((rows, columns), jnp.float32),
            jax.ShapeDtypeStruct((rows, columns), jnp.bfloat16),
        ],
        scratch_shapes=[pltpu.VMEM((rows, columns), jnp.float32)] * 2,
        compiler_params=pltpu.CompilerParams(vmem_limit_bytes=VMEM_LIMIT),
        cost_estimate=cost_of(9),
        name="text",
    )(captions, key_weight, value_weight)


def project_kernel(here, own, far, near, last, mods, gains, segment_q, query_w, key_w, value_w,
                   rows_out, raw_q, raw_k, value):
    table = mods[here[0]]
    rows = own.shape[0]
    for block, part in enumerate((own, far, near, last)):
        index = slice(block * rows, (block + 1) * rows)
        values = part[...].astype(jnp.float32)
        marks = segment_q[index, :].astype(jnp.float32)
        scale = jnp.where(
            marks[:, 0:1] > 0.0, table[0:1], jnp.where(marks[:, 1:2] > 0.0, table[1:2], table[2:3])
        )
        rows_out[index, :] = (
            values * inverse_rms(values) * gains[0:1] * (1.0 + scale)
        ).astype(jnp.bfloat16)
    raw_q[...] = dot(rows_out[...], query_w[...])
    raw_k[...] = dot(rows_out[...], key_w[...])
    value[...] = dot(rows_out[...], value_w[...]).astype(jnp.bfloat16)


def middle_kernel(here, block, upper, near, far, mods, gains, segment, attn_out, middle_out, rows_out):
    attn_sum = total_of((upper, near, far))
    label = segment[:, 0:1]
    factor = jnp.tanh(per_row(mods[here[0] ^ 1], label)) * gains[1:2]
    middle = block[...].astype(jnp.float32) + factor * (attn_sum * inverse_rms(attn_sum))
    attn_out[...] = attn_sum
    middle_out[...] = middle
    scale = per_row(mods[here[0] ^ 2], label)
    rows_out[...] = (middle * inverse_rms(middle) * gains[2:3] * (1.0 + scale)).astype(jnp.bfloat16)


def block_out_kernel(here, middle, upper, near, far, grad, mods, gains, segment, member,
                     block_out, grad_out, sums):
    ffn_sum = total_of((upper, near, far))
    inverse = inverse_rms(ffn_sum)
    unit = ffn_sum * inverse
    factor = jnp.tanh(per_row(mods[here[0] ^ 3], segment[:, 0:1])) * gains[3:4]
    block_out[...] = (middle[...] + factor * unit).astype(jnp.bfloat16)
    incoming = grad[...].astype(jnp.float32)
    grad_out[...] = row_norm_back(incoming * factor, unit, inverse).astype(jnp.bfloat16)
    sums[...] = segment_sums(member[...], incoming * unit)


def middle_back_kernel(here, middle, attn, upper, near, far, grad, mods, gains, segment, member,
                       middle_grad, attn_grad, ffn_sums, attn_sums):
    grad_in = total_of((upper, near, far))
    label = segment[:, 0:1]
    inverse = inverse_rms(middle[...])
    unit = middle[...] * inverse
    factor = gains[2:3] * (1.0 + per_row(mods[here[0] ^ 2], label))
    ffn_sums[...] = segment_sums(member[...], grad_in * unit)
    grad_middle = grad[...].astype(jnp.float32) + row_norm_back(grad_in * factor, unit, inverse)
    middle_grad[...] = grad_middle
    inverse = inverse_rms(attn[...])
    unit = attn[...] * inverse
    factor = jnp.tanh(per_row(mods[here[0] ^ 1], label)) * gains[1:2]
    attn_grad[...] = row_norm_back(grad_middle * factor, unit, inverse).astype(jnp.bfloat16)
    attn_sums[...] = segment_sums(member[...], grad_middle * unit)


def block_in_kernel(here, block, middle_grad, upper, near, far, mods, gains, segment, member,
                    in_grad, sums):
    grad_in = total_of((upper, near, far))
    values = block[...].astype(jnp.float32)
    inverse = inverse_rms(values)
    unit = values * inverse
    factor = gains[0:1] * (1.0 + per_row(mods[here[0]], segment[:, 0:1]))
    in_grad[...] = (
        middle_grad[...] + row_norm_back(grad_in * factor, unit, inverse)
    ).astype(jnp.bfloat16)
    sums[...] = segment_sums(member[...], grad_in * unit)


def stack_sums_kernel(here, first, second, third, fourth, head_gain, text_gain, gate_sum, gate, out):
    width = out.shape[1]
    heads = jnp.concatenate([head_gain[0:1], head_gain[1:2], text_gain[...]], axis=1)
    inner = heads.shape[1] // 3
    gates = gate_sum[...] * (1.0 - gate[...] * gate[...])
    gates = jnp.concatenate([gates, jnp.zeros((1, width - inner), jnp.float32)], axis=1)
    lane = lane_index(gates.shape)
    moved = jnp.zeros_like(gates)
    for position in range(4):
        turn = pltpu.roll(gates, position * inner, 1) if position else gates
        moved = jnp.where((lane // inner == position) & (here[0] == position), turn, moved)
    out[...] = jnp.concatenate(
        [part[0:SEGS] for part in (first, second, third, fourth)]
        + [
            jnp.concatenate([heads, jnp.zeros((1, width - 3 * inner), jnp.float32)], axis=1),
            moved,
            jnp.zeros((2, width), jnp.float32),
        ],
        axis=0,
    )


def pack_kernel(here, own, far, near, last, mods, gains, cond, packed):
    total = own[...] + far[...] + near[...] + last[...]
    grad = jnp.zeros((SEGS, total.shape[1]), jnp.float32)
    rows = []
    for name in range(4):
        part = total[name * SEGS : (name + 1) * SEGS]
        mod = mods[here[0] ^ name]
        gain = gains[name : name + 1]
        if name % 2 == 1:
            factor = jnp.tanh(mod)
            slope = 1.0 - factor * factor
        else:
            factor = 1.0 + mod
            slope = jnp.ones_like(mod)
        rows.append(jnp.sum(part * factor, axis=0, keepdims=True))
        mine = (jnp.zeros(part.shape, jnp.int32) + here[0]) == name
        grad = jnp.where(mine, part * slope * gain, grad)
    rows.append(total[4 * SEGS : 4 * SEGS + 2])
    rows = jnp.concatenate(rows, axis=0)
    high = rows.astype(jnp.bfloat16).astype(jnp.float32)
    pad = jnp.zeros((packed.shape[0] - 2 * SEGS - 2 * SUM_ROWS, total.shape[1]), jnp.float32)
    packed[...] = jnp.concatenate(
        [grad, cond[...].astype(jnp.float32), high, rows - high, pad], axis=0
    ).astype(jnp.bfloat16)


def rider_rows(count):
    return -(-(2 * SEGS * count + 2 * SUM_ROWS) // 16) * 16


def merge_rows(count, first, second, size):
    first, second = first.astype(jnp.float32), second.astype(jnp.float32)
    wide = SEGS * count
    start = 2 * wide
    sums = (
        first[start : start + SUM_ROWS]
        + first[start + SUM_ROWS : start + 2 * SUM_ROWS]
        + second[start : start + SUM_ROWS]
        + second[start + SUM_ROWS : start + 2 * SUM_ROWS]
    )
    high = sums.astype(jnp.bfloat16).astype(jnp.float32)
    pieces = [first[:wide], second[:wide], first[wide:start], second[wide:start], high, sums - high]
    rest = size - 4 * wide - 2 * SUM_ROWS
    if rest:
        pieces.append(jnp.zeros((rest, first.shape[1]), jnp.float32))
    return jnp.concatenate(pieces, axis=0).astype(jnp.bfloat16)


def merge_kernel(ours, theirs, out):
    out[...] = merge_rows(1, ours[...], theirs[...], out.shape[0])


def ada_kernel(count, heads, dp, own, *refs):
    parts = (own,) + refs[:3]
    ada_out, norm_out, head_out, gate_out = refs[3:]
    wide = SEGS * count
    base = own.shape[0] - rider_rows(count)
    columns = ada_out.shape[0]
    share = LANES // columns
    start = pl.multiple_of(dp[0] // share * LANES, LANES)
    grads, conds = [], []
    sums = jnp.zeros((SUM_ROWS, own.shape[1]), jnp.float32)
    for part in parts:
        rows = part[base:, :].astype(jnp.float32)
        grads.append(rows[:wide])
        conds.append(part[base:, pl.ds(start, LANES)].astype(jnp.float32)[wide : 2 * wide])
        for half in range(2):
            place = 2 * wide + half * SUM_ROWS
            sums = sums + rows[place : place + SUM_ROWS]
    conds = jnp.concatenate(conds, axis=0)
    conds = pltpu.roll(conds, (LANES - dp[0] % share * columns) % LANES, 1)
    acts = conds / (1.0 + jnp.exp(-conds))
    ada_out[...] = dot(
        acts.astype(jnp.bfloat16).astype(jnp.float32).T.astype(jnp.bfloat16),
        jnp.concatenate(grads, axis=0).astype(jnp.bfloat16),
    )[:columns]
    norm_out[...] = sums[:4]
    inner = heads * HEAD
    for row in range(3):
        line = jnp.zeros((1, HEAD), jnp.float32)
        for head in range(heads):
            place = row * inner + head * HEAD
            line = line + sums[4:5, place : place + HEAD]
        head_out[row : row + 1, :] = line
    lane = lane_index((1, LANES))
    line = jnp.zeros((1, LANES), jnp.float32)
    for head in range(HEADS):
        value = jnp.sum(sums[5:6, head * HEAD : (head + 1) * HEAD], axis=1, keepdims=True)
        line = jnp.where(lane == head, value, line)
    gate_out[...] = line


def back_kernel(count, *refs):
    grads, weights, upper, lower = refs[:count], refs[count : 2 * count], refs[-2], refs[-1]
    total = dot_t(grads[0][...], weights[0][...])
    for grad, weight in zip(grads[1:], weights[1:]):
        total = total + dot_t(grad[...], weight[...])
    half = upper.shape[0]
    upper[...] = total[:half].astype(jnp.bfloat16)
    lower[...] = total[half:].astype(jnp.bfloat16)


def back_call(grads, weights, name, ties=(), micros=0):
    rows, inner = grads[0].shape
    columns = weights[0].shape[0]
    tile = columns // 3
    return pl.pallas_call(
        lambda *refs: back_kernel(len(grads), *refs[: 2 * len(grads)], *refs[-2:]),
        grid=(columns // tile,),
        in_specs=[pl.BlockSpec((rows, inner), lambda step: (0, 0))] * len(grads)
        + [pl.BlockSpec((tile, inner), lambda step: (step, 0))] * len(grads)
        + [pl.BlockSpec(memory_space=pl.ANY)] * len(ties),
        out_specs=[pl.BlockSpec((rows // 2, tile), lambda step: (0, step))] * 2,
        out_shape=[jax.ShapeDtypeStruct((rows // 2, columns), jnp.bfloat16)] * 2,
        compiler_params=pltpu.CompilerParams(vmem_limit_bytes=VMEM_LIMIT),
        cost_estimate=cost_of(micros),
        name=name,
    )(*grads, *weights, *ties)


def shards(
    block_in,
    out_grad,
    condition,
    captions,
    caption_len,
    segment_ids,
    ada_weight,
    norm_gains,
    query_weight,
    key_weight,
    value_weight,
    head_gains,
    textkey_weight,
    textvalue_weight,
    cross_gate,
    out_weight,
    gate_weight,
    up_weight,
    down_weight,
):
    rows, width = block_in.shape
    length = segment_ids.shape[0]
    heads = cross_gate.shape[0]
    inner = heads * HEAD
    half_rows = length // 2
    position = lax.axis_index("tensor")
    spot = dp_spot(position)
    here = position.reshape(1)
    b16, f32 = jnp.bfloat16, jnp.float32

    blocks = gather_tensor(block_in)
    cond_rows = jnp.pad(condition, ((0, 0), (0, width - condition.shape[1])))
    own_act = jax.nn.silu(condition.astype(f32)).astype(b16)
    own_part = jnp.dot(own_act, ada_weight, preferred_element_type=f32)
    parts = gather_tensor(own_part)
    mods = jnp.stack([parts[ROW_ORDER.index(code)] for code in range(4)])

    cosine, sine, mark_q, mark_k, mark_t, segment, member, gate_lanes, gate_swapped, gains = whole_call(
        tables_kernel,
        (here, caption_len, cross_gate),
        [segment_ids.reshape(length // rows, rows), head_gains],
        [((length, LANES), f32)] * 2
        + [((length, LANES), b16)] * 2
        + [((SEGS * TXT, LANES), b16), ((rows, LANES), f32), ((8, rows), b16)]
        + [((1, inner), f32)] * 2
        + [((3, inner), f32)],
        "tables",
        micros=2,
    )
    caption_flat = captions.reshape(-1, captions.shape[-1])
    texts = caption_flat.shape[0]
    raw_t, text_value = text_call(caption_flat, textkey_weight, textvalue_weight)
    attn_rows, raw_q, raw_k, value = whole_call(
        project_kernel,
        (here,),
        blocks + [mods, norm_gains, mark_q, query_weight, key_weight, value_weight],
        [((length, width), b16), ((length, inner), f32), ((length, inner), f32), ((length, inner), b16)],
        "project",
        micros=6,
    )
    query, key, text, mixed, self_out, cross_out, self_log, cross_log = pair_call(
        attend_kernel,
        [(raw_q, 1), (raw_k, 1), (value, 1), (raw_t, 1), (text_value, 1), (cosine, None), (sine, None)]
        + [(gains, 1), (gate_lanes, 1), (gate_swapped, 1), (mark_q, None), (mark_k, None), (mark_t, None)],
        [((length, inner), b16, 1)] * 2
        + [((texts, inner), b16, 1), ((length, inner), b16, 1)]
        + [((length, inner), f32, 1)] * 4,
        "attend",
        micros=11,
    )

    def halves(product):
        return product(slice(0, half_rows)).astype(b16), product(slice(half_rows, None)).astype(b16)

    def all_of(block):
        return jnp.concatenate(gather_tensor(block), axis=0)

    upper, lower = halves(lambda part: jnp.dot(mixed[part], out_weight, preferred_element_type=f32))
    sums, sent = scatter_tensor(upper, lower)
    attn_rows_t = turned(attn_rows, (sent,))
    wide = ((rows, width), f32)
    narrow = ((rows, width), b16)
    totals = ((8, width), f32)
    attn_sum, middle, ffn_own = whole_call(
        middle_kernel,
        (here,),
        [block_in] + sums + [mods, norm_gains, segment],
        [wide, wide, narrow],
        "middle",
    )
    ffn_rows = all_of(ffn_own)
    gate_pre = jnp.dot(ffn_rows, gate_weight, preferred_element_type=f32)
    up_pre = jnp.dot(ffn_rows, up_weight, preferred_element_type=f32)
    sigmoid_gate = jax.nn.sigmoid(gate_pre)
    silu_gate = gate_pre * sigmoid_gate
    hidden = (silu_gate * up_pre).astype(b16)
    upper, lower = halves(lambda part: jnp.dot(hidden[part], down_weight, preferred_element_type=f32))
    sums, sent = scatter_tensor(upper, lower)
    ffn_rows_t = turned(ffn_rows, (sent,))
    block_out, grad_own, sum_gate_ffn = whole_call(
        block_out_kernel,
        (here,),
        [middle] + sums + [out_grad, mods, norm_gains, segment, member],
        [narrow, narrow, totals],
        "block_out",
    )

    grad_ffn = all_of(grad_own)
    grad_hidden = times_transpose(grad_ffn, down_weight)
    grad_gate = (
        grad_hidden * up_pre * sigmoid_gate * (1.0 + gate_pre * (1.0 - sigmoid_gate))
    ).astype(b16)
    grad_up = (grad_hidden * silu_gate).astype(b16)
    upper, lower = halves(
        lambda part: times_transpose(grad_gate[part], gate_weight)
        + times_transpose(grad_up[part], up_weight)
    )
    sums, sent = scatter_tensor(upper, lower)
    grad_ffn_t = turned(grad_ffn, (sent,))
    ffn_pairs = [(ffn_rows_t, [grad_gate, grad_up]), (grad_ffn_t, [hidden])]
    (halves_two,) = row_chunks(ffn_pairs, (2,), spot, ties=(sent,), micros=FFN_MICROS)
    ffn_passed = one_on(halves_two)
    grad_middle, grad_own, sum_scale_ffn, sum_gate_attn = whole_call(
        middle_back_kernel,
        (here,),
        [middle, attn_sum] + sums + [out_grad, mods, norm_gains, segment, member],
        [wide, narrow, totals, totals],
        "middle_back",
        micros=MIDDLE_MICROS,
    )

    grad_attn = all_of(grad_own)
    grad_mixed = times_transpose(grad_attn, out_weight).astype(b16)
    cross_grad, text_grad, text_value_grad, text_gain, gate_sum = pair_call(
        cross_back_kernel,
        [(query, 1), (text, 1), (text_value, 1), (raw_t, 1), (grad_mixed, 1), (cross_out, 1)]
        + [(cross_log, 1), (gains, 1), (mark_q, None), (mark_t, None)],
        [((length, inner), f32, 1), ((inner, texts), b16, 0), ((inner, texts), b16, 0)]
        + [((1, inner), f32, 1)] * 2,
        "cross_back",
        micros=CROSS_MICROS,
    )
    ffn_one, ffn_three, ffn_kept = row_chunks(
        ffn_pairs, (1, 3, 0), spot, extra=ffn_passed, ties=(text_grad,), micros=FFN_NEXT_MICROS
    )
    text_lefts = [text_grad, text_value_grad]
    (halves_two,) = column_chunks(text_lefts, caption_flat, (2,), spot, ties=(ffn_kept,))
    text_passed = one_on(halves_two)
    query_grad, key_grad, value_grad, head_gain = pair_call(
        self_back_kernel,
        [(query, 1), (key, 1), (value, 1), (raw_q, 1), (raw_k, 1), (grad_mixed, 1), (self_out, 1)]
        + [(self_log, 1), (cross_grad, 1), (cosine, None), (sine, None), (gains, 1)]
        + [(mark_q, None), (mark_k, None)],
        [((length, inner), b16, 1)] * 3 + [((2, inner), f32, 1)],
        "self_back",
        (halves_two[0],),
        micros=SELF_MICROS,
    )

    hidden_cols = hidden.shape[1]
    block_rows = width // BLOCKS
    got = [by_slots(part) for part in to_neighbours(ffn_kept, ffn_one, ffn_three)]
    shape = (PAIR, block_rows, 3 * hidden_cols)
    ffn_stage = tiled_call(
        ffn_second_kernel, (spot,), got, [(shape, b16)] * RING, "ffn_second",
        -1,
        4, (query_grad,)
    )
    upper, lower = back_call(
        [query_grad, key_grad, value_grad], [query_weight, key_weight, value_weight], "attn_back"
    )
    sums, sent = scatter_tensor(upper, lower)
    in_grad, sum_scale_attn = whole_call(
        block_in_kernel,
        (here,),
        [block_in, grad_middle] + sums + [mods, norm_gains, segment, member],
        [narrow, totals],
        "block_in",
        (ffn_stage[0],),
        micros=BLOCK_IN_MICROS,
    )
    (stacked,) = whole_call(
        stack_sums_kernel,
        (here,),
        [sum_scale_attn, sum_gate_attn, sum_scale_ffn, sum_gate_ffn]
        + [head_gain, text_gain, gate_sum, gate_lanes],
        [((16, width), f32)],
        "stack_sums",
    )
    sums_stacked = stacked
    text_one, text_three, text_kept = column_chunks(
        text_lefts, caption_flat, (1, 3, 0), spot, extra=text_passed, ties=(sums_stacked,), micros=TEXT_MICROS
    )
    stacked = gather_tensor(stacked)
    kept, sent = tiled_call(
        ffn_third_kernel,
        (spot,),
        exchange(ffn_stage, "second"),
        [(shape[1:], b16)] * 2,
        "ffn_third",
        -1,
        2,
        (text_kept,),
    )
    (riders,) = whole_call(
        pack_kernel,
        (here,),
        stacked + [mods, norm_gains, cond_rows],
        [((rider_rows(1), width), b16)],
        "pack",
        (kept,),
    )
    theirs = dp_permute(riders, "z", 1)
    (riders,) = whole_call(
        merge_kernel, (), [riders, theirs], [((rider_rows(PAIR), width), b16)], "merge"
    )
    attn_pairs = [
        (attn_rows_t, [query_grad, key_grad, value_grad]),
        (turned(grad_attn, (halves_two[0],)), [mixed]),
    ]
    (halves_two,) = row_chunks(attn_pairs, (2,), spot, riders=(riders,), micros=ATTN_FIRST_MICROS)
    attn_passed = one_on(halves_two)
    gate_sum_out, up_sum_out, down_sum_out = whole_call(
        ffn_last_kernel,
        (),
        exchange([kept, sent], "z"),
        [((block_rows, hidden_cols), f32)] * 2 + [((hidden_cols, block_rows), f32)],
        "ffn_last",
    )
    text_rows = caption_flat.shape[1] // BLOCKS
    attn_one, attn_three, attn_kept = row_chunks(
        attn_pairs, (1, 3, 0), spot, extra=attn_passed, ties=(kept,), riders=(riders,), micros=ATTN_MICROS
    )
    stage = tiled_call(
        text_second_kernel,
        (spot,),
        to_neighbours(text_kept, text_one, text_three),
        [((2 * inner, PAIR * text_rows), b16)] * RING,
        "text_second",
        0,
        4,
        (attn_kept,),
    )
    kept, sent = tiled_call(
        text_third_kernel,
        (spot,),
        exchange(stage, "second"),
        [((2 * inner, text_rows), b16)] * 2,
        "text_third",
        0,
        2,
        (gate_sum_out,),
    )
    textkey_sum, textvalue_sum = whole_call(
        text_last_kernel,
        (),
        exchange([kept, sent], "z"),
        [((text_rows, inner), f32)] * 2,
        "text_last",
    )
    stage = tiled_call(
        functools.partial(attn_second_kernel, block_rows),
        (spot,),
        [riders] + to_neighbours(attn_kept, attn_one, attn_three),
        [((PAIR * block_rows + rider_rows(4 * PAIR), width), b16)] * RING,
        "attn_second",
        -1,
        4,
        (kept,),
    )
    got = exchange(stage, "second")
    kept, sent = tiled_call(
        attn_third_kernel, (spot,), got, [((block_rows, width), b16)] * 2, "attn_third",
        -1,
        2
    )
    ada_grad, norm_grads, head_grads, crossgate = tiled_call(
        functools.partial(ada_kernel, 4 * PAIR, heads),
        (lax.axis_index("dp").reshape(1),),
        got,
        [((condition.shape[1] // BLOCKS, width), f32), ((4, width), f32), ((3, HEAD), f32)]
        + [((1, LANES), f32)],
        "ada",
        0,
        1,
        (kept,),
    )
    crossgate_grad = crossgate[0, :HEADS]
    query_sum, key_sum, value_sum, outw_sum = whole_call(
        attn_last_kernel,
        (),
        exchange([kept, sent], "z"),
        [((block_rows, inner), f32)] * 3 + [((inner, block_rows), f32)],
        "attn_last",
    )
    return (
        block_out,
        in_grad,
        ada_grad,
        norm_grads,
        query_sum,
        key_sum,
        value_sum,
        head_grads,
        textkey_sum,
        textvalue_sum,
        crossgate_grad,
        outw_sum,
        gate_sum_out,
        up_sum_out,
        down_sum_out,
    )


def solution(mesh):
    return jax.shard_map(
        shards,
        mesh=mesh,
        in_specs=(
            P(("dp", "tensor"), None),
            P(("dp", "tensor"), None),
            P("dp", None),
            P("dp", None, None),
            P("dp"),
            P("dp"),
            P(None, "tensor"),
            P(),
            P(None, "tensor"),
            P(None, "tensor"),
            P(None, "tensor"),
            P(),
            P(None, "tensor"),
            P(None, "tensor"),
            P("tensor"),
            P("tensor", None),
            P(None, "tensor"),
            P(None, "tensor"),
            P("tensor", None),
        ),
        out_specs=(
            P(("dp", "tensor"), None),
            P(("dp", "tensor"), None),
            P("dp", "tensor"),
            P(),
            P("dp", "tensor"),
            P("dp", "tensor"),
            P("dp", "tensor"),
            P(),
            P("dp", "tensor"),
            P("dp", "tensor"),
            P(),
            P("tensor", "dp"),
            P("dp", "tensor"),
            P("dp", "tensor"),
            P("tensor", "dp"),
        ),
        check_vma=False,
    )
```

profile of v0, /device:TPU:0, one launch (start us, length us, event | category | flops | bytes accessed | tf_op | source)
XLA Modules:
  0.0 314.2 jit_solution(2497122545564404351)
XLA Ops:
  0.7 3.2 %fusion.16 = f32[3,1536]{1,0:T(4,128)} fusion(bf16[1024,1536]{1,0:T(8,128)(2,1)} %param.25, bf16[3,1024]{1,0:T(4,128)(2,1)} %param.21), kind=kOutput, calls=%fused_computation.46 | convolution fusion | flops 9455616 | bytes 3170304 | tf_op jit(solution)/shard_map/dot_general | solution.py:1018
  13.0 7.8 %text.1 = (f32[768,384]{1,0:T(8,128)S(1)}, bf16[768,384]{1,0:T(8,128)(2,1)S(1)}) custom-call(bf16[768,4096]{1,0:T(8,128)(2,1)S(1)} %bitcast.38, bf16[4096,384]{1,0:T(8,128)(2,1)S(1)} %copy-done.74, bf16[4096,384]{1,0:T(8,128)(2,1)S(1)} %copy-done.75), custom_call_target="tpu_custom_call" | custom-call | flops 8999999488 | tf_op jit(solution)/shard_map/text/pallas_call | solution.py:750
  29.0 4.9 %project.1 = (bf16[512,1536]{1,0:T(8,128)(2,1)S(1)}, f32[512,384]{1,0:T(8,128)S(1)}, f32[512,384]{1,0:T(8,128)S(1)}, bf16[512,384]{1,0:T(8,128)(2,1)S(1)}) custom-call(s32[1]{0:T(128)} %bitcast.refs_0_, bf16[128,1536]{1,0:T(8,128)(2,1)S(1)} %copy-done.26, bf16[128,1536]{1,0:T(8,128)(2,1)} %collective-permute-done.refs_2_, ...), custom_call_target="tpu_custom_call" | custom-call | flops 6000000000 | tf_op jit(solution)/shard_map/project/pallas_call | solution.py:432
  35.1 9.9 %attend.1 = (bf16[512,384]{1,0:T(8,128)(2,1)S(1)}, bf16[512,384]{1,0:T(8,128)(2,1)S(1)}, bf16[768,384]{1,0:T(8,128)(2,1)S(1)}, bf16[512,384]{1,0:T(8,128)(2,1)S(...) custom-call(f32[512,384]{1,0:T(8,128)S(1)} %get-tuple-element.109.refs_0_, ...), custom_call_target="tpu_custom_call" | custom-call | flops 11000000512 | tf_op jit(solution)/shard_map/attend/pallas_call | solution.py:642
  51.0 9.4 %collective-permute-done.7.refs_4_ = bf16[128,1536]{1,0:T(8,128)(2,1)S(1)} collective-permute-done((bf16[128,1536]{1,0:T(8,128)(2,1)S(1)}, bf16[128,1536]{1,0:T(8,128)(2,1)S(1)}, u32[]{:S(2)}, u32[]{:S(2)}) %collective-permute-start.7) | collective-permute-done | bytes 393248 | tf_op jit(solution)/shard_map/ppermute | solution.py:90
  63.1 8.9 %collective-permute-done.8 = bf16[128,1536]{1,0:T(8,128)(2,1)S(1)} collective-permute-done((bf16[128,1536]{1,0:T(8,128)(2,1)S(1)}, bf16[128,1536]{1,0:T(8,128)(2,1)S(1)}, u32[]{:S(2)}, u32[]{:S(2)}) %collective-permute-start.8) | collective-permute-done | bytes 393248 | tf_op jit(solution)/shard_map/ppermute | solution.py:90
  84.2 9.0 %collective-permute-done.12.refs_4_ = bf16[128,1536]{1,0:T(8,128)(2,1)S(1)} collective-permute-done((bf16[128,1536]{1,0:T(8,128)(2,1)S(1)}, bf16[128,1536]{1,0:T(8,128)(2,1)S(1)}, u32[]{:S(2)}, u32[]{:S(2)}) %collective-permute-start.12) | collective-permute-done | bytes 393248 | tf_op jit(solution)/shard_map/ppermute | solution.py:90
  96.2 8.9 %collective-permute-done.13 = bf16[128,1536]{1,0:T(8,128)(2,1)S(1)} collective-permute-done((bf16[128,1536]{1,0:T(8,128)(2,1)S(1)}, bf16[128,1536]{1,0:T(8,128)(2,1)S(1)}, u32[]{:S(2)}, u32[]{:S(2)}) %collective-permute-start.13) | collective-permute-done | bytes 393248 | tf_op jit(solution)/shard_map/ppermute | solution.py:90
  118.5 7.8 %collective-permute-done.17.refs_5_ = bf16[128,1536]{1,0:T(8,128)(2,1)} collective-permute-done((bf16[128,1536]{1,0:T(8,128)(2,1)S(1)}, bf16[128,1536]{1,0:T(8,128)(2,1)}, u32[]{:S(2)}, u32[]{:S(2)}) %collective-permute-start.17) | collective-permute-done | bytes 393248 | tf_op jit(solution)/shard_map/ppermute | solution.py:90
  135.8 3.6 %collective-permute-done.18 = bf16[128,1536]{1,0:T(8,128)(2,1)S(1)} collective-permute-done((bf16[128,1536]{1,0:T(8,128)(2,1)S(1)}, bf16[128,1536]{1,0:T(8,128)(2,1)S(1)}, u32[]{:S(2)}, u32[]{:S(2)}) %collective-permute-start.18) | collective-permute-done | bytes 393248 | tf_op jit(solution)/shard_map/ppermute | solution.py:90
  143.4 8.2 %cross_back.1 = (f32[512,384]{1,0:T(8,128)S(1)}, bf16[384,768]{1,0:T(8,128)(2,1)S(1)}, bf16[384,768]{1,0:T(8,128)(2,1)S(1)}, f32[1,384]{1,0:T(1,128)S(1)}, f32[1,384]{1,0:T(1,128)S(1)}) custom-call(bf16[512,384]{1,0:T(8,128)(2,1)S(1)} %copy-done.53, bf16[768,384]{1,0:T(8,128)(2,1)S(1)} %copy-done.95, bf16[768,384]{1,0:T(8,128)(2,1)S(1)} %copy-done.89, ...), custom_call_target="tpu_custom_call" | custom-call | flops 10000000000 | tf_op jit(solution)/shard_map/cross_back/pallas_call | solution.py:642
  151.6 5.5 %row_chunks.5 = (bf16[384,3072]{1,0:T(8,128)(2,1)S(1)}, bf16[384,3072]{1,0:T(8,128)(2,1)S(1)}, bf16[384,3072]{1,0:T(8,128)(2,1)S(1)}) custom-call(s32[4]{0:T(128)S(1)} %pad_add_fusion.spot_ref.refs_0_, bf16[32,48,512]{2,1,0:T(8,128)(2,1)S(1)} %bitcast.65, bf16[32,48,512]{2,1,0:T(8,128)(2,1)S(1)} %bitcast.66, bf16[32,48,512]{2,1,0:T(8,128)(2,1)S(1)} %bitcast.67, ...), custom_call_target="tpu_custom_call" | custom-call | flops 8000000000 | tf_op jit(solution)/shard_map/row_chunks/pallas_call | solution.py:194
  163.2 7.9 %self_back.1 = (bf16[512,384]{1,0:T(8,128)(2,1)S(1)}, bf16[512,384]{1,0:T(8,128)(2,1)S(1)}, bf16[512,384]{1,0:T(8,128)(2,1)S(1)}, f32[2,384]{1,0:T(2,128)S(1)}) custom-call(bf16[512,384]{1,0:T(8,128)(2,1)S(1)} %copy-done.53, bf16[512,384]{1,0:T(8,128)(2,1)S(1)} %copy-done.55, bf16[512,384]{1,0:T(8,128)(2,1)S(1)} %copy-done.51, f32[512,384]{1,0:T(8,128)S(1)} %copy-done.37, ...), custom_call_target="tpu_custom_call" | custom-call | tf_op jit(solution)/shard_map/self_back/pallas_call | solution.py:642
  171.1 3.1 attn_back.1
  179.3 8.0 %collective-permute-done.25 = bf16[384,3072]{1,0:T(8,128)(2,1)S(1)} collective-permute-done((bf16[384,3072]{1,0:T(8,128)(2,1)S(1)}, bf16[384,3072]{1,0:T(8,128)(2,1)S(1)}, u32[]{:S(2)}, u32[]{:S(2)}) %collective-permute-start.25) | collective-permute-done | bytes 2359328 | tf_op jit(solution)/shard_map/ppermute | solution.py:75
  188.7 4.1 %ffn_second.1 = (bf16[2,48,3072]{2,1,0:T(8,128)(2,1)S(1)}, bf16[2,48,3072]{2,1,0:T(8,128)(2,1)S(1)}, bf16[2,48,3072]{2,1,0:T(8,128)(2,1)S(1)}, bf16[2,48,3072]{2,1,0:T(8,128)(2,1)S(1)}) custom-call(s32[4]{0:T(128)S(1)} %pad_add_fusion.spot_ref.refs_0_, bf16[8,48,3072]{2,1,0:T(8,128)(2,1)} %bitcast.121, bf16[8,48,3072]{2,1,0:T(8,128)(2,1)} %bitcast.123, ...), custom_call_target="tpu_custom_call" | custom-call | tf_op jit(solution)/shard_map/ffn_second/pallas_call | solution.py:455
  202.3 7.0 %column_chunks.3 = (bf16[768,1024]{1,0:T(8,128)(2,1)S(1)}, bf16[768,1024]{1,0:T(8,128)(2,1)S(1)}, bf16[768,1024]{1,0:T(8,128)(2,1)S(1)}) custom-call(s32[4]{0:T(128)S(1)} %pad_add_fusion.spot_ref.refs_0_, bf16[384,768]{1,0:T(8,128)(2,1)S(1)} %get-tuple-element.139.refs_21_.refs_0_, bf16[384,768]{1,0:T(8,128)(2,1)S(1)} %get-tuple-element.140.refs_1_, ...), custom_call_target="tpu_custom_call" | custom-call | flops 8000000000 | tf_op jit(solution)/shard_map/column_chunks/pallas_call | solution.py:194
  209.3 5.5 %collective-permute-done.31.refs_3_ = bf16[2,48,3072]{2,1,0:T(8,128)(2,1)S(1)} collective-permute-done((bf16[2,48,3072]{2,1,0:T(8,128)(2,1)S(1)}, bf16[2,48,3072]{2,1,0:T(8,128)(2,1)S(1)}, u32[]{:S(2)}, u32[]{:S(2)}) %collective-permute-start.31) | collective-permute-done | bytes 589856 | tf_op jit(solution)/shard_map/ppermute | solution.py:75
  218.1 3.7 %collective-permute-start.35 = (bf16[32,1536]{1,0:T(8,128)(2,1)S(1)}, bf16[32,1536]{1,0:T(8,128)(2,1)S(1)}, u32[]{:S(2)}, u32[]{:S(2)}) collective-permute-start(bf16[32,1536]{1,0:T(8,128)(2,1)S(1)} %pack.1.refs_0_), channel_id=1, source_target_pairs={{0,16},{1,17},{2,18},{3,19},{4,20},{5,21},{6,22},{7,23},{8,24},{9,... | collective-permute-start | bytes 294920 | tf_op jit(solution)/shard_map/ppermute | solution.py:75
  229.5 3.2 %collective-permute-start.41 = (bf16[768,1024]{1,0:T(8,128)(2,1)S(1)}, bf16[768,1024]{1,0:T(8,128)(2,1)S(1)}, u32[]{:S(2)}, u32[]{:S(2)}) collective-permute-start(bf16[768,1024]{1,0:T(8,128)(2,1)S(1)} %get-tuple-element.174), channel_id=1, source_target_pairs={{0,96},{1,13},{2,98},{3,15},{4,100},{5,1},{6,102},{7,3},{8,104},{9... | collective-permute-start | bytes 4718600 | tf_op jit(solution)/shard_map/ppermute | solution.py:75
  232.7 5.7 %collective-permute-done.36.refs_21_ = bf16[448,768]{1,0:T(8,128)(2,1)S(1)} collective-permute-done((bf16[448,768]{1,0:T(8,128)(2,1)S(1)}, bf16[448,768]{1,0:T(8,128)(2,1)S(1)}, u32[]{:S(2)}, u32[]{:S(2)}) %collective-permute-start.36) | collective-permute-done | bytes 688160 | tf_op jit(solution)/shard_map/ppermute | solution.py:75
  238.4 4.4 %row_chunks.7 = (bf16[448,1536]{1,0:T(8,128)(2,1)S(1)}, bf16[448,1536]{1,0:T(8,128)(2,1)S(1)}, bf16[448,1536]{1,0:T(8,128)(2,1)S(1)}) custom-call(s32[4]{0:T(128)S(1)} %pad_add_fusion.spot_ref.refs_0_, bf16[32,48,512]{2,1,0:T(8,128)(2,1)S(1)} %bitcast.97, bf16[32,48,512]{2,1,0:T(8,128)(2,1)S(1)} %bitcast.98, bf16[32,48,512]{2,1,0:T(8,128)(2,1)S(1)} %bitcast.99, ...), custom_call_target="tpu_custom_call" | custom-call | flops 7000000000 | tf_op jit(solution)/shard_map/row_chunks/pallas_call | solution.py:194
  246.2 3.5 %collective-permute-start.45 = (bf16[48,3072]{1,0:T(8,128)(2,1)S(1)}, bf16[48,3072]{1,0:T(8,128)(2,1)S(1)}, u32[]{:S(2)}, u32[]{:S(2)}) collective-permute-start(bf16[48,3072]{1,0:T(8,128)(2,1)S(1)} %get-tuple-element.179), channel_id=1, source_target_pairs={{0,16},{1,17},{2,18},{3,19},{4,20},{5,21},{6,22},{7,23},{8,24},{9,... | collective-permute-start | bytes 884744 | tf_op jit(solution)/shard_map/ppermute | solution.py:75
  249.7 5.5 %collective-permute-done.40.refs_2_ = bf16[768,1024]{1,0:T(8,128)(2,1)S(1)} collective-permute-done((bf16[768,1024]{1,0:T(8,128)(2,1)S(1)}, bf16[768,1024]{1,0:T(8,128)(2,1)S(1)}, u32[]{:S(2)}, u32[]{:S(2)}) %collective-permute-start.40) | collective-permute-done | bytes 1572896 | tf_op jit(solution)/shard_map/ppermute | solution.py:75
  257.0 3.6 %text_second.1 = (bf16[768,256]{1,0:T(8,128)(2,1)S(1)}, bf16[768,256]{1,0:T(8,128)(2,1)S(1)}, bf16[768,256]{1,0:T(8,128)(2,1)S(1)}, bf16[768,256]{1,0:T(8,128)(2,1)S(1)}) custom-call(s32[4]{0:T(128)S(1)} %pad_add_fusion.spot_ref.refs_0_, bf16[768,1024]{1,0:T(8,128)(2,1)} %copy-done.8, bf16[768,1024]{1,0:T(8,128)(2,1)} %copy-done.102, ...), custom_call_target="tpu_custom_call" | custom-call | tf_op jit(solution)/shard_map/text_second/pallas_call | solution.py:455
  267.1 4.4 %collective-permute-done.42.refs_2_ = bf16[768,256]{1,0:T(8,128)(2,1)S(1)} collective-permute-done((bf16[768,256]{1,0:T(8,128)(2,1)S(1)}, bf16[768,256]{1,0:T(8,128)(2,1)S(1)}, u32[]{:S(2)}, u32[]{:S(2)}) %collective-permute-start.42) | collective-permute-done | bytes 393248 | tf_op jit(solution)/shard_map/ppermute | solution.py:75
  271.5 5.4 %collective-permute-done.43.refs_3_ = bf16[768,256]{1,0:T(8,128)(2,1)S(1)} collective-permute-done((bf16[768,256]{1,0:T(8,128)(2,1)S(1)}, bf16[768,256]{1,0:T(8,128)(2,1)S(1)}, u32[]{:S(2)}, u32[]{:S(2)}) %collective-permute-start.43) | collective-permute-done | bytes 393248 | tf_op jit(solution)/shard_map/ppermute | solution.py:75
  281.9 3.3 %attn_second.1 = (bf16[160,1536]{1,0:T(8,128)(2,1)S(1)}, bf16[160,1536]{1,0:T(8,128)(2,1)S(1)}, bf16[160,1536]{1,0:T(8,128)(2,1)S(1)}, bf16[160,1536]{1,0:T(8,128)(2,1)S(1)}) custom-call(s32[4]{0:T(128)S(1)} %pad_add_fusion.spot_ref.refs_0_, bf16[32,1536]{1,0:T(8,128)(2,1)} %copy-done.29, bf16[448,1536]{1,0:T(8,128)(2,1)} %copy-done.9, ...), custom_call_target="tpu_custom_call" | custom-call | tf_op jit(solution)/shard_map/attn_second/pallas_call | solution.py:455
  286.0 3.1 %collective-permute-start.47 = (bf16[160,1536]{1,0:T(8,128)(2,1)S(1)}, bf16[160,1536]{1,0:T(8,128)(2,1)}, u32[]{:S(2)}, u32[]{:S(2)}) collective-permute-start(bf16[160,1536]{1,0:T(8,128)(2,1)S(1)} %get-tuple-element.184), channel_id=1, source_target_pairs={{0,8},{1,65},{2,10},{3,67},{4,12},{5,69},{6,14},{7,71},{8,0},{9,73... | collective-permute-start | bytes 1474568 | tf_op jit(solution)/shard_map/ppermute | solution.py:75
  290.3 2.9 collective-permute-start.50
  294.0 5.2 %collective-permute-done.50.refs_1_ = bf16[768,128]{1,0:T(8,128)(2,1)S(1)} collective-permute-done((bf16[768,128]{1,0:T(8,128)(2,1)S(1)}, bf16[768,128]{1,0:T(8,128)(2,1)S(1)}, u32[]{:S(2)}, u32[]{:S(2)}) %collective-permute-start.50) | collective-permute-done | bytes 196640 | tf_op jit(solution)/shard_map/ppermute | solution.py:75
  304.2 3.0 collective-permute-start.49
  (370 shorter events, 131.7 us)
Async XLA Ops:
  3.9 18.8 %collective-permute-start.4 = (f32[3,1536]{1,0:T(4,128)}, f32[3,1536]{1,0:T(4,128)}, u32[]{:S(2)}, u32[]{:S(2)}) collective-permute-start(f32[3,1536]{1,0:T(4,128)} %fusion.16), channel_id=1, source_target_pairs={{0,2},{2,0},{1,3},{3,1},{4,6},{6,4},{5,7},{7,5},{8,10},{10,8},{9,1... | collective-permute-start | bytes 55304 | tf_op jit(solution)/shard_map/ppermute | solution.py:90
  5.9 22.1 %collective-permute-start.3 = (f32[3,1536]{1,0:T(4,128)}, f32[3,1536]{1,0:T(4,128)}, u32[]{:S(2)}, u32[]{:S(2)}) collective-permute-start(f32[3,1536]{1,0:T(4,128)} %fusion.16), channel_id=1, source_target_pairs={{0,1},{1,0},{2,3},{3,2},{4,5},{5,4},{6,7},{7,6},{8,9},{9,8},{10,11... | collective-permute-start | bytes 55304 | tf_op jit(solution)/shard_map/ppermute | solution.py:86
  5.9 23.0 %collective-permute-start.1 = (bf16[128,1536]{1,0:T(8,128)(2,1)S(1)}, bf16[128,1536]{1,0:T(8,128)(2,1)}, u32[]{:S(2)}, u32[]{:S(2)}) collective-permute-start(bf16[128,1536]{1,0:T(8,128)(2,1)S(1)} %copy-done.26), channel_id=1, source_target_pairs={{0,1},{1,0},{2,3},{3,2},{4,5},{5,4},{6,7},{7,6},{8,9},{9,8},{10,11... | collective-permute-start | bytes 1179656 | tf_op jit(solution)/shard_map/ppermute | solution.py:86
  6.4 16.3 %collective-permute-start = (bf16[128,1536]{1,0:T(8,128)(2,1)S(1)}, bf16[128,1536]{1,0:T(8,128)(2,1)}, u32[]{:S(2)}, u32[]{:S(2)}) collective-permute-start(bf16[128,1536]{1,0:T(8,128)(2,1)S(1)} %copy-done.26), channel_id=1, source_target_pairs={{0,2},{2,0},{1,3},{3,1},{4,6},{6,4},{5,7},{7,5},{8,10},{10,8},{9,1... | collective-permute-start | bytes 1179656 | tf_op jit(solution)/shard_map/ppermute | solution.py:90
  48.9 11.5 %collective-permute-start.7 = (bf16[128,1536]{1,0:T(8,128)(2,1)S(1)}, bf16[128,1536]{1,0:T(8,128)(2,1)S(1)}, u32[]{:S(2)}, u32[]{:S(2)}) collective-permute-start(bf16[128,1536]{1,0:T(8,128)(2,1)S(1)} %add_convert_fusion.3.rest_0_), channel_id=1, source_target_pairs={{0,2},{2,0},{1,3},{3,1},{4,6},{6,4},{5,7},{7,5},{8,10},{10,8},{9,1... | collective-permute-start | bytes 1179656 | tf_op jit(solution)/shard_map/ppermute | solution.py:90
  82.0 11.2 %collective-permute-start.12 = (bf16[128,1536]{1,0:T(8,128)(2,1)S(1)}, bf16[128,1536]{1,0:T(8,128)(2,1)S(1)}, u32[]{:S(2)}, u32[]{:S(2)}) collective-permute-start(bf16[128,1536]{1,0:T(8,128)(2,1)S(1)} %add_convert_fusion.2.rest_0_), channel_id=1, source_target_pairs={{0,2},{2,0},{1,3},{3,1},{4,6},{6,4},{5,7},{7,5},{8,10},{10,8},{9,1... | collective-permute-start | bytes 1179656 | tf_op jit(solution)/shard_map/ppermute | solution.py:90
  114.6 11.6 %collective-permute-start.17 = (bf16[128,1536]{1,0:T(8,128)(2,1)S(1)}, bf16[128,1536]{1,0:T(8,128)(2,1)}, u32[]{:S(2)}, u32[]{:S(2)}) collective-permute-start(bf16[128,1536]{1,0:T(8,128)(2,1)S(1)} %add_convert_fusion.1.rest_0_.refs_19_), channel_id=1, source_target_pairs={{0,2},{2,0},{1,3},{3,1},{4,6},{6,4},{5,7},{7,5},{8,10},{10,8},{9,1... | collective-permute-start | bytes 1179656 | tf_op jit(solution)/shard_map/ppermute | solution.py:90
  132.5 19.1 %collective-permute-start.21 = (bf16[384,1536]{1,0:T(8,128)(2,1)S(1)}, bf16[384,1536]{1,0:T(8,128)(2,1)S(1)}, u32[]{:S(2)}, u32[]{:S(2)}) collective-permute-start(bf16[384,1536]{1,0:T(8,128)(2,1)S(1)} %get-tuple-element.141), channel_id=1, source_target_pairs={{0,32},{1,5},{2,34},{3,7},{4,36},{5,9},{6,38},{7,11},{8,40},{9,13}... | collective-permute-start | bytes 3538952 | tf_op jit(solution)/shard_map/ppermute | solution.py:75
  134.0 17.6 %collective-permute-start.22 = (bf16[384,1536]{1,0:T(8,128)(2,1)S(1)}, bf16[384,1536]{1,0:T(8,128)(2,1)S(1)}, u32[]{:S(2)}, u32[]{:S(2)}) collective-permute-start(bf16[384,1536]{1,0:T(8,128)(2,1)S(1)} %get-tuple-element.142), channel_id=1, source_target_pairs={{0,96},{1,13},{2,98},{3,15},{4,100},{5,1},{6,102},{7,3},{8,104},{9... | collective-permute-start | bytes 3538952 | tf_op jit(solution)/shard_map/ppermute | solution.py:75
  157.2 30.1 %collective-permute-start.25 = (bf16[384,3072]{1,0:T(8,128)(2,1)S(1)}, bf16[384,3072]{1,0:T(8,128)(2,1)S(1)}, u32[]{:S(2)}, u32[]{:S(2)}) collective-permute-start(bf16[384,3072]{1,0:T(8,128)(2,1)S(1)} %get-tuple-element.150), channel_id=1, source_target_pairs={{0,32},{1,5},{2,34},{3,7},{4,36},{5,9},{6,38},{7,11},{8,40},{9,13}... | collective-permute-start | bytes 7077896 | tf_op jit(solution)/shard_map/ppermute | solution.py:75
  158.6 29.1 %collective-permute-start.26 = (bf16[384,3072]{1,0:T(8,128)(2,1)S(1)}, bf16[384,3072]{1,0:T(8,128)(2,1)}, u32[]{:S(2)}, u32[]{:S(2)}) collective-permute-start(bf16[384,3072]{1,0:T(8,128)(2,1)S(1)} %get-tuple-element.151), channel_id=1, source_target_pairs={{0,96},{1,13},{2,98},{3,15},{4,100},{5,1},{6,102},{7,3},{8,104},{9... | collective-permute-start | bytes 7077896 | tf_op jit(solution)/shard_map/ppermute | solution.py:75
  174.3 26.3 %collective-permute-start.33 = (bf16[384,1024]{1,0:T(8,128)(2,1)S(1)}, bf16[384,1024]{1,0:T(8,128)(2,1)S(1)}, u32[]{:S(2)}, u32[]{:S(2)}) collective-permute-start(bf16[384,1024]{1,0:T(8,128)(2,1)S(1)} %get-tuple-element.144.refs_14_.rest_0_), channel_id=1, source_target_pairs={{0,32},{1,5},{2,34},{3,7},{4,36},{5,9},{6,38},{7,11},{8,40},{9,13}... | collective-permute-start | bytes 2359304 | tf_op jit(solution)/shard_map/ppermute | solution.py:75
  175.5 22.3 %collective-permute-start.34 = (bf16[384,1024]{1,0:T(8,128)(2,1)S(1)}, bf16[384,1024]{1,0:T(8,128)(2,1)S(1)}, u32[]{:S(2)}, u32[]{:S(2)}) collective-permute-start(bf16[384,1024]{1,0:T(8,128)(2,1)S(1)} %get-tuple-element.164), channel_id=1, source_target_pairs={{0,96},{1,13},{2,98},{3,15},{4,100},{5,1},{6,102},{7,3},{8,104},{9... | collective-permute-start | bytes 2359304 | tf_op jit(solution)/shard_map/ppermute | solution.py:75
  177.7 15.2 %collective-permute-start.24 = (bf16[128,1536]{1,0:T(8,128)(2,1)S(1)}, bf16[128,1536]{1,0:T(8,128)(2,1)S(1)}, u32[]{:S(2)}, u32[]{:S(2)}) collective-permute-start(bf16[128,1536]{1,0:T(8,128)(2,1)S(1)} %add_convert_fusion), channel_id=1, source_target_pairs={{0,2},{2,0},{1,3},{3,1},{4,6},{6,4},{5,7},{7,5},{8,10},{10,8},{9,1... | collective-permute-start | bytes 1179656 | tf_op jit(solution)/shard_map/ppermute | solution.py:90
  196.0 21.9 %collective-permute-start.28 = (f32[16,1536]{1,0:T(8,128)S(1)}, f32[16,1536]{1,0:T(8,128)S(1)}, u32[]{:S(2)}, u32[]{:S(2)}) collective-permute-start(f32[16,1536]{1,0:T(8,128)S(1)} %stack_sums.1.refs_12_.refs_1_), channel_id=1, source_target_pairs={{0,1},{1,0},{2,3},{3,2},{4,5},{5,4},{6,7},{7,6},{8,9},{9,8},{10,11... | collective-permute-start | bytes 294920 | tf_op jit(solution)/shard_map/ppermute | solution.py:86
  196.1 13.2 %collective-permute-start.30 = (bf16[2,48,3072]{2,1,0:T(8,128)(2,1)S(1)}, bf16[2,48,3072]{2,1,0:T(8,128)(2,1)S(1)}, u32[]{:S(2)}, u32[]{:S(2)}) collective-permute-start(bf16[2,48,3072]{2,1,0:T(8,128)(2,1)S(1)} %get-tuple-element.161), channel_id=1, source_target_pairs={{0,4},{1,33},{2,6},{3,35},{4,8},{5,37},{6,10},{7,39},{8,12},{9,41}... | collective-permute-start | bytes 1769480 | tf_op jit(solution)/shard_map/ppermute | solution.py:75
  197.8 17.1 %collective-permute-start.31 = (bf16[2,48,3072]{2,1,0:T(8,128)(2,1)S(1)}, bf16[2,48,3072]{2,1,0:T(8,128)(2,1)S(1)}, u32[]{:S(2)}, u32[]{:S(2)}) collective-permute-start(bf16[2,48,3072]{2,1,0:T(8,128)(2,1)S(1)} %get-tuple-element.162), channel_id=1, source_target_pairs={{0,8},{1,65},{2,10},{3,67},{4,12},{5,69},{6,14},{7,71},{8,0},{9,73... | collective-permute-start | bytes 1769480 | tf_op jit(solution)/shard_map/ppermute | solution.py:75
  200.7 14.2 %collective-permute-start.32 = (bf16[2,48,3072]{2,1,0:T(8,128)(2,1)S(1)}, bf16[2,48,3072]{2,1,0:T(8,128)(2,1)S(1)}, u32[]{:S(2)}, u32[]{:S(2)}) collective-permute-start(bf16[2,48,3072]{2,1,0:T(8,128)(2,1)S(1)} %get-tuple-element.163), channel_id=1, source_target_pairs={{0,12},{1,97},{2,14},{3,99},{4,0},{5,101},{6,2},{7,103},{8,4},{9,1... | collective-permute-start | bytes 1769480 | tf_op jit(solution)/shard_map/ppermute | solution.py:75
  202.0 15.9 %collective-permute-start.29 = (f32[16,1536]{1,0:T(8,128)S(1)}, f32[16,1536]{1,0:T(8,128)S(1)}, u32[]{:S(2)}, u32[]{:S(2)}) collective-permute-start(f32[16,1536]{1,0:T(8,128)S(1)} %collective-permute-done.27.refs_2_), channel_id=1, source_target_pairs={{0,1},{1,0},{2,3},{3,2},{4,5},{5,4},{6,7},{7,6},{8,9},{9,8},{10,11... | collective-permute-start | bytes 294920 | tf_op jit(solution)/shard_map/ppermute | solution.py:86
  226.2 12.2 %collective-permute-start.36 = (bf16[448,768]{1,0:T(8,128)(2,1)S(1)}, bf16[448,768]{1,0:T(8,128)(2,1)S(1)}, u32[]{:S(2)}, u32[]{:S(2)}) collective-permute-start(bf16[448,768]{1,0:T(8,128)(2,1)S(1)} %get-tuple-element.168), channel_id=1, source_target_pairs={{0,32},{1,5},{2,34},{3,7},{4,36},{5,9},{6,38},{7,11},{8,40},{9,13}... | collective-permute-start | bytes 2064392 | tf_op jit(solution)/shard_map/ppermute | solution.py:75
  226.9 11.5 %collective-permute-start.37 = (bf16[448,768]{1,0:T(8,128)(2,1)S(1)}, bf16[448,768]{1,0:T(8,128)(2,1)S(1)}, u32[]{:S(2)}, u32[]{:S(2)}) collective-permute-start(bf16[448,768]{1,0:T(8,128)(2,1)S(1)} %get-tuple-element.169), channel_id=1, source_target_pairs={{0,96},{1,13},{2,98},{3,15},{4,100},{5,1},{6,102},{7,3},{8,104},{9... | collective-permute-start | bytes 2064392 | tf_op jit(solution)/shard_map/ppermute | solution.py:75
  229.5 25.8 %collective-permute-start.40 = (bf16[768,1024]{1,0:T(8,128)(2,1)S(1)}, bf16[768,1024]{1,0:T(8,128)(2,1)S(1)}, u32[]{:S(2)}, u32[]{:S(2)}) collective-permute-start(bf16[768,1024]{1,0:T(8,128)(2,1)S(1)} %get-tuple-element.173), channel_id=1, source_target_pairs={{0,32},{1,5},{2,34},{3,7},{4,36},{5,9},{6,38},{7,11},{8,40},{9,13}... | collective-permute-start | bytes 4718600 | tf_op jit(solution)/shard_map/ppermute | solution.py:75
  229.5 25.8 %collective-permute-start.41 = (bf16[768,1024]{1,0:T(8,128)(2,1)S(1)}, bf16[768,1024]{1,0:T(8,128)(2,1)S(1)}, u32[]{:S(2)}, u32[]{:S(2)}) collective-permute-start(bf16[768,1024]{1,0:T(8,128)(2,1)S(1)} %get-tuple-element.174), channel_id=1, source_target_pairs={{0,96},{1,13},{2,98},{3,15},{4,100},{5,1},{6,102},{7,3},{8,104},{9... | collective-permute-start | bytes 4718600 | tf_op jit(solution)/shard_map/ppermute | solution.py:75
  242.8 37.5 %collective-permute-start.38 = (bf16[448,1536]{1,0:T(8,128)(2,1)S(1)}, bf16[448,1536]{1,0:T(8,128)(2,1)S(1)}, u32[]{:S(2)}, u32[]{:S(2)}) collective-permute-start(bf16[448,1536]{1,0:T(8,128)(2,1)S(1)} %get-tuple-element.171), channel_id=1, source_target_pairs={{0,32},{1,5},{2,34},{3,7},{4,36},{5,9},{6,38},{7,11},{8,40},{9,13}... | collective-permute-start | bytes 4128776 | tf_op jit(solution)/shard_map/ppermute | solution.py:75
  243.5 36.9 %collective-permute-start.39 = (bf16[448,1536]{1,0:T(8,128)(2,1)S(1)}, bf16[448,1536]{1,0:T(8,128)(2,1)S(1)}, u32[]{:S(2)}, u32[]{:S(2)}) collective-permute-start(bf16[448,1536]{1,0:T(8,128)(2,1)S(1)} %get-tuple-element.172), channel_id=1, source_target_pairs={{0,96},{1,13},{2,98},{3,15},{4,100},{5,1},{6,102},{7,3},{8,104},{9... | collective-permute-start | bytes 4128776 | tf_op jit(solution)/shard_map/ppermute | solution.py:75
  246.2 18.0 %collective-permute-start.45 = (bf16[48,3072]{1,0:T(8,128)(2,1)S(1)}, bf16[48,3072]{1,0:T(8,128)(2,1)S(1)}, u32[]{:S(2)}, u32[]{:S(2)}) collective-permute-start(bf16[48,3072]{1,0:T(8,128)(2,1)S(1)} %get-tuple-element.179), channel_id=1, source_target_pairs={{0,16},{1,17},{2,18},{3,19},{4,20},{5,21},{6,22},{7,23},{8,24},{9,... | collective-permute-start | bytes 884744 | tf_op jit(solution)/shard_map/ppermute | solution.py:75
  260.6 10.9 %collective-permute-start.42 = (bf16[768,256]{1,0:T(8,128)(2,1)S(1)}, bf16[768,256]{1,0:T(8,128)(2,1)S(1)}, u32[]{:S(2)}, u32[]{:S(2)}) collective-permute-start(bf16[768,256]{1,0:T(8,128)(2,1)S(1)} %get-tuple-element.176), channel_id=1, source_target_pairs={{0,4},{1,33},{2,6},{3,35},{4,8},{5,37},{6,10},{7,39},{8,12},{9,41}... | collective-permute-start | bytes 1179656 | tf_op jit(solution)/shard_map/ppermute | solution.py:75
  262.0 14.8 %collective-permute-start.43 = (bf16[768,256]{1,0:T(8,128)(2,1)S(1)}, bf16[768,256]{1,0:T(8,128)(2,1)S(1)}, u32[]{:S(2)}, u32[]{:S(2)}) collective-permute-start(bf16[768,256]{1,0:T(8,128)(2,1)S(1)} %get-tuple-element.177), channel_id=1, source_target_pairs={{0,8},{1,65},{2,10},{3,67},{4,12},{5,69},{6,14},{7,71},{8,0},{9,73... | collective-permute-start | bytes 1179656 | tf_op jit(solution)/shard_map/ppermute | solution.py:75
  264.2 12.7 %collective-permute-start.44 = (bf16[768,256]{1,0:T(8,128)(2,1)S(1)}, bf16[768,256]{1,0:T(8,128)(2,1)S(1)}, u32[]{:S(2)}, u32[]{:S(2)}) collective-permute-start(bf16[768,256]{1,0:T(8,128)(2,1)S(1)} %get-tuple-element.178), channel_id=1, source_target_pairs={{0,12},{1,97},{2,14},{3,99},{4,0},{5,101},{6,2},{7,103},{8,4},{9,1... | collective-permute-start | bytes 1179656 | tf_op jit(solution)/shard_map/ppermute | solution.py:75
  286.0 14.1 %collective-permute-start.46 = (bf16[160,1536]{1,0:T(8,128)(2,1)S(1)}, bf16[160,1536]{1,0:T(8,128)(2,1)S(1)}, u32[]{:S(2)}, u32[]{:S(2)}) collective-permute-start(bf16[160,1536]{1,0:T(8,128)(2,1)S(1)} %get-tuple-element.183), channel_id=1, source_target_pairs={{0,4},{1,33},{2,6},{3,35},{4,8},{5,37},{6,10},{7,39},{8,12},{9,41}... | collective-permute-start | bytes 1474568 | tf_op jit(solution)/shard_map/ppermute | solution.py:75
  286.0 15.4 %collective-permute-start.47 = (bf16[160,1536]{1,0:T(8,128)(2,1)S(1)}, bf16[160,1536]{1,0:T(8,128)(2,1)}, u32[]{:S(2)}, u32[]{:S(2)}) collective-permute-start(bf16[160,1536]{1,0:T(8,128)(2,1)S(1)} %get-tuple-element.184), channel_id=1, source_target_pairs={{0,8},{1,65},{2,10},{3,67},{4,12},{5,69},{6,14},{7,71},{8,0},{9,73... | collective-permute-start | bytes 1474568 | tf_op jit(solution)/shard_map/ppermute | solution.py:75
  289.2 13.2 %collective-permute-start.48 = (bf16[160,1536]{1,0:T(8,128)(2,1)S(1)}, bf16[160,1536]{1,0:T(8,128)(2,1)}, u32[]{:S(2)}, u32[]{:S(2)}) collective-permute-start(bf16[160,1536]{1,0:T(8,128)(2,1)S(1)} %get-tuple-element.185), channel_id=1, source_target_pairs={{0,12},{1,97},{2,14},{3,99},{4,0},{5,101},{6,2},{7,103},{8,4},{9,1... | collective-permute-start | bytes 1474568 | tf_op jit(solution)/shard_map/ppermute | solution.py:75
  (134 other events, 868.0 us)
where the time goes:
time: 320 us; the launch traced here: 314 us
  waiting for transfers between devices  100 us (31%)
  Pallas kernels  97.6 us (30%)
  starting transfers between devices  66.4 us (21%)
  local copies, waits for them, and re-layouts  28.5 us (9%)
  matrix products  17.4 us (5%)
    ppermute x25, starting transfers between devices, dp_permute(): return lax.ppermute(values, ('dp', 'tensor'), dp_perm(axis, step))  48.9 us
    ppermute x10, waiting for transfers between devices, swap_chip(): return lax.ppermute(values, 'tensor', CHIP_SWAP)  47.5 us
    ppermute x25, waiting for transfers between devices, dp_permute(): return lax.ppermute(values, ('dp', 'tensor'), dp_perm(axis, step))  45.5 us
    unnamed x241, local copies, waits for them, and re-layouts  27.9 us
    pallas_call x3, Pallas kernels, pair_call(): pl.pallas_call(lambda *refs: kernel(*refs[:len(operands)], *refs[len(oper...  25.9 us
    pallas_call x6, Pallas kernels, chunk_call(): pl.pallas_call(kernel, grid_spec=pltpu.PrefetchScalarGridSpec(num_scalar_...  23.1 us
    pallas_call x7, Pallas kernels, tiled_call(): pl.pallas_call(lambda *refs: kernel(*refs[:count], *refs[count + len(ties...  19 us
    pallas_call x12, Pallas kernels, whole_call(): pl.pallas_call(lambda *refs: kernel(*refs[:count], *refs[count + len(ties...  15.7 us
  transfers between devices with their start and end apart: 51, of which 24 were waited for; matrix products, arithmetic and copies ran while one was open for 2% of the time, Pallas kernels for 21%

commit v1 on v0

--- a/solution.py
+++ b/solution.py
@@ -31,7 +31,7 @@
 FFN_NEXT_MICROS = 8
 MIDDLE_MICROS = 10
 SELF_MICROS = 0
-ATTN_MICROS = 7
+ATTN_MICROS = 3
 TEXT_MICROS = 8
 ATTN_FIRST_MICROS = 0
 
@@ -50,6 +50,14 @@
 
 def dp_perm(axis, step):
     pairs = []
+
+    def moved(place, size):
+        if step == "flip":
+            return place ^ 1
+        if step == "mirror":
+            return size - 1 - place
+        return (place + step) % size
+
     for x in range(RING):
         for z in range(PAIR):
             for y in range(RING):
@@ -58,9 +66,9 @@
                     if axis in ("first", "second"):
                         way = "x" if (tensor % 2 == 0) == (axis == "first") else "y"
                     target = {
-                        "x": ((x + step) % RING, z, y),
-                        "y": (x, z, (y + step) % RING),
-                        "z": (x, (z + step) % PAIR, y),
+                        "x": (moved(x, RING), z, y),
+                        "y": (x, z, moved(y, RING)),
+                        "z": (x, moved(z, PAIR), y),
                     }[way]
                     pairs.append(
                         (
@@ -347,17 +355,29 @@
     return (slice(None), pl.ds(pl.multiple_of(start * size, size), size))
 
 
+def halving_places(spot):
+    own = spot[2]
+    other = own ^ 1
+    return (own, RING - 1 - own), (other, RING - 1 - other)
+
+
 def ffn_second_kernel(spot, *refs):
-    parts, outs = refs[:-RING], refs[-RING:]
-    for offset in range(RING):
+    parts = refs[:-2]
+    for out, places in zip(refs[-2:], halving_places(spot)):
+        for index, place in enumerate(places):
+            for z in range(PAIR):
+                out[index * PAIR + z] = add_up(parts, z * RING + place).astype(jnp.bfloat16)
+
+
+def ffn_middle_kernel(kept, got, own, sent):
+    for out, start in ((own, 0), (sent, PAIR)):
         for z in range(PAIR):
-            slot = z * RING + (spot[2] + offset) % RING
-            outs[offset][z] = add_up(parts, slot).astype(jnp.bfloat16)
+            out[z] = add_up((kept, got), start + z).astype(jnp.bfloat16)
 
 
 def ffn_third_kernel(spot, *refs):
     for out, z in ((refs[-2], spot[1]), (refs[-1], (spot[1] + 1) % PAIR)):
-        out[...] = add_up(refs[:RING], z).astype(jnp.bfloat16)
+        out[...] = add_up(refs[:-2], z).astype(jnp.bfloat16)
 
 
 def ffn_last_kernel(kept, got, gate_out, up_out, down_out):
@@ -369,20 +389,28 @@
 
 
 def text_second_kernel(spot, *refs):
-    parts, outs = refs[:-RING], refs[-RING:]
+    parts = refs[:-2]
     lanes = parts[0].shape[1] // SLOTS
-    for offset in range(RING):
-        for z in range(PAIR):
-            slot = z * RING + (spot[2] + offset) % RING
-            outs[offset][:, z * lanes : (z + 1) * lanes] = add_up(
-                parts, lane_slice(slot, lanes)
-            ).astype(jnp.bfloat16)
+    for out, places in zip(refs[-2:], halving_places(spot)):
+        for index, place in enumerate(places):
+            for z in range(PAIR):
+                start = (index * PAIR + z) * lanes
+                out[:, start : start + lanes] = add_up(
+                    parts, lane_slice(z * RING + place, lanes)
+                ).astype(jnp.bfloat16)
+
+
+def text_middle_kernel(kept, got, own, sent):
+    wide = own.shape[1]
+    for out, start in ((own, 0), (sent, wide)):
+        index = (slice(None), slice(start, start + wide))
+        out[...] = add_up((kept, got), index).astype(jnp.bfloat16)
 
 
 def text_third_kernel(spot, *refs):
     lanes = refs[-1].shape[1]
     for out, z in ((refs[-2], spot[1]), (refs[-1], (spot[1] + 1) % PAIR)):
-        out[...] = add_up(refs[:RING], lane_slice(z, lanes)).astype(jnp.bfloat16)
+        out[...] = add_up(refs[:-2], lane_slice(z, lanes)).astype(jnp.bfloat16)
 
 
 def text_last_kernel(kept, got, textkey, textvalue):
@@ -764,7 +792,7 @@
         compiler_params=pltpu.CompilerParams(vmem_limit_bytes=VMEM_LIMIT),
         cost_estimate=cost_of(9),
         name="text",
-    )(captions, key_weight, value_weight)
+    )(*[pltpu.with_memory_space_constraint(part, pltpu.HBM) for part in (captions, key_weight, value_weight)])
 
 
 def project_kernel(here, own, far, near, last, mods, gains, segment_q, query_w, key_w, value_w,
@@ -1145,10 +1173,15 @@
     block_rows = width // BLOCKS
     got = [by_slots(part) for part in to_neighbours(ffn_kept, ffn_one, ffn_three)]
     shape = (PAIR, block_rows, 3 * hidden_cols)
-    ffn_stage = tiled_call(
-        ffn_second_kernel, (spot,), got, [(shape, b16)] * RING, "ffn_second",
+    ffn_kept, ffn_sent = tiled_call(
+        ffn_second_kernel,
+        (spot,),
+        got,
+        [((2 * PAIR,) + shape[1:], b16)] * 2,
+        "ffn_second",
         -1,
-        4, (query_grad,)
+        4,
+        (query_grad,),
     )
     upper, lower = back_call(
         [query_grad, key_grad, value_grad], [query_weight, key_weight, value_weight], "attn_back"
@@ -1160,7 +1193,7 @@
         [block_in, grad_middle] + sums + [mods, norm_gains, segment, member],
         [narrow, totals],
         "block_in",
-        (ffn_stage[0],),
+        (ffn_sent,),
         micros=BLOCK_IN_MICROS,
     )
     (stacked,) = whole_call(
@@ -1176,12 +1209,12 @@
         text_lefts, caption_flat, (1, 3, 0), spot, extra=text_passed, ties=(sums_stacked,), micros=TEXT_MICROS
     )
     stacked = gather_tensor(stacked)
-    kept, sent = tiled_call(
-        ffn_third_kernel,
-        (spot,),
-        exchange(ffn_stage, "second"),
-        [(shape[1:], b16)] * 2,
-        "ffn_third",
+    ffn_own, ffn_sent = tiled_call(
+        ffn_middle_kernel,
+        (),
+        [ffn_kept, dp_permute(ffn_sent, "second", "flip")],
+        [(shape, b16)] * 2,
+        "ffn_middle",
         -1,
         2,
         (text_kept,),
@@ -1192,7 +1225,7 @@
         stacked + [mods, norm_gains, cond_rows],
         [((rider_rows(1), width), b16)],
         "pack",
-        (kept,),
+        (ffn_sent,),
     )
     theirs = dp_permute(riders, "z", 1)
     (riders,) = whole_call(
@@ -1204,6 +1237,16 @@
     ]
     (halves_two,) = row_chunks(attn_pairs, (2,), spot, riders=(riders,), micros=ATTN_FIRST_MICROS)
     attn_passed = one_on(halves_two)
+    kept, sent = tiled_call(
+        ffn_third_kernel,
+        (spot,),
+        [ffn_own, dp_permute(ffn_sent, "second", "mirror")],
+        [(shape[1:], b16)] * 2,
+        "ffn_third",
+        -1,
+        2,
+        (halves_two[0],),
+    )
     gate_sum_out, up_sum_out, down_sum_out = whole_call(
         ffn_last_kernel,
         (),
@@ -1215,25 +1258,33 @@
     attn_one, attn_three, attn_kept = row_chunks(
         attn_pairs, (1, 3, 0), spot, extra=attn_passed, ties=(kept,), riders=(riders,), micros=ATTN_MICROS
     )
-    stage = tiled_call(
+    text_own, text_sent = tiled_call(
         text_second_kernel,
         (spot,),
         to_neighbours(text_kept, text_one, text_three),
-        [((2 * inner, PAIR * text_rows), b16)] * RING,
+        [((2 * inner, 2 * PAIR * text_rows), b16)] * 2,
         "text_second",
         0,
         4,
         (attn_kept,),
     )
+    text_own, text_sent = tiled_call(
+        text_middle_kernel,
+        (),
+        [text_own, dp_permute(text_sent, "second", "flip")],
+        [((2 * inner, PAIR * text_rows), b16)] * 2,
+        "text_middle",
+        0,
+        2,
+    )
     kept, sent = tiled_call(
         text_third_kernel,
         (spot,),
-        exchange(stage, "second"),
+        [text_own, dp_permute(text_sent, "second", "mirror")],
         [((2 * inner, text_rows), b16)] * 2,
         "text_third",
         0,
         2,
-        (gate_sum_out,),
     )
     textkey_sum, textvalue_sum = whole_call(
         text_last_kernel,
@@ -1250,7 +1301,7 @@
         "attn_second",
         -1,
         4,
-        (kept,),
+        (text_own,),
     )
     got = exchange(stage, "second")
     kept, sent = tiled_call(

time: 320 us -> 317 us (level)
  starting transfers between devices: 66.4 us -> 56.9 us
  waiting for transfers between devices: 100 us -> 107 us
  Pallas kernels: 97.6 us -> 102 us
  local copies, waits for them, and re-layouts: 28.5 us -> 25 us
    ppermute x25 -> x23, starting transfers between devices: 48.9 us -> 39.5 us  [dp_permute(): return lax.ppermute(values, ('dp', 'tensor'), dp_perm(axis, step))]
    ppermute x25 -> x23, waiting for transfers between devices: 45.5 us -> 49.6 us  [dp_permute(): return lax.ppermute(values, ('dp', 'tensor'), dp_perm(axis, step))]
    unnamed x241 -> x235, local copies, waits for them, and re-layouts: 27.9 us -> 24.4 us
    pallas_call x7 -> x9, Pallas kernels: 19 us -> 21.5 us  [tiled_call(): pl.pallas_call(lambda *refs: kernel(*refs[:count], *refs[count + len(ties...]
  transfers between devices with their start and end apart: 51 -> 49, of which waited for: 24 -> 21; matrix products, arithmetic and copies ran while one was open for 2% -> 2% of each run, Pallas kernels for 21% -> 24%
where the time goes in v1:
time: 317 us; the launch traced here: 312 us
  waiting for transfers between devices  107 us (34%)
  Pallas kernels  102 us (32%)
  starting transfers between devices  56.9 us (18%)
  local copies, waits for them, and re-layouts  25 us (8%)
  matrix products  17.4 us (5%)
    ppermute x10, waiting for transfers between devices, swap_chip(): return lax.ppermute(values, 'tensor', CHIP_SWAP)  50.4 us
    ppermute x23, waiting for transfers between devices, dp_permute(): return lax.ppermute(values, ('dp', 'tensor'), dp_perm(axis, step))  49.6 us
    ppermute x23, starting transfers between devices, dp_permute(): return lax.ppermute(values, ('dp', 'tensor'), dp_perm(axis, step))  39.5 us
    pallas_call x3, Pallas kernels, pair_call(): pl.pallas_call(lambda *refs: kernel(*refs[:len(operands)], *refs[len(oper...  25.9 us
    unnamed x235, local copies, waits for them, and re-layouts  24.4 us
    pallas_call x6, Pallas kernels, chunk_call(): pl.pallas_call(kernel, grid_spec=pltpu.PrefetchScalarGridSpec(num_scalar_...  23.1 us
    pallas_call x9, Pallas kernels, tiled_call(): pl.pallas_call(lambda *refs: kernel(*refs[:count], *refs[count + len(ties...  21.5 us
    pallas_call x12, Pallas kernels, whole_call(): pl.pallas_call(lambda *refs: kernel(*refs[:count], *refs[count + len(ties...  15.7 us
  transfers between devices with their start and end apart: 49, of which 21 were waited for; matrix products, arithmetic and copies ran while one was open for 2% of the time, Pallas kernels for 24%

profile of v1, /device:TPU:0, one launch (start us, length us, event | category | flops | bytes accessed | tf_op | source)
XLA Modules:
  0.0 312.1 jit_solution(10761954961753661087)
XLA Ops:
  0.7 3.2 %fusion.16 = f32[3,1536]{1,0:T(4,128)} fusion(bf16[1024,1536]{1,0:T(8,128)(2,1)} %param.25, bf16[3,1024]{1,0:T(4,128)(2,1)} %param.21), kind=kOutput, calls=%fused_computation.46 | convolution fusion | flops 9455616 | bytes 3170304 | tf_op jit(solution)/shard_map/dot_general | solution.py:1046
  6.4 9.3 %text.1 = (f32[768,384]{1,0:T(8,128)S(1)}, bf16[768,384]{1,0:T(8,128)(2,1)S(1)}) custom-call(bf16[768,4096]{1,0:T(8,128)(2,1)} %bitcast.38, bf16[4096,384]{1,0:T(8,128)(2,1)} %key_weight.1, bf16[4096,384]{1,0:T(8,128)(2,1)} %value_weight.1), custom_call_target="tpu_custom_call" | custom-call | flops 8999999488 | tf_op jit(solution)/shard_map/text/pallas_call | solution.py:778
  23.9 4.9 %project.1 = (bf16[512,1536]{1,0:T(8,128)(2,1)S(1)}, f32[512,384]{1,0:T(8,128)S(1)}, f32[512,384]{1,0:T(8,128)S(1)}, bf16[512,384]{1,0:T(8,128)(2,1)S(1)}) custom-call(s32[1]{0:T(128)} %bitcast.refs_0_, bf16[128,1536]{1,0:T(8,128)(2,1)S(1)} %copy-done.25, bf16[128,1536]{1,0:T(8,128)(2,1)} %collective-permute-done.refs_2_, ...), custom_call_target="tpu_custom_call" | custom-call | flops 6000000000 | tf_op jit(solution)/shard_map/project/pallas_call | solution.py:460
  30.0 9.9 %attend.1 = (bf16[512,384]{1,0:T(8,128)(2,1)S(1)}, bf16[512,384]{1,0:T(8,128)(2,1)S(1)}, bf16[768,384]{1,0:T(8,128)(2,1)S(1)}, bf16[512,384]{1,0:T(8,128)(2,1)S(...) custom-call(f32[512,384]{1,0:T(8,128)S(1)} %get-tuple-element.109.refs_0_, ...), custom_call_target="tpu_custom_call" | custom-call | flops 11000000512 | tf_op jit(solution)/shard_map/attend/pallas_call | solution.py:670
  45.9 9.4 %collective-permute-done.7.refs_4_ = bf16[128,1536]{1,0:T(8,128)(2,1)S(1)} collective-permute-done((bf16[128,1536]{1,0:T(8,128)(2,1)S(1)}, bf16[128,1536]{1,0:T(8,128)(2,1)S(1)}, u32[]{:S(2)}, u32[]{:S(2)}) %collective-permute-start.7) | collective-permute-done | bytes 393248 | tf_op jit(solution)/shard_map/ppermute | solution.py:98
  58.0 8.8 %collective-permute-done.8 = bf16[128,1536]{1,0:T(8,128)(2,1)S(1)} collective-permute-done((bf16[128,1536]{1,0:T(8,128)(2,1)S(1)}, bf16[128,1536]{1,0:T(8,128)(2,1)S(1)}, u32[]{:S(2)}, u32[]{:S(2)}) %collective-permute-start.8) | collective-permute-done | bytes 393248 | tf_op jit(solution)/shard_map/ppermute | solution.py:98
  79.1 9.0 %collective-permute-done.12.refs_4_ = bf16[128,1536]{1,0:T(8,128)(2,1)S(1)} collective-permute-done((bf16[128,1536]{1,0:T(8,128)(2,1)S(1)}, bf16[128,1536]{1,0:T(8,128)(2,1)S(1)}, u32[]{:S(2)}, u32[]{:S(2)}) %collective-permute-start.12) | collective-permute-done | bytes 393248 | tf_op jit(solution)/shard_map/ppermute | solution.py:98
  91.1 8.8 %collective-permute-done.13 = bf16[128,1536]{1,0:T(8,128)(2,1)S(1)} collective-permute-done((bf16[128,1536]{1,0:T(8,128)(2,1)S(1)}, bf16[128,1536]{1,0:T(8,128)(2,1)S(1)}, u32[]{:S(2)}, u32[]{:S(2)}) %collective-permute-start.13) | collective-permute-done | bytes 393248 | tf_op jit(solution)/shard_map/ppermute | solution.py:98
  101.7 2.4 multiply_convert_fusion
  113.4 7.7 %collective-permute-done.17.refs_5_ = bf16[128,1536]{1,0:T(8,128)(2,1)} collective-permute-done((bf16[128,1536]{1,0:T(8,128)(2,1)S(1)}, bf16[128,1536]{1,0:T(8,128)(2,1)}, u32[]{:S(2)}, u32[]{:S(2)}) %collective-permute-start.17) | collective-permute-done | bytes 393248 | tf_op jit(solution)/shard_map/ppermute | solution.py:98
  121.2 2.5 middle_back.1
  130.7 3.6 %collective-permute-done.18 = bf16[128,1536]{1,0:T(8,128)(2,1)S(1)} collective-permute-done((bf16[128,1536]{1,0:T(8,128)(2,1)S(1)}, bf16[128,1536]{1,0:T(8,128)(2,1)S(1)}, u32[]{:S(2)}, u32[]{:S(2)}) %collective-permute-start.18) | collective-permute-done | bytes 393248 | tf_op jit(solution)/shard_map/ppermute | solution.py:98
  138.2 8.2 %cross_back.1 = (f32[512,384]{1,0:T(8,128)S(1)}, bf16[384,768]{1,0:T(8,128)(2,1)S(1)}, bf16[384,768]{1,0:T(8,128)(2,1)S(1)}, f32[1,384]{1,0:T(1,128)S(1)}, f32[1,384]{1,0:T(1,128)S(1)}) custom-call(bf16[512,384]{1,0:T(8,128)(2,1)S(1)} %copy-done.55, bf16[768,384]{1,0:T(8,128)(2,1)S(1)} %copy-done.93, bf16[768,384]{1,0:T(8,128)(2,1)S(1)} %copy-done.87, ...), custom_call_target="tpu_custom_call" | custom-call | flops 10000000000 | tf_op jit(solution)/shard_map/cross_back/pallas_call | solution.py:670
  146.5 5.5 %row_chunks.5 = (bf16[384,3072]{1,0:T(8,128)(2,1)S(1)}, bf16[384,3072]{1,0:T(8,128)(2,1)S(1)}, bf16[384,3072]{1,0:T(8,128)(2,1)S(1)}) custom-call(s32[4]{0:T(128)S(1)} %pad_add_fusion.spot_ref.refs_0_, bf16[32,48,512]{2,1,0:T(8,128)(2,1)S(1)} %bitcast.65, bf16[32,48,512]{2,1,0:T(8,128)(2,1)S(1)} %bitcast.66, bf16[32,48,512]{2,1,0:T(8,128)(2,1)S(1)} %bitcast.67, ...), custom_call_target="tpu_custom_call" | custom-call | flops 8000000000 | tf_op jit(solution)/shard_map/row_chunks/pallas_call | solution.py:202
  158.0 7.9 %self_back.1 = (bf16[512,384]{1,0:T(8,128)(2,1)S(1)}, bf16[512,384]{1,0:T(8,128)(2,1)S(1)}, bf16[512,384]{1,0:T(8,128)(2,1)S(1)}, f32[2,384]{1,0:T(2,128)S(1)}) custom-call(bf16[512,384]{1,0:T(8,128)(2,1)S(1)} %copy-done.55, bf16[512,384]{1,0:T(8,128)(2,1)S(1)} %copy-done.57, bf16[512,384]{1,0:T(8,128)(2,1)S(1)} %copy-done.53, f32[512,384]{1,0:T(8,128)S(1)} %copy-done.37, ...), custom_call_target="tpu_custom_call" | custom-call | tf_op jit(solution)/shard_map/self_back/pallas_call | solution.py:670
  165.9 3.1 %attn_back.1 = (bf16[256,1536]{1,0:T(8,128)(2,1)S(1)}, bf16[256,1536]{1,0:T(8,128)(2,1)S(1)}) custom-call(bf16[512,384]{1,0:T(8,128)(2,1)S(1)} %get-tuple-element.145.refs_0_.refs_4_.refs_16_, bf16[512,384]{1,0:T(8,128)(2,1)S(1)} %get-tuple-element.146.refs_1_.refs_17_, bf16[512,384]{1,0:T(8,128)(2,1)S(1)} %get-tuple-element.147.refs_2_.refs_18_, ...), custom_call_target="tpu_custom_call" | custom-call | tf_op jit(solution)/shard_map/attn_back/pallas_call | solution.py:998
  174.1 8.0 %collective-permute-done.25 = bf16[384,3072]{1,0:T(8,128)(2,1)S(1)} collective-permute-done((bf16[384,3072]{1,0:T(8,128)(2,1)S(1)}, bf16[384,3072]{1,0:T(8,128)(2,1)S(1)}, u32[]{:S(2)}, u32[]{:S(2)}) %collective-permute-start.25) | collective-permute-done | bytes 2359328 | tf_op jit(solution)/shard_map/ppermute | solution.py:83
  184.3 4.1 %ffn_second.1 = (bf16[4,48,3072]{2,1,0:T(8,128)(2,1)S(1)}, bf16[4,48,3072]{2,1,0:T(8,128)(2,1)S(1)}) custom-call(s32[4]{0:T(128)S(1)} %pad_add_fusion.spot_ref.refs_0_, bf16[8,48,3072]{2,1,0:T(8,128)(2,1)} %bitcast.121, bf16[8,48,3072]{2,1,0:T(8,128)(2,1)} %bitcast.123, bf16[8,48,3072]{2,1,0:T(8,128)(2,1)} %bitcast.124, ...), custom_call_target="tpu_custom_call" | custom-call | tf_op jit(solution)/shard_map/ffn_second/pallas_call | solution.py:483
  193.2 3.1 collective-permute-done.27.refs_2_
  196.3 7.0 %column_chunks.3 = (bf16[768,1024]{1,0:T(8,128)(2,1)S(1)}, bf16[768,1024]{1,0:T(8,128)(2,1)S(1)}, bf16[768,1024]{1,0:T(8,128)(2,1)S(1)}) custom-call(s32[4]{0:T(128)S(1)} %pad_add_fusion.spot_ref.refs_0_, bf16[384,768]{1,0:T(8,128)(2,1)S(1)} %get-tuple-element.139.refs_21_.refs_0_, bf16[384,768]{1,0:T(8,128)(2,1)S(1)} %get-tuple-element.140.refs_1_, ...), custom_call_target="tpu_custom_call" | custom-call | flops 8000000000 | tf_op jit(solution)/shard_map/column_chunks/pallas_call | solution.py:202
  210.1 3.7 %collective-permute-start.33 = (bf16[32,1536]{1,0:T(8,128)(2,1)S(1)}, bf16[32,1536]{1,0:T(8,128)(2,1)S(1)}, u32[]{:S(2)}, u32[]{:S(2)}) collective-permute-start(bf16[32,1536]{1,0:T(8,128)(2,1)S(1)} %pack.1.refs_0_), channel_id=1, source_target_pairs={{0,16},{1,17},{2,18},{3,19},{4,20},{5,21},{6,22},{7,23},{8,24},{9,... | collective-permute-start | bytes 294920 | tf_op jit(solution)/shard_map/ppermute | solution.py:83
  222.5 15.6 %collective-permute-done.36.refs_2_ = bf16[2,48,3072]{2,1,0:T(8,128)(2,1)S(1)} collective-permute-done((bf16[2,48,3072]{2,1,0:T(8,128)(2,1)S(1)}, bf16[2,48,3072]{2,1,0:T(8,128)(2,1)S(1)}, u32[]{:S(2)}, u32[]{:S(2)}) %collective-permute-start.36) | collective-permute-done | bytes 589856 | tf_op jit(solution)/shard_map/ppermute | solution.py:83
  240.3 4.4 %row_chunks.7 = (bf16[448,1536]{1,0:T(8,128)(2,1)S(1)}, bf16[448,1536]{1,0:T(8,128)(2,1)S(1)}, bf16[448,1536]{1,0:T(8,128)(2,1)S(1)}) custom-call(s32[4]{0:T(128)S(1)} %pad_add_fusion.spot_ref.refs_0_, bf16[32,48,512]{2,1,0:T(8,128)(2,1)S(1)} %bitcast.97, bf16[32,48,512]{2,1,0:T(8,128)(2,1)S(1)} %bitcast.98, bf16[32,48,512]{2,1,0:T(8,128)(2,1)S(1)} %bitcast.99, ...), custom_call_target="tpu_custom_call" | custom-call | flops 3000000000 | tf_op jit(solution)/shard_map/row_chunks/pallas_call | solution.py:202
  245.2 2.8 collective-permute-start.38
  249.7 3.6 %text_second.1 = (bf16[768,512]{1,0:T(8,128)(2,1)S(1)}, bf16[768,512]{1,0:T(8,128)(2,1)S(1)}) custom-call(s32[4]{0:T(128)S(1)} %pad_add_fusion.spot_ref.refs_0_, bf16[768,1024]{1,0:T(8,128)(2,1)} %copy-done.7, bf16[768,1024]{1,0:T(8,128)(2,1)} %copy-done.101, bf16[768,1024]{1,0:T(8,128)(2,1)} %copy-done.102, ...), custom_call_target="tpu_custom_call" | custom-call | tf_op jit(solution)/shard_map/text_second/pallas_call | solution.py:483
  254.2 15.5 %collective-permute-done.41.refs_1_ = bf16[768,512]{1,0:T(8,128)(2,1)S(1)} collective-permute-done((bf16[768,512]{1,0:T(8,128)(2,1)S(1)}, bf16[768,512]{1,0:T(8,128)(2,1)S(1)}, u32[]{:S(2)}, u32[]{:S(2)}) %collective-permute-start.41) | collective-permute-done | bytes 786464 | tf_op jit(solution)/shard_map/ppermute | solution.py:83
  275.6 3.3 %attn_second.1 = (bf16[160,1536]{1,0:T(8,128)(2,1)S(1)}, bf16[160,1536]{1,0:T(8,128)(2,1)S(1)}, bf16[160,1536]{1,0:T(8,128)(2,1)S(1)}, bf16[160,1536]{1,0:T(8,128)(2,1)S(1)}) custom-call(s32[4]{0:T(128)S(1)} %pad_add_fusion.spot_ref.refs_0_, bf16[32,1536]{1,0:T(8,128)(2,1)} %copy-done.28, bf16[448,1536]{1,0:T(8,128)(2,1)} %copy-done.8, ...), custom_call_target="tpu_custom_call" | custom-call | tf_op jit(solution)/shard_map/attn_second/pallas_call | solution.py:483
  283.5 3.6 %collective-permute-start.48 = (bf16[48,3072]{1,0:T(8,128)(2,1)S(1)}, bf16[48,3072]{1,0:T(8,128)(2,1)S(1)}, u32[]{:S(2)}, u32[]{:S(2)}) collective-permute-start(bf16[48,3072]{1,0:T(8,128)(2,1)S(1)} %get-tuple-element.197), channel_id=1, source_target_pairs={{0,16},{1,17},{2,18},{3,19},{4,20},{5,21},{6,22},{7,23},{8,24},{9,... | collective-permute-start | bytes 884744 | tf_op jit(solution)/shard_map/ppermute | solution.py:83
  289.3 5.0 %collective-permute-done.48.refs_1_ = bf16[48,3072]{1,0:T(8,128)(2,1)S(1)} collective-permute-done((bf16[48,3072]{1,0:T(8,128)(2,1)S(1)}, bf16[48,3072]{1,0:T(8,128)(2,1)S(1)}, u32[]{:S(2)}, u32[]{:S(2)}) %collective-permute-start.48) | collective-permute-done | bytes 294944 | tf_op jit(solution)/shard_map/ppermute | solution.py:83
  296.0 2.6 collective-permute-done.47.refs_1_
  302.1 3.8 %collective-permute-start.45 = (bf16[48,1536]{1,0:T(8,128)(2,1)S(1)}, bf16[48,1536]{1,0:T(8,128)(2,1)S(1)}, u32[]{:S(2)}, u32[]{:S(2)}) collective-permute-start(bf16[48,1536]{1,0:T(8,128)(2,1)S(1)} %get-tuple-element.185), channel_id=1, source_target_pairs={{0,16},{1,17},{2,18},{3,19},{4,20},{5,21},{6,22},{7,23},{8,24},{9,... | collective-permute-start | bytes 442376 | tf_op jit(solution)/shard_map/ppermute | solution.py:83
  305.9 2.5 ada.1
  (362 shorter events, 116.6 us)
Async XLA Ops:
  3.9 13.7 %collective-permute-start.4 = (f32[3,1536]{1,0:T(4,128)}, f32[3,1536]{1,0:T(4,128)}, u32[]{:S(2)}, u32[]{:S(2)}) collective-permute-start(f32[3,1536]{1,0:T(4,128)} %fusion.16), channel_id=1, source_target_pairs={{0,2},{2,0},{1,3},{3,1},{4,6},{6,4},{5,7},{7,5},{8,10},{10,8},{9,1... | collective-permute-start | bytes 55304 | tf_op jit(solution)/shard_map/ppermute | solution.py:98
  5.9 17.0 %collective-permute-start.3 = (f32[3,1536]{1,0:T(4,128)}, f32[3,1536]{1,0:T(4,128)}, u32[]{:S(2)}, u32[]{:S(2)}) collective-permute-start(f32[3,1536]{1,0:T(4,128)} %fusion.16), channel_id=1, source_target_pairs={{0,1},{1,0},{2,3},{3,2},{4,5},{5,4},{6,7},{7,6},{8,9},{9,8},{10,11... | collective-permute-start | bytes 55304 | tf_op jit(solution)/shard_map/ppermute | solution.py:94
  5.9 17.9 %collective-permute-start.1 = (bf16[128,1536]{1,0:T(8,128)(2,1)S(1)}, bf16[128,1536]{1,0:T(8,128)(2,1)}, u32[]{:S(2)}, u32[]{:S(2)}) collective-permute-start(bf16[128,1536]{1,0:T(8,128)(2,1)S(1)} %copy-done.25), channel_id=1, source_target_pairs={{0,1},{1,0},{2,3},{3,2},{4,5},{5,4},{6,7},{7,6},{8,9},{9,8},{10,11... | collective-permute-start | bytes 1179656 | tf_op jit(solution)/shard_map/ppermute | solution.py:94
  6.4 11.2 %collective-permute-start = (bf16[128,1536]{1,0:T(8,128)(2,1)S(1)}, bf16[128,1536]{1,0:T(8,128)(2,1)}, u32[]{:S(2)}, u32[]{:S(2)}) collective-permute-start(bf16[128,1536]{1,0:T(8,128)(2,1)S(1)} %copy-done.25), channel_id=1, source_target_pairs={{0,2},{2,0},{1,3},{3,1},{4,6},{6,4},{5,7},{7,5},{8,10},{10,8},{9,1... | collective-permute-start | bytes 1179656 | tf_op jit(solution)/shard_map/ppermute | solution.py:98
  43.8 11.5 %collective-permute-start.7 = (bf16[128,1536]{1,0:T(8,128)(2,1)S(1)}, bf16[128,1536]{1,0:T(8,128)(2,1)S(1)}, u32[]{:S(2)}, u32[]{:S(2)}) collective-permute-start(bf16[128,1536]{1,0:T(8,128)(2,1)S(1)} %add_convert_fusion.3.rest_0_), channel_id=1, source_target_pairs={{0,2},{2,0},{1,3},{3,1},{4,6},{6,4},{5,7},{7,5},{8,10},{10,8},{9,1... | collective-permute-start | bytes 1179656 | tf_op jit(solution)/shard_map/ppermute | solution.py:98
  56.1 10.7 %collective-permute-start.8 = (bf16[128,1536]{1,0:T(8,128)(2,1)S(1)}, bf16[128,1536]{1,0:T(8,128)(2,1)S(1)}, u32[]{:S(2)}, u32[]{:S(2)}) collective-permute-start(bf16[128,1536]{1,0:T(8,128)(2,1)S(1)} %get-tuple-element.124), channel_id=1, source_target_pairs={{0,2},{2,0},{1,3},{3,1},{4,6},{6,4},{5,7},{7,5},{8,10},{10,8},{9,1... | collective-permute-start | bytes 1179656 | tf_op jit(solution)/shard_map/ppermute | solution.py:98
  76.8 11.2 %collective-permute-start.12 = (bf16[128,1536]{1,0:T(8,128)(2,1)S(1)}, bf16[128,1536]{1,0:T(8,128)(2,1)S(1)}, u32[]{:S(2)}, u32[]{:S(2)}) collective-permute-start(bf16[128,1536]{1,0:T(8,128)(2,1)S(1)} %add_convert_fusion.2.rest_0_), channel_id=1, source_target_pairs={{0,2},{2,0},{1,3},{3,1},{4,6},{6,4},{5,7},{7,5},{8,10},{10,8},{9,1... | collective-permute-start | bytes 1179656 | tf_op jit(solution)/shard_map/ppermute | solution.py:98
  109.5 11.6 %collective-permute-start.17 = (bf16[128,1536]{1,0:T(8,128)(2,1)S(1)}, bf16[128,1536]{1,0:T(8,128)(2,1)}, u32[]{:S(2)}, u32[]{:S(2)}) collective-permute-start(bf16[128,1536]{1,0:T(8,128)(2,1)S(1)} %add_convert_fusion.1.rest_0_.refs_19_), channel_id=1, source_target_pairs={{0,2},{2,0},{1,3},{3,1},{4,6},{6,4},{5,7},{7,5},{8,10},{10,8},{9,1... | collective-permute-start | bytes 1179656 | tf_op jit(solution)/shard_map/ppermute | solution.py:98
  123.7 10.6 %collective-permute-start.18 = (bf16[128,1536]{1,0:T(8,128)(2,1)S(1)}, bf16[128,1536]{1,0:T(8,128)(2,1)S(1)}, u32[]{:S(2)}, u32[]{:S(2)}) collective-permute-start(bf16[128,1536]{1,0:T(8,128)(2,1)S(1)} %get-tuple-element.132), channel_id=1, source_target_pairs={{0,2},{2,0},{1,3},{3,1},{4,6},{6,4},{5,7},{7,5},{8,10},{10,8},{9,1... | collective-permute-start | bytes 1179656 | tf_op jit(solution)/shard_map/ppermute | solution.py:98
  127.3 19.1 %collective-permute-start.21 = (bf16[384,1536]{1,0:T(8,128)(2,1)S(1)}, bf16[384,1536]{1,0:T(8,128)(2,1)S(1)}, u32[]{:S(2)}, u32[]{:S(2)}) collective-permute-start(bf16[384,1536]{1,0:T(8,128)(2,1)S(1)} %get-tuple-element.141), channel_id=1, source_target_pairs={{0,32},{1,5},{2,34},{3,7},{4,36},{5,9},{6,38},{7,11},{8,40},{9,13}... | collective-permute-start | bytes 3538952 | tf_op jit(solution)/shard_map/ppermute | solution.py:83
  128.9 17.5 %collective-permute-start.22 = (bf16[384,1536]{1,0:T(8,128)(2,1)S(1)}, bf16[384,1536]{1,0:T(8,128)(2,1)S(1)}, u32[]{:S(2)}, u32[]{:S(2)}) collective-permute-start(bf16[384,1536]{1,0:T(8,128)(2,1)S(1)} %get-tuple-element.142), channel_id=1, source_target_pairs={{0,96},{1,13},{2,98},{3,15},{4,100},{5,1},{6,102},{7,3},{8,104},{9... | collective-permute-start | bytes 3538952 | tf_op jit(solution)/shard_map/ppermute | solution.py:83
  152.0 30.1 %collective-permute-start.25 = (bf16[384,3072]{1,0:T(8,128)(2,1)S(1)}, bf16[384,3072]{1,0:T(8,128)(2,1)S(1)}, u32[]{:S(2)}, u32[]{:S(2)}) collective-permute-start(bf16[384,3072]{1,0:T(8,128)(2,1)S(1)} %get-tuple-element.150), channel_id=1, source_target_pairs={{0,32},{1,5},{2,34},{3,7},{4,36},{5,9},{6,38},{7,11},{8,40},{9,13}... | collective-permute-start | bytes 7077896 | tf_op jit(solution)/shard_map/ppermute | solution.py:83
  153.5 29.0 %collective-permute-start.26 = (bf16[384,3072]{1,0:T(8,128)(2,1)S(1)}, bf16[384,3072]{1,0:T(8,128)(2,1)S(1)}, u32[]{:S(2)}, u32[]{:S(2)}) collective-permute-start(bf16[384,3072]{1,0:T(8,128)(2,1)S(1)} %get-tuple-element.151), channel_id=1, source_target_pairs={{0,96},{1,13},{2,98},{3,15},{4,100},{5,1},{6,102},{7,3},{8,104},{9... | collective-permute-start | bytes 7077896 | tf_op jit(solution)/shard_map/ppermute | solution.py:83
  169.2 27.1 %collective-permute-start.31 = (bf16[384,1024]{1,0:T(8,128)(2,1)S(1)}, bf16[384,1024]{1,0:T(8,128)(2,1)S(1)}, u32[]{:S(2)}, u32[]{:S(2)}) collective-permute-start(bf16[384,1024]{1,0:T(8,128)(2,1)S(1)} %get-tuple-element.144.refs_14_.rest_0_), channel_id=1, source_target_pairs={{0,32},{1,5},{2,34},{3,7},{4,36},{5,9},{6,38},{7,11},{8,40},{9,13}... | collective-permute-start | bytes 2359304 | tf_op jit(solution)/shard_map/ppermute | solution.py:83
  170.3 25.9 %collective-permute-start.32 = (bf16[384,1024]{1,0:T(8,128)(2,1)S(1)}, bf16[384,1024]{1,0:T(8,128)(2,1)S(1)}, u32[]{:S(2)}, u32[]{:S(2)}) collective-permute-start(bf16[384,1024]{1,0:T(8,128)(2,1)S(1)} %get-tuple-element.162), channel_id=1, source_target_pairs={{0,96},{1,13},{2,98},{3,15},{4,100},{5,1},{6,102},{7,3},{8,104},{9... | collective-permute-start | bytes 2359304 | tf_op jit(solution)/shard_map/ppermute | solution.py:83
  172.6 17.4 %collective-permute-start.24 = (bf16[128,1536]{1,0:T(8,128)(2,1)S(1)}, bf16[128,1536]{1,0:T(8,128)(2,1)S(1)}, u32[]{:S(2)}, u32[]{:S(2)}) collective-permute-start(bf16[128,1536]{1,0:T(8,128)(2,1)S(1)} %add_convert_fusion), channel_id=1, source_target_pairs={{0,2},{2,0},{1,3},{3,1},{4,6},{6,4},{5,7},{7,5},{8,10},{10,8},{9,1... | collective-permute-start | bytes 1179656 | tf_op jit(solution)/shard_map/ppermute | solution.py:98
  188.4 18.5 %collective-permute-start.30 = (bf16[4,48,3072]{2,1,0:T(8,128)(2,1)S(1)}, bf16[4,48,3072]{2,1,0:T(8,128)(2,1)S(1)}, u32[]{:S(2)}, u32[]{:S(2)}) collective-permute-start(bf16[4,48,3072]{2,1,0:T(8,128)(2,1)S(1)} %get-tuple-element.152.refs_10_), channel_id=1, source_target_pairs={{0,4},{1,33},{2,6},{3,35},{4,0},{5,37},{6,2},{7,39},{8,12},{9,41},... | collective-permute-start | bytes 3538952 | tf_op jit(solution)/shard_map/ppermute | solution.py:83
  193.2 16.8 %collective-permute-start.28 = (f32[16,1536]{1,0:T(8,128)S(1)}, f32[16,1536]{1,0:T(8,128)S(1)}, u32[]{:S(2)}, u32[]{:S(2)}) collective-permute-start(f32[16,1536]{1,0:T(8,128)S(1)} %stack_sums.1.refs_12_.refs_1_), channel_id=1, source_target_pairs={{0,1},{1,0},{2,3},{3,2},{4,5},{5,4},{6,7},{7,6},{8,9},{9,8},{10,11... | collective-permute-start | bytes 294920 | tf_op jit(solution)/shard_map/ppermute | solution.py:94
  196.3 13.7 %collective-permute-start.29 = (f32[16,1536]{1,0:T(8,128)S(1)}, f32[16,1536]{1,0:T(8,128)S(1)}, u32[]{:S(2)}, u32[]{:S(2)}) collective-permute-start(f32[16,1536]{1,0:T(8,128)S(1)} %collective-permute-done.27.refs_2_), channel_id=1, source_target_pairs={{0,1},{1,0},{2,3},{3,2},{4,5},{5,4},{6,7},{7,6},{8,9},{9,8},{10,11... | collective-permute-start | bytes 294920 | tf_op jit(solution)/shard_map/ppermute | solution.py:94
  203.3 44.7 %collective-permute-start.39 = (bf16[768,1024]{1,0:T(8,128)(2,1)S(1)}, bf16[768,1024]{1,0:T(8,128)(2,1)S(1)}, u32[]{:S(2)}, u32[]{:S(2)}) collective-permute-start(bf16[768,1024]{1,0:T(8,128)(2,1)S(1)} %get-tuple-element.173), channel_id=1, source_target_pairs={{0,32},{1,5},{2,34},{3,7},{4,36},{5,9},{6,38},{7,11},{8,40},{9,13}... | collective-permute-start | bytes 4718600 | tf_op jit(solution)/shard_map/ppermute | solution.py:83
  204.9 43.1 %collective-permute-start.40 = (bf16[768,1024]{1,0:T(8,128)(2,1)S(1)}, bf16[768,1024]{1,0:T(8,128)(2,1)S(1)}, u32[]{:S(2)}, u32[]{:S(2)}) collective-permute-start(bf16[768,1024]{1,0:T(8,128)(2,1)S(1)} %get-tuple-element.174), channel_id=1, source_target_pairs={{0,96},{1,13},{2,98},{3,15},{4,100},{5,1},{6,102},{7,3},{8,104},{9... | collective-permute-start | bytes 4718600 | tf_op jit(solution)/shard_map/ppermute | solution.py:83
  218.5 21.8 %collective-permute-start.35 = (bf16[448,768]{1,0:T(8,128)(2,1)S(1)}, bf16[448,768]{1,0:T(8,128)(2,1)S(1)}, u32[]{:S(2)}, u32[]{:S(2)}) collective-permute-start(bf16[448,768]{1,0:T(8,128)(2,1)S(1)} %get-tuple-element.167), channel_id=1, source_target_pairs={{0,96},{1,13},{2,98},{3,15},{4,100},{5,1},{6,102},{7,3},{8,104},{9... | collective-permute-start | bytes 2064392 | tf_op jit(solution)/shard_map/ppermute | solution.py:83
  220.4 19.8 %collective-permute-start.34 = (bf16[448,768]{1,0:T(8,128)(2,1)S(1)}, bf16[448,768]{1,0:T(8,128)(2,1)S(1)}, u32[]{:S(2)}, u32[]{:S(2)}) collective-permute-start(bf16[448,768]{1,0:T(8,128)(2,1)S(1)} %get-tuple-element.166.refs_3_), channel_id=1, source_target_pairs={{0,32},{1,5},{2,34},{3,7},{4,36},{5,9},{6,38},{7,11},{8,40},{9,13}... | collective-permute-start | bytes 2064392 | tf_op jit(solution)/shard_map/ppermute | solution.py:83
  220.6 17.5 %collective-permute-start.36 = (bf16[2,48,3072]{2,1,0:T(8,128)(2,1)S(1)}, bf16[2,48,3072]{2,1,0:T(8,128)(2,1)S(1)}, u32[]{:S(2)}, u32[]{:S(2)}) collective-permute-start(bf16[2,48,3072]{2,1,0:T(8,128)(2,1)S(1)} %get-tuple-element.164.refs_8_), channel_id=1, source_target_pairs={{0,12},{1,97},{2,14},{3,99},{4,8},{5,101},{6,10},{7,103},{8,4},{9,... | collective-permute-start | bytes 1769480 | tf_op jit(solution)/shard_map/ppermute | solution.py:83
  244.7 29.3 %collective-permute-start.37 = (bf16[448,1536]{1,0:T(8,128)(2,1)S(1)}, bf16[448,1536]{1,0:T(8,128)(2,1)S(1)}, u32[]{:S(2)}, u32[]{:S(2)}) collective-permute-start(bf16[448,1536]{1,0:T(8,128)(2,1)S(1)} %get-tuple-element.171), channel_id=1, source_target_pairs={{0,32},{1,5},{2,34},{3,7},{4,36},{5,9},{6,38},{7,11},{8,40},{9,13}... | collective-permute-start | bytes 4128776 | tf_op jit(solution)/shard_map/ppermute | solution.py:83
  245.2 28.8 %collective-permute-start.38 = (bf16[448,1536]{1,0:T(8,128)(2,1)S(1)}, bf16[448,1536]{1,0:T(8,128)(2,1)S(1)}, u32[]{:S(2)}, u32[]{:S(2)}) collective-permute-start(bf16[448,1536]{1,0:T(8,128)(2,1)S(1)} %get-tuple-element.172), channel_id=1, source_target_pairs={{0,96},{1,13},{2,98},{3,15},{4,100},{5,1},{6,102},{7,3},{8,104},{9... | collective-permute-start | bytes 4128776 | tf_op jit(solution)/shard_map/ppermute | solution.py:83
  254.2 15.5 %collective-permute-start.41 = (bf16[768,512]{1,0:T(8,128)(2,1)S(1)}, bf16[768,512]{1,0:T(8,128)(2,1)S(1)}, u32[]{:S(2)}, u32[]{:S(2)}) collective-permute-start(bf16[768,512]{1,0:T(8,128)(2,1)S(1)} %get-tuple-element.176), channel_id=1, source_target_pairs={{0,4},{1,33},{2,6},{3,35},{4,0},{5,37},{6,2},{7,39},{8,12},{9,41},... | collective-permute-start | bytes 2359304 | tf_op jit(solution)/shard_map/ppermute | solution.py:83
  272.0 15.1 %collective-permute-start.46 = (bf16[768,256]{1,0:T(8,128)(2,1)S(1)}, bf16[768,256]{1,0:T(8,128)(2,1)S(1)}, u32[]{:S(2)}, u32[]{:S(2)}) collective-permute-start(bf16[768,256]{1,0:T(8,128)(2,1)S(1)} %get-tuple-element.190), channel_id=1, source_target_pairs={{0,12},{1,97},{2,14},{3,99},{4,8},{5,101},{6,10},{7,103},{8,4},{9,... | collective-permute-start | bytes 1179656 | tf_op jit(solution)/shard_map/ppermute | solution.py:83
  279.7 19.8 %collective-permute-start.42 = (bf16[160,1536]{1,0:T(8,128)(2,1)S(1)}, bf16[160,1536]{1,0:T(8,128)(2,1)S(1)}, u32[]{:S(2)}, u32[]{:S(2)}) collective-permute-start(bf16[160,1536]{1,0:T(8,128)(2,1)S(1)} %get-tuple-element.179), channel_id=1, source_target_pairs={{0,4},{1,33},{2,6},{3,35},{4,8},{5,37},{6,10},{7,39},{8,12},{9,41}... | collective-permute-start | bytes 1474568 | tf_op jit(solution)/shard_map/ppermute | solution.py:83
  280.8 18.6 %collective-permute-start.43 = (bf16[160,1536]{1,0:T(8,128)(2,1)S(1)}, bf16[160,1536]{1,0:T(8,128)(2,1)}, u32[]{:S(2)}, u32[]{:S(2)}) collective-permute-start(bf16[160,1536]{1,0:T(8,128)(2,1)S(1)} %get-tuple-element.180), channel_id=1, source_target_pairs={{0,8},{1,65},{2,10},{3,67},{4,12},{5,69},{6,14},{7,71},{8,0},{9,73... | collective-permute-start | bytes 1474568 | tf_op jit(solution)/shard_map/ppermute | solution.py:83
  282.5 17.0 %collective-permute-start.44 = (bf16[160,1536]{1,0:T(8,128)(2,1)S(1)}, bf16[160,1536]{1,0:T(8,128)(2,1)}, u32[]{:S(2)}, u32[]{:S(2)}) collective-permute-start(bf16[160,1536]{1,0:T(8,128)(2,1)S(1)} %get-tuple-element.181), channel_id=1, source_target_pairs={{0,12},{1,97},{2,14},{3,99},{4,0},{5,101},{6,2},{7,103},{8,4},{9,1... | collective-permute-start | bytes 1474568 | tf_op jit(solution)/shard_map/ppermute | solution.py:83
  283.5 10.7 %collective-permute-start.48 = (bf16[48,3072]{1,0:T(8,128)(2,1)S(1)}, bf16[48,3072]{1,0:T(8,128)(2,1)S(1)}, u32[]{:S(2)}, u32[]{:S(2)}) collective-permute-start(bf16[48,3072]{1,0:T(8,128)(2,1)S(1)} %get-tuple-element.197), channel_id=1, source_target_pairs={{0,16},{1,17},{2,18},{3,19},{4,20},{5,21},{6,22},{7,23},{8,24},{9,... | collective-permute-start | bytes 884744 | tf_op jit(solution)/shard_map/ppermute | solution.py:83
  (129 other events, 830.4 us)

commit v2 on v1

--- a/solution.py
+++ b/solution.py
@@ -16,7 +16,7 @@
 LANES = 2 * HEAD
 SHUT = 256.0
 ROOT = HEAD ** (-0.5)
-VMEM_LIMIT = 24 * 2**20
+VMEM_LIMIT = 16 * 2**20
 NO_COST = pl.CostEstimate(flops=0, bytes_accessed=0, transcendentals=0)
 
 
@@ -31,7 +31,7 @@
 FFN_NEXT_MICROS = 8
 MIDDLE_MICROS = 10
 SELF_MICROS = 0
-ATTN_MICROS = 3
+ATTN_MICROS = 1
 TEXT_MICROS = 8
 ATTN_FIRST_MICROS = 0
 
@@ -1237,26 +1237,9 @@
     ]
     (halves_two,) = row_chunks(attn_pairs, (2,), spot, riders=(riders,), micros=ATTN_FIRST_MICROS)
     attn_passed = one_on(halves_two)
-    kept, sent = tiled_call(
-        ffn_third_kernel,
-        (spot,),
-        [ffn_own, dp_permute(ffn_sent, "second", "mirror")],
-        [(shape[1:], b16)] * 2,
-        "ffn_third",
-        -1,
-        2,
-        (halves_two[0],),
-    )
-    gate_sum_out, up_sum_out, down_sum_out = whole_call(
-        ffn_last_kernel,
-        (),
-        exchange([kept, sent], "z"),
-        [((block_rows, hidden_cols), f32)] * 2 + [((hidden_cols, block_rows), f32)],
-        "ffn_last",
-    )
     text_rows = caption_flat.shape[1] // BLOCKS
     attn_one, attn_three, attn_kept = row_chunks(
-        attn_pairs, (1, 3, 0), spot, extra=attn_passed, ties=(kept,), riders=(riders,), micros=ATTN_MICROS
+        attn_pairs, (1, 3, 0), spot, extra=attn_passed, riders=(riders,), micros=ATTN_MICROS
     )
     text_own, text_sent = tiled_call(
         text_second_kernel,
@@ -1268,6 +1251,26 @@
         4,
         (attn_kept,),
     )
+    stage = tiled_call(
+        functools.partial(attn_second_kernel, block_rows),
+        (spot,),
+        [riders] + to_neighbours(attn_kept, attn_one, attn_three),
+        [((PAIR * block_rows + rider_rows(4 * PAIR), width), b16)] * RING,
+        "attn_second",
+        -1,
+        4,
+        (text_sent,),
+    )
+    ffn_own_kept, ffn_own_sent = tiled_call(
+        ffn_third_kernel,
+        (spot,),
+        [ffn_own, dp_permute(ffn_sent, "second", "mirror")],
+        [(shape[1:], b16)] * 2,
+        "ffn_third",
+        -1,
+        2,
+        (stage[0],),
+    )
     text_own, text_sent = tiled_call(
         text_middle_kernel,
         (),
@@ -1276,8 +1279,23 @@
         "text_middle",
         0,
         2,
-    )
+        (stage[0],),
+    )
+    got = exchange(stage, "second")
     kept, sent = tiled_call(
+        attn_third_kernel, (spot,), got, [((block_rows, width), b16)] * 2, "attn_third",
+        -1,
+        2
+    )
+    gate_sum_out, up_sum_out, down_sum_out = whole_call(
+        ffn_last_kernel,
+        (),
+        exchange([ffn_own_kept, ffn_own_sent], "z"),
+        [((block_rows, hidden_cols), f32)] * 2 + [((hidden_cols, block_rows), f32)],
+        "ffn_last",
+        (kept,),
+    )
+    text_own_kept, text_own_sent = tiled_call(
         text_third_kernel,
         (spot,),
         [text_own, dp_permute(text_sent, "second", "mirror")],
@@ -1285,29 +1303,14 @@
         "text_third",
         0,
         2,
+        (kept,),
     )
     textkey_sum, textvalue_sum = whole_call(
         text_last_kernel,
         (),
-        exchange([kept, sent], "z"),
+        exchange([text_own_kept, text_own_sent], "z"),
         [((text_rows, inner), f32)] * 2,
         "text_last",
-    )
-    stage = tiled_call(
-        functools.partial(attn_second_kernel, block_rows),
-        (spot,),
-        [riders] + to_neighbours(attn_kept, attn_one, attn_three),
-        [((PAIR * block_rows + rider_rows(4 * PAIR), width), b16)] * RING,
-        "attn_second",
-        -1,
-        4,
-        (text_own,),
-    )
-    got = exchange(stage, "second")
-    kept, sent = tiled_call(
-        attn_third_kernel, (spot,), got, [((block_rows, width), b16)] * 2, "attn_third",
-        -1,
-        2
     )
     ada_grad, norm_grads, head_grads, crossgate = tiled_call(
         functools.partial(ada_kernel, 4 * PAIR, heads),

time: 317 us -> 314 us (level)
  waiting for transfers between devices: 107 us -> 95.4 us
    ppermute x23, waiting for transfers between devices: 49.6 us -> 37.9 us  [dp_permute(): return lax.ppermute(values, ('dp', 'tensor'), dp_perm(axis, step))]
    unnamed x235 -> x241, local copies, waits for them, and re-layouts: 24.4 us -> 27 us
  transfers between devices with their start and end apart: 49 -> 49, of which waited for: 21 -> 23; matrix products, arithmetic and copies ran while one was open for 2% -> 3% of each run, Pallas kernels for 24% -> 25%
where the time goes in v2:
time: 314 us; the launch traced here: 309 us
  Pallas kernels  105 us (33%)
  waiting for transfers between devices  95.4 us (30%)
  starting transfers between devices  59.3 us (19%)
  local copies, waits for them, and re-layouts  27.6 us (9%)
  matrix products  17.7 us (6%)
    ppermute x10, waiting for transfers between devices, swap_chip(): return lax.ppermute(values, 'tensor', CHIP_SWAP)  50.4 us
    ppermute x23, starting transfers between devices, dp_permute(): return lax.ppermute(values, ('dp', 'tensor'), dp_perm(axis, step))  41.8 us
    ppermute x23, waiting for transfers between devices, dp_permute(): return lax.ppermute(values, ('dp', 'tensor'), dp_perm(axis, step))  37.9 us
    unnamed x241, local copies, waits for them, and re-layouts  27 us
    pallas_call x3, Pallas kernels, pair_call(): pl.pallas_call(lambda *refs: kernel(*refs[:len(operands)], *refs[len(oper...  26 us
    pallas_call x6, Pallas kernels, chunk_call(): pl.pallas_call(kernel, grid_spec=pltpu.PrefetchScalarGridSpec(num_scalar_...  23 us
    pallas_call x9, Pallas kernels, tiled_call(): pl.pallas_call(lambda *refs: kernel(*refs[:count], *refs[count + len(ties...  22.7 us
    pallas_call x12, Pallas kernels, whole_call(): pl.pallas_call(lambda *refs: kernel(*refs[:count], *refs[count + len(ties...  17.5 us
  transfers between devices with their start and end apart: 49, of which 23 were waited for; matrix products, arithmetic and copies ran while one was open for 3% of the time, Pallas kernels for 25%

profile of v2, /device:TPU:0, one launch (start us, length us, event | category | flops | bytes accessed | tf_op | source)
XLA Modules:
  0.0 308.6 jit_solution(7384490673132755740)
XLA Ops:
  0.7 3.2 %fusion.16 = f32[3,1536]{1,0:T(4,128)} fusion(bf16[1024,1536]{1,0:T(8,128)(2,1)} %param.25, bf16[3,1024]{1,0:T(4,128)(2,1)} %param.21), kind=kOutput, calls=%fused_computation.46 | convolution fusion | flops 9455616 | bytes 3170304 | tf_op jit(solution)/shard_map/dot_general | solution.py:1046
  6.4 9.3 %text.1 = (f32[768,384]{1,0:T(8,128)S(1)}, bf16[768,384]{1,0:T(8,128)(2,1)S(1)}) custom-call(bf16[768,4096]{1,0:T(8,128)(2,1)} %bitcast.38, bf16[4096,384]{1,0:T(8,128)(2,1)} %key_weight.1, bf16[4096,384]{1,0:T(8,128)(2,1)} %value_weight.1), custom_call_target="tpu_custom_call" | custom-call | flops 8999999488 | tf_op jit(solution)/shard_map/text/pallas_call | solution.py:778
  23.9 4.9 %project.1 = (bf16[512,1536]{1,0:T(8,128)(2,1)S(1)}, f32[512,384]{1,0:T(8,128)S(1)}, f32[512,384]{1,0:T(8,128)S(1)}, bf16[512,384]{1,0:T(8,128)(2,1)S(1)}) custom-call(s32[1]{0:T(128)} %bitcast.refs_0_, bf16[128,1536]{1,0:T(8,128)(2,1)S(1)} %copy-done.25, bf16[128,1536]{1,0:T(8,128)(2,1)} %collective-permute-done.refs_2_, ...), custom_call_target="tpu_custom_call" | custom-call | flops 6000000000 | tf_op jit(solution)/shard_map/project/pallas_call | solution.py:460
  30.0 9.9 %attend.1 = (bf16[512,384]{1,0:T(8,128)(2,1)S(1)}, bf16[512,384]{1,0:T(8,128)(2,1)S(1)}, bf16[768,384]{1,0:T(8,128)(2,1)S(1)}, bf16[512,384]{1,0:T(8,128)(2,1)S(...) custom-call(f32[512,384]{1,0:T(8,128)S(1)} %get-tuple-element.109.refs_0_, ...), custom_call_target="tpu_custom_call" | custom-call | flops 11000000512 | tf_op jit(solution)/shard_map/attend/pallas_call | solution.py:670
  45.9 9.4 %collective-permute-done.7.refs_4_ = bf16[128,1536]{1,0:T(8,128)(2,1)S(1)} collective-permute-done((bf16[128,1536]{1,0:T(8,128)(2,1)S(1)}, bf16[128,1536]{1,0:T(8,128)(2,1)S(1)}, u32[]{:S(2)}, u32[]{:S(2)}) %collective-permute-start.7) | collective-permute-done | bytes 393248 | tf_op jit(solution)/shard_map/ppermute | solution.py:98
  58.0 8.8 %collective-permute-done.8 = bf16[128,1536]{1,0:T(8,128)(2,1)S(1)} collective-permute-done((bf16[128,1536]{1,0:T(8,128)(2,1)S(1)}, bf16[128,1536]{1,0:T(8,128)(2,1)S(1)}, u32[]{:S(2)}, u32[]{:S(2)}) %collective-permute-start.8) | collective-permute-done | bytes 393248 | tf_op jit(solution)/shard_map/ppermute | solution.py:98
  79.2 9.0 %collective-permute-done.12.refs_4_ = bf16[128,1536]{1,0:T(8,128)(2,1)S(1)} collective-permute-done((bf16[128,1536]{1,0:T(8,128)(2,1)S(1)}, bf16[128,1536]{1,0:T(8,128)(2,1)S(1)}, u32[]{:S(2)}, u32[]{:S(2)}) %collective-permute-start.12) | collective-permute-done | bytes 393248 | tf_op jit(solution)/shard_map/ppermute | solution.py:98
  91.2 8.8 %collective-permute-done.13 = bf16[128,1536]{1,0:T(8,128)(2,1)S(1)} collective-permute-done((bf16[128,1536]{1,0:T(8,128)(2,1)S(1)}, bf16[128,1536]{1,0:T(8,128)(2,1)S(1)}, u32[]{:S(2)}, u32[]{:S(2)}) %collective-permute-start.13) | collective-permute-done | bytes 393248 | tf_op jit(solution)/shard_map/ppermute | solution.py:98
  101.8 2.4 multiply_convert_fusion
  113.6 7.7 %collective-permute-done.17.refs_5_ = bf16[128,1536]{1,0:T(8,128)(2,1)} collective-permute-done((bf16[128,1536]{1,0:T(8,128)(2,1)S(1)}, bf16[128,1536]{1,0:T(8,128)(2,1)}, u32[]{:S(2)}, u32[]{:S(2)}) %collective-permute-start.17) | collective-permute-done | bytes 393248 | tf_op jit(solution)/shard_map/ppermute | solution.py:98
  121.3 2.5 middle_back.1
  130.8 3.6 %collective-permute-done.18 = bf16[128,1536]{1,0:T(8,128)(2,1)S(1)} collective-permute-done((bf16[128,1536]{1,0:T(8,128)(2,1)S(1)}, bf16[128,1536]{1,0:T(8,128)(2,1)S(1)}, u32[]{:S(2)}, u32[]{:S(2)}) %collective-permute-start.18) | collective-permute-done | bytes 393248 | tf_op jit(solution)/shard_map/ppermute | solution.py:98
  138.4 8.3 %cross_back.1 = (f32[512,384]{1,0:T(8,128)S(1)}, bf16[384,768]{1,0:T(8,128)(2,1)S(1)}, bf16[384,768]{1,0:T(8,128)(2,1)S(1)}, f32[1,384]{1,0:T(1,128)S(1)}, f32[1,384]{1,0:T(1,128)S(1)}) custom-call(bf16[512,384]{1,0:T(8,128)(2,1)S(1)} %copy-done.54, bf16[768,384]{1,0:T(8,128)(2,1)S(1)} %copy-done.94, bf16[768,384]{1,0:T(8,128)(2,1)S(1)} %copy-done.88, ...), custom_call_target="tpu_custom_call" | custom-call | flops 10000000000 | tf_op jit(solution)/shard_map/cross_back/pallas_call | solution.py:670
  146.7 5.5 %row_chunks.5 = (bf16[384,3072]{1,0:T(8,128)(2,1)S(1)}, bf16[384,3072]{1,0:T(8,128)(2,1)S(1)}, bf16[384,3072]{1,0:T(8,128)(2,1)S(1)}) custom-call(s32[4]{0:T(128)S(1)} %pad_add_fusion.spot_ref.refs_0_, bf16[32,48,512]{2,1,0:T(8,128)(2,1)S(1)} %bitcast.65, bf16[32,48,512]{2,1,0:T(8,128)(2,1)S(1)} %bitcast.66, bf16[32,48,512]{2,1,0:T(8,128)(2,1)S(1)} %bitcast.67, ...), custom_call_target="tpu_custom_call" | custom-call | flops 8000000000 | tf_op jit(solution)/shard_map/row_chunks/pallas_call | solution.py:202
  158.3 7.9 %self_back.1 = (bf16[512,384]{1,0:T(8,128)(2,1)S(1)}, bf16[512,384]{1,0:T(8,128)(2,1)S(1)}, bf16[512,384]{1,0:T(8,128)(2,1)S(1)}, f32[2,384]{1,0:T(2,128)S(1)}) custom-call(bf16[512,384]{1,0:T(8,128)(2,1)S(1)} %copy-done.54, bf16[512,384]{1,0:T(8,128)(2,1)S(1)} %copy-done.56, bf16[512,384]{1,0:T(8,128)(2,1)S(1)} %copy-done.52, f32[512,384]{1,0:T(8,128)S(1)} %copy-done.36, ...), custom_call_target="tpu_custom_call" | custom-call | tf_op jit(solution)/shard_map/self_back/pallas_call | solution.py:670
  166.2 3.1 %attn_back.1 = (bf16[256,1536]{1,0:T(8,128)(2,1)S(1)}, bf16[256,1536]{1,0:T(8,128)(2,1)S(1)}) custom-call(bf16[512,384]{1,0:T(8,128)(2,1)S(1)} %get-tuple-element.145.refs_0_.refs_4_.refs_16_, bf16[512,384]{1,0:T(8,128)(2,1)S(1)} %get-tuple-element.146.refs_1_.refs_17_, bf16[512,384]{1,0:T(8,128)(2,1)S(1)} %get-tuple-element.147.refs_2_.refs_18_, ...), custom_call_target="tpu_custom_call" | custom-call | tf_op jit(solution)/shard_map/attn_back/pallas_call | solution.py:998
  174.3 8.0 %collective-permute-done.25 = bf16[384,3072]{1,0:T(8,128)(2,1)S(1)} collective-permute-done((bf16[384,3072]{1,0:T(8,128)(2,1)S(1)}, bf16[384,3072]{1,0:T(8,128)(2,1)S(1)}, u32[]{:S(2)}, u32[]{:S(2)}) %collective-permute-start.25) | collective-permute-done | bytes 2359328 | tf_op jit(solution)/shard_map/ppermute | solution.py:83
  184.5 4.1 %ffn_second.1 = (bf16[4,48,3072]{2,1,0:T(8,128)(2,1)S(1)}, bf16[4,48,3072]{2,1,0:T(8,128)(2,1)S(1)}) custom-call(s32[4]{0:T(128)S(1)} %pad_add_fusion.spot_ref.refs_0_, bf16[8,48,3072]{2,1,0:T(8,128)(2,1)} %bitcast.121, bf16[8,48,3072]{2,1,0:T(8,128)(2,1)} %bitcast.123, bf16[8,48,3072]{2,1,0:T(8,128)(2,1)} %bitcast.124, ...), custom_call_target="tpu_custom_call" | custom-call | tf_op jit(solution)/shard_map/ffn_second/pallas_call | solution.py:483
  194.5 3.1 collective-permute-done.27.refs_2_
  197.5 7.0 %column_chunks.3 = (bf16[768,1024]{1,0:T(8,128)(2,1)S(1)}, bf16[768,1024]{1,0:T(8,128)(2,1)S(1)}, bf16[768,1024]{1,0:T(8,128)(2,1)S(1)}) custom-call(s32[4]{0:T(128)S(1)} %pad_add_fusion.spot_ref.refs_0_, bf16[384,768]{1,0:T(8,128)(2,1)S(1)} %get-tuple-element.139.refs_21_.refs_0_, bf16[384,768]{1,0:T(8,128)(2,1)S(1)} %get-tuple-element.140.refs_1_, ...), custom_call_target="tpu_custom_call" | custom-call | flops 8000000000 | tf_op jit(solution)/shard_map/column_chunks/pallas_call | solution.py:202
  211.3 3.7 %collective-permute-start.33 = (bf16[32,1536]{1,0:T(8,128)(2,1)S(1)}, bf16[32,1536]{1,0:T(8,128)(2,1)S(1)}, u32[]{:S(2)}, u32[]{:S(2)}) collective-permute-start(bf16[32,1536]{1,0:T(8,128)(2,1)S(1)} %pack.1.refs_0_), channel_id=1, source_target_pairs={{0,16},{1,17},{2,18},{3,19},{4,20},{5,21},{6,22},{7,23},{8,24},{9,... | collective-permute-start | bytes 294920 | tf_op jit(solution)/shard_map/ppermute | solution.py:83
  220.2 2.8 collective-permute-start.35
  223.0 10.9 %collective-permute-done.34.refs_21_ = bf16[448,768]{1,0:T(8,128)(2,1)S(1)} collective-permute-done((bf16[448,768]{1,0:T(8,128)(2,1)S(1)}, bf16[448,768]{1,0:T(8,128)(2,1)S(1)}, u32[]{:S(2)}, u32[]{:S(2)}) %collective-permute-start.34) | collective-permute-done | bytes 688160 | tf_op jit(solution)/shard_map/ppermute | solution.py:83
  234.0 4.4 %row_chunks.7 = (bf16[448,1536]{1,0:T(8,128)(2,1)S(1)}, bf16[448,1536]{1,0:T(8,128)(2,1)S(1)}, bf16[448,1536]{1,0:T(8,128)(2,1)S(1)}) custom-call(s32[4]{0:T(128)S(1)} %pad_add_fusion.spot_ref.refs_0_, bf16[32,48,512]{2,1,0:T(8,128)(2,1)S(1)} %bitcast.97, bf16[32,48,512]{2,1,0:T(8,128)(2,1)S(1)} %bitcast.98, bf16[32,48,512]{2,1,0:T(8,128)(2,1)S(1)} %bitcast.99, ...), custom_call_target="tpu_custom_call" | custom-call | flops 1000000000 | tf_op jit(solution)/shard_map/row_chunks/pallas_call | solution.py:202
  243.4 3.6 %text_second.1 = (bf16[768,512]{1,0:T(8,128)(2,1)S(1)}, bf16[768,512]{1,0:T(8,128)(2,1)S(1)}) custom-call(s32[4]{0:T(128)S(1)} %pad_add_fusion.spot_ref.refs_0_, bf16[768,1024]{1,0:T(8,128)(2,1)} %copy-done.8, bf16[768,1024]{1,0:T(8,128)(2,1)} %copy-done.104, bf16[768,1024]{1,0:T(8,128)(2,1)} %copy-done.105, ...), custom_call_target="tpu_custom_call" | custom-call | tf_op jit(solution)/shard_map/text_second/pallas_call | solution.py:483
  248.4 2.9 collective-permute-start.47
  251.4 12.9 %collective-permute-done.36.refs_3_ = bf16[448,1536]{1,0:T(8,128)(2,1)S(1)} collective-permute-done((bf16[448,1536]{1,0:T(8,128)(2,1)S(1)}, bf16[448,1536]{1,0:T(8,128)(2,1)S(1)}, u32[]{:S(2)}, u32[]{:S(2)}) %collective-permute-start.36) | collective-permute-done | bytes 1376288 | tf_op jit(solution)/shard_map/ppermute | solution.py:83
  267.5 3.3 %attn_second.1 = (bf16[160,1536]{1,0:T(8,128)(2,1)S(1)}, bf16[160,1536]{1,0:T(8,128)(2,1)S(1)}, bf16[160,1536]{1,0:T(8,128)(2,1)S(1)}, bf16[160,1536]{1,0:T(8,128)(2,1)S(1)}) custom-call(s32[4]{0:T(128)S(1)} %pad_add_fusion.spot_ref.refs_0_, bf16[32,1536]{1,0:T(8,128)(2,1)} %copy-done.18, bf16[448,1536]{1,0:T(8,128)(2,1)} %copy-done.9, ...), custom_call_target="tpu_custom_call" | custom-call | tf_op jit(solution)/shard_map/attn_second/pallas_call | solution.py:483
  271.4 3.2 %collective-permute-start.41 = (bf16[160,1536]{1,0:T(8,128)(2,1)S(1)}, bf16[160,1536]{1,0:T(8,128)(2,1)S(1)}, u32[]{:S(2)}, u32[]{:S(2)}) collective-permute-start(bf16[160,1536]{1,0:T(8,128)(2,1)S(1)} %get-tuple-element.176), channel_id=1, source_target_pairs={{0,8},{1,65},{2,10},{3,67},{4,12},{5,69},{6,14},{7,71},{8,0},{9,73... | collective-permute-start | bytes 1474568 | tf_op jit(solution)/shard_map/ppermute | solution.py:83
  281.8 3.7 %collective-permute-start.48 = (bf16[48,3072]{1,0:T(8,128)(2,1)S(1)}, bf16[48,3072]{1,0:T(8,128)(2,1)S(1)}, u32[]{:S(2)}, u32[]{:S(2)}) collective-permute-start(bf16[48,3072]{1,0:T(8,128)(2,1)S(1)} %get-tuple-element.197), channel_id=1, source_target_pairs={{0,16},{1,17},{2,18},{3,19},{4,20},{5,21},{6,22},{7,23},{8,24},{9,... | collective-permute-start | bytes 884744 | tf_op jit(solution)/shard_map/ppermute | solution.py:83
  290.7 3.6 %collective-permute-start.43 = (bf16[48,1536]{1,0:T(8,128)(2,1)}, bf16[48,1536]{1,0:T(8,128)(2,1)}, u32[]{:S(2)}, u32[]{:S(2)}) collective-permute-start(bf16[48,1536]{1,0:T(8,128)(2,1)} %get-tuple-element.181), channel_id=1, source_target_pairs={{0,16},{1,17},{2,18},{3,19},{4,20},{5,21},{6,22},{7,23},{8,24},{9,... | collective-permute-start | bytes 442376 | tf_op jit(solution)/shard_map/ppermute | solution.py:83
  298.9 2.5 ada.1
  (368 shorter events, 122.0 us)
Async XLA Ops:
  3.9 13.7 %collective-permute-start.4 = (f32[3,1536]{1,0:T(4,128)}, f32[3,1536]{1,0:T(4,128)}, u32[]{:S(2)}, u32[]{:S(2)}) collective-permute-start(f32[3,1536]{1,0:T(4,128)} %fusion.16), channel_id=1, source_target_pairs={{0,2},{2,0},{1,3},{3,1},{4,6},{6,4},{5,7},{7,5},{8,10},{10,8},{9,1... | collective-permute-start | bytes 55304 | tf_op jit(solution)/shard_map/ppermute | solution.py:98
  5.9 17.0 %collective-permute-start.3 = (f32[3,1536]{1,0:T(4,128)}, f32[3,1536]{1,0:T(4,128)}, u32[]{:S(2)}, u32[]{:S(2)}) collective-permute-start(f32[3,1536]{1,0:T(4,128)} %fusion.16), channel_id=1, source_target_pairs={{0,1},{1,0},{2,3},{3,2},{4,5},{5,4},{6,7},{7,6},{8,9},{9,8},{10,11... | collective-permute-start | bytes 55304 | tf_op jit(solution)/shard_map/ppermute | solution.py:94
  5.9 17.9 %collective-permute-start.1 = (bf16[128,1536]{1,0:T(8,128)(2,1)S(1)}, bf16[128,1536]{1,0:T(8,128)(2,1)}, u32[]{:S(2)}, u32[]{:S(2)}) collective-permute-start(bf16[128,1536]{1,0:T(8,128)(2,1)S(1)} %copy-done.25), channel_id=1, source_target_pairs={{0,1},{1,0},{2,3},{3,2},{4,5},{5,4},{6,7},{7,6},{8,9},{9,8},{10,11... | collective-permute-start | bytes 1179656 | tf_op jit(solution)/shard_map/ppermute | solution.py:94
  6.4 11.2 %collective-permute-start = (bf16[128,1536]{1,0:T(8,128)(2,1)S(1)}, bf16[128,1536]{1,0:T(8,128)(2,1)}, u32[]{:S(2)}, u32[]{:S(2)}) collective-permute-start(bf16[128,1536]{1,0:T(8,128)(2,1)S(1)} %copy-done.25), channel_id=1, source_target_pairs={{0,2},{2,0},{1,3},{3,1},{4,6},{6,4},{5,7},{7,5},{8,10},{10,8},{9,1... | collective-permute-start | bytes 1179656 | tf_op jit(solution)/shard_map/ppermute | solution.py:98
  43.8 11.5 %collective-permute-start.7 = (bf16[128,1536]{1,0:T(8,128)(2,1)S(1)}, bf16[128,1536]{1,0:T(8,128)(2,1)S(1)}, u32[]{:S(2)}, u32[]{:S(2)}) collective-permute-start(bf16[128,1536]{1,0:T(8,128)(2,1)S(1)} %add_convert_fusion.3.rest_0_), channel_id=1, source_target_pairs={{0,2},{2,0},{1,3},{3,1},{4,6},{6,4},{5,7},{7,5},{8,10},{10,8},{9,1... | collective-permute-start | bytes 1179656 | tf_op jit(solution)/shard_map/ppermute | solution.py:98
  56.1 10.7 %collective-permute-start.8 = (bf16[128,1536]{1,0:T(8,128)(2,1)S(1)}, bf16[128,1536]{1,0:T(8,128)(2,1)S(1)}, u32[]{:S(2)}, u32[]{:S(2)}) collective-permute-start(bf16[128,1536]{1,0:T(8,128)(2,1)S(1)} %get-tuple-element.124), channel_id=1, source_target_pairs={{0,2},{2,0},{1,3},{3,1},{4,6},{6,4},{5,7},{7,5},{8,10},{10,8},{9,1... | collective-permute-start | bytes 1179656 | tf_op jit(solution)/shard_map/ppermute | solution.py:98
  76.9 11.2 %collective-permute-start.12 = (bf16[128,1536]{1,0:T(8,128)(2,1)S(1)}, bf16[128,1536]{1,0:T(8,128)(2,1)S(1)}, u32[]{:S(2)}, u32[]{:S(2)}) collective-permute-start(bf16[128,1536]{1,0:T(8,128)(2,1)S(1)} %add_convert_fusion.2.rest_0_), channel_id=1, source_target_pairs={{0,2},{2,0},{1,3},{3,1},{4,6},{6,4},{5,7},{7,5},{8,10},{10,8},{9,1... | collective-permute-start | bytes 1179656 | tf_op jit(solution)/shard_map/ppermute | solution.py:98
  109.7 11.6 %collective-permute-start.17 = (bf16[128,1536]{1,0:T(8,128)(2,1)S(1)}, bf16[128,1536]{1,0:T(8,128)(2,1)}, u32[]{:S(2)}, u32[]{:S(2)}) collective-permute-start(bf16[128,1536]{1,0:T(8,128)(2,1)S(1)} %add_convert_fusion.1.rest_0_.refs_19_), channel_id=1, source_target_pairs={{0,2},{2,0},{1,3},{3,1},{4,6},{6,4},{5,7},{7,5},{8,10},{10,8},{9,1... | collective-permute-start | bytes 1179656 | tf_op jit(solution)/shard_map/ppermute | solution.py:98
  127.5 19.1 %collective-permute-start.21 = (bf16[384,1536]{1,0:T(8,128)(2,1)S(1)}, bf16[384,1536]{1,0:T(8,128)(2,1)S(1)}, u32[]{:S(2)}, u32[]{:S(2)}) collective-permute-start(bf16[384,1536]{1,0:T(8,128)(2,1)S(1)} %get-tuple-element.141), channel_id=1, source_target_pairs={{0,32},{1,5},{2,34},{3,7},{4,36},{5,9},{6,38},{7,11},{8,40},{9,13}... | collective-permute-start | bytes 3538952 | tf_op jit(solution)/shard_map/ppermute | solution.py:83
  129.1 17.6 %collective-permute-start.22 = (bf16[384,1536]{1,0:T(8,128)(2,1)S(1)}, bf16[384,1536]{1,0:T(8,128)(2,1)S(1)}, u32[]{:S(2)}, u32[]{:S(2)}) collective-permute-start(bf16[384,1536]{1,0:T(8,128)(2,1)S(1)} %get-tuple-element.142), channel_id=1, source_target_pairs={{0,96},{1,13},{2,98},{3,15},{4,100},{5,1},{6,102},{7,3},{8,104},{9... | collective-permute-start | bytes 3538952 | tf_op jit(solution)/shard_map/ppermute | solution.py:83
  152.2 30.1 %collective-permute-start.25 = (bf16[384,3072]{1,0:T(8,128)(2,1)S(1)}, bf16[384,3072]{1,0:T(8,128)(2,1)S(1)}, u32[]{:S(2)}, u32[]{:S(2)}) collective-permute-start(bf16[384,3072]{1,0:T(8,128)(2,1)S(1)} %get-tuple-element.150), channel_id=1, source_target_pairs={{0,32},{1,5},{2,34},{3,7},{4,36},{5,9},{6,38},{7,11},{8,40},{9,13}... | collective-permute-start | bytes 7077896 | tf_op jit(solution)/shard_map/ppermute | solution.py:83
  153.7 29.0 %collective-permute-start.26 = (bf16[384,3072]{1,0:T(8,128)(2,1)S(1)}, bf16[384,3072]{1,0:T(8,128)(2,1)S(1)}, u32[]{:S(2)}, u32[]{:S(2)}) collective-permute-start(bf16[384,3072]{1,0:T(8,128)(2,1)S(1)} %get-tuple-element.151), channel_id=1, source_target_pairs={{0,96},{1,13},{2,98},{3,15},{4,100},{5,1},{6,102},{7,3},{8,104},{9... | collective-permute-start | bytes 7077896 | tf_op jit(solution)/shard_map/ppermute | solution.py:83
  169.4 28.1 %collective-permute-start.31 = (bf16[384,1024]{1,0:T(8,128)(2,1)S(1)}, bf16[384,1024]{1,0:T(8,128)(2,1)S(1)}, u32[]{:S(2)}, u32[]{:S(2)}) collective-permute-start(bf16[384,1024]{1,0:T(8,128)(2,1)S(1)} %get-tuple-element.144.refs_14_.rest_0_), channel_id=1, source_target_pairs={{0,32},{1,5},{2,34},{3,7},{4,36},{5,9},{6,38},{7,11},{8,40},{9,13}... | collective-permute-start | bytes 2359304 | tf_op jit(solution)/shard_map/ppermute | solution.py:83
  170.5 27.0 %collective-permute-start.32 = (bf16[384,1024]{1,0:T(8,128)(2,1)S(1)}, bf16[384,1024]{1,0:T(8,128)(2,1)S(1)}, u32[]{:S(2)}, u32[]{:S(2)}) collective-permute-start(bf16[384,1024]{1,0:T(8,128)(2,1)S(1)} %get-tuple-element.162), channel_id=1, source_target_pairs={{0,96},{1,13},{2,98},{3,15},{4,100},{5,1},{6,102},{7,3},{8,104},{9... | collective-permute-start | bytes 2359304 | tf_op jit(solution)/shard_map/ppermute | solution.py:83
  172.8 18.5 %collective-permute-start.24 = (bf16[128,1536]{1,0:T(8,128)(2,1)S(1)}, bf16[128,1536]{1,0:T(8,128)(2,1)S(1)}, u32[]{:S(2)}, u32[]{:S(2)}) collective-permute-start(bf16[128,1536]{1,0:T(8,128)(2,1)S(1)} %add_convert_fusion), channel_id=1, source_target_pairs={{0,2},{2,0},{1,3},{3,1},{4,6},{6,4},{5,7},{7,5},{8,10},{10,8},{9,1... | collective-permute-start | bytes 1179656 | tf_op jit(solution)/shard_map/ppermute | solution.py:98
  189.8 18.4 %collective-permute-start.30 = (bf16[4,48,3072]{2,1,0:T(8,128)(2,1)S(1)}, bf16[4,48,3072]{2,1,0:T(8,128)(2,1)S(1)}, u32[]{:S(2)}, u32[]{:S(2)}) collective-permute-start(bf16[4,48,3072]{2,1,0:T(8,128)(2,1)S(1)} %get-tuple-element.152.refs_10_), channel_id=1, source_target_pairs={{0,4},{1,33},{2,6},{3,35},{4,0},{5,37},{6,2},{7,39},{8,12},{9,41},... | collective-permute-start | bytes 3538952 | tf_op jit(solution)/shard_map/ppermute | solution.py:83
  194.5 16.7 %collective-permute-start.28 = (f32[16,1536]{1,0:T(8,128)S(1)}, f32[16,1536]{1,0:T(8,128)S(1)}, u32[]{:S(2)}, u32[]{:S(2)}) collective-permute-start(f32[16,1536]{1,0:T(8,128)S(1)} %stack_sums.1.refs_12_.refs_1_), channel_id=1, source_target_pairs={{0,1},{1,0},{2,3},{3,2},{4,5},{5,4},{6,7},{7,6},{8,9},{9,8},{10,11... | collective-permute-start | bytes 294920 | tf_op jit(solution)/shard_map/ppermute | solution.py:94
  197.5 13.6 %collective-permute-start.29 = (f32[16,1536]{1,0:T(8,128)S(1)}, f32[16,1536]{1,0:T(8,128)S(1)}, u32[]{:S(2)}, u32[]{:S(2)}) collective-permute-start(f32[16,1536]{1,0:T(8,128)S(1)} %collective-permute-done.27.refs_2_), channel_id=1, source_target_pairs={{0,1},{1,0},{2,3},{3,2},{4,5},{5,4},{6,7},{7,6},{8,9},{9,8},{10,11... | collective-permute-start | bytes 294920 | tf_op jit(solution)/shard_map/ppermute | solution.py:94
  204.6 37.1 %collective-permute-start.38 = (bf16[768,1024]{1,0:T(8,128)(2,1)S(1)}, bf16[768,1024]{1,0:T(8,128)(2,1)S(1)}, u32[]{:S(2)}, u32[]{:S(2)}) collective-permute-start(bf16[768,1024]{1,0:T(8,128)(2,1)S(1)} %get-tuple-element.171), channel_id=1, source_target_pairs={{0,32},{1,5},{2,34},{3,7},{4,36},{5,9},{6,38},{7,11},{8,40},{9,13}... | collective-permute-start | bytes 4718600 | tf_op jit(solution)/shard_map/ppermute | solution.py:83
  206.2 35.5 %collective-permute-start.39 = (bf16[768,1024]{1,0:T(8,128)(2,1)S(1)}, bf16[768,1024]{1,0:T(8,128)(2,1)S(1)}, u32[]{:S(2)}, u32[]{:S(2)}) collective-permute-start(bf16[768,1024]{1,0:T(8,128)(2,1)S(1)} %get-tuple-element.172), channel_id=1, source_target_pairs={{0,96},{1,13},{2,98},{3,15},{4,100},{5,1},{6,102},{7,3},{8,104},{9... | collective-permute-start | bytes 4718600 | tf_op jit(solution)/shard_map/ppermute | solution.py:83
  219.7 14.2 %collective-permute-start.34 = (bf16[448,768]{1,0:T(8,128)(2,1)S(1)}, bf16[448,768]{1,0:T(8,128)(2,1)S(1)}, u32[]{:S(2)}, u32[]{:S(2)}) collective-permute-start(bf16[448,768]{1,0:T(8,128)(2,1)S(1)} %get-tuple-element.166), channel_id=1, source_target_pairs={{0,32},{1,5},{2,34},{3,7},{4,36},{5,9},{6,38},{7,11},{8,40},{9,13}... | collective-permute-start | bytes 2064392 | tf_op jit(solution)/shard_map/ppermute | solution.py:83
  220.2 13.8 %collective-permute-start.35 = (bf16[448,768]{1,0:T(8,128)(2,1)S(1)}, bf16[448,768]{1,0:T(8,128)(2,1)S(1)}, u32[]{:S(2)}, u32[]{:S(2)}) collective-permute-start(bf16[448,768]{1,0:T(8,128)(2,1)S(1)} %get-tuple-element.167), channel_id=1, source_target_pairs={{0,96},{1,13},{2,98},{3,15},{4,100},{5,1},{6,102},{7,3},{8,104},{9... | collective-permute-start | bytes 2064392 | tf_op jit(solution)/shard_map/ppermute | solution.py:83
  238.4 25.9 %collective-permute-start.36 = (bf16[448,1536]{1,0:T(8,128)(2,1)S(1)}, bf16[448,1536]{1,0:T(8,128)(2,1)S(1)}, u32[]{:S(2)}, u32[]{:S(2)}) collective-permute-start(bf16[448,1536]{1,0:T(8,128)(2,1)S(1)} %get-tuple-element.169), channel_id=1, source_target_pairs={{0,32},{1,5},{2,34},{3,7},{4,36},{5,9},{6,38},{7,11},{8,40},{9,13}... | collective-permute-start | bytes 4128776 | tf_op jit(solution)/shard_map/ppermute | solution.py:83
  239.6 26.7 %collective-permute-start.37 = (bf16[448,1536]{1,0:T(8,128)(2,1)S(1)}, bf16[448,1536]{1,0:T(8,128)(2,1)S(1)}, u32[]{:S(2)}, u32[]{:S(2)}) collective-permute-start(bf16[448,1536]{1,0:T(8,128)(2,1)S(1)} %get-tuple-element.170), channel_id=1, source_target_pairs={{0,96},{1,13},{2,98},{3,15},{4,100},{5,1},{6,102},{7,3},{8,104},{9... | collective-permute-start | bytes 4128776 | tf_op jit(solution)/shard_map/ppermute | solution.py:83
  247.9 28.6 %collective-permute-start.44 = (bf16[768,512]{1,0:T(8,128)(2,1)S(1)}, bf16[768,512]{1,0:T(8,128)(2,1)S(1)}, u32[]{:S(2)}, u32[]{:S(2)}) collective-permute-start(bf16[768,512]{1,0:T(8,128)(2,1)S(1)} %get-tuple-element.173.refs_5_), channel_id=1, source_target_pairs={{0,4},{1,33},{2,6},{3,35},{4,0},{5,37},{6,2},{7,39},{8,12},{9,41},... | collective-permute-start | bytes 2359304 | tf_op jit(solution)/shard_map/ppermute | solution.py:83
  248.4 31.1 %collective-permute-start.47 = (bf16[2,48,3072]{2,1,0:T(8,128)(2,1)S(1)}, bf16[2,48,3072]{2,1,0:T(8,128)(2,1)S(1)}, u32[]{:S(2)}, u32[]{:S(2)}) collective-permute-start(bf16[2,48,3072]{2,1,0:T(8,128)(2,1)S(1)} %get-tuple-element.164.refs_8_), channel_id=1, source_target_pairs={{0,12},{1,97},{2,14},{3,99},{4,8},{5,101},{6,10},{7,103},{8,4},{9,... | collective-permute-start | bytes 1769480 | tf_op jit(solution)/shard_map/ppermute | solution.py:83
  270.9 14.6 %collective-permute-start.40 = (bf16[160,1536]{1,0:T(8,128)(2,1)S(1)}, bf16[160,1536]{1,0:T(8,128)(2,1)S(1)}, u32[]{:S(2)}, u32[]{:S(2)}) collective-permute-start(bf16[160,1536]{1,0:T(8,128)(2,1)S(1)} %get-tuple-element.175), channel_id=1, source_target_pairs={{0,4},{1,33},{2,6},{3,35},{4,8},{5,37},{6,10},{7,39},{8,12},{9,41}... | collective-permute-start | bytes 1474568 | tf_op jit(solution)/shard_map/ppermute | solution.py:83
  271.4 15.4 %collective-permute-start.41 = (bf16[160,1536]{1,0:T(8,128)(2,1)S(1)}, bf16[160,1536]{1,0:T(8,128)(2,1)S(1)}, u32[]{:S(2)}, u32[]{:S(2)}) collective-permute-start(bf16[160,1536]{1,0:T(8,128)(2,1)S(1)} %get-tuple-element.176), channel_id=1, source_target_pairs={{0,8},{1,65},{2,10},{3,67},{4,12},{5,69},{6,14},{7,71},{8,0},{9,73... | collective-permute-start | bytes 1474568 | tf_op jit(solution)/shard_map/ppermute | solution.py:83
  274.6 12.5 %collective-permute-start.42 = (bf16[160,1536]{1,0:T(8,128)(2,1)S(1)}, bf16[160,1536]{1,0:T(8,128)(2,1)S(1)}, u32[]{:S(2)}, u32[]{:S(2)}) collective-permute-start(bf16[160,1536]{1,0:T(8,128)(2,1)S(1)} %get-tuple-element.177), channel_id=1, source_target_pairs={{0,12},{1,97},{2,14},{3,99},{4,0},{5,101},{6,2},{7,103},{8,4},{9,1... | collective-permute-start | bytes 1474568 | tf_op jit(solution)/shard_map/ppermute | solution.py:83
  279.6 16.5 %collective-permute-start.45 = (bf16[768,256]{1,0:T(8,128)(2,1)S(1)}, bf16[768,256]{1,0:T(8,128)(2,1)S(1)}, u32[]{:S(2)}, u32[]{:S(2)}) collective-permute-start(bf16[768,256]{1,0:T(8,128)(2,1)S(1)} %get-tuple-element.188), channel_id=1, source_target_pairs={{0,12},{1,97},{2,14},{3,99},{4,8},{5,101},{6,10},{7,103},{8,4},{9,... | collective-permute-start | bytes 1179656 | tf_op jit(solution)/shard_map/ppermute | solution.py:83
  281.8 12.5 %collective-permute-start.48 = (bf16[48,3072]{1,0:T(8,128)(2,1)S(1)}, bf16[48,3072]{1,0:T(8,128)(2,1)S(1)}, u32[]{:S(2)}, u32[]{:S(2)}) collective-permute-start(bf16[48,3072]{1,0:T(8,128)(2,1)S(1)} %get-tuple-element.197), channel_id=1, source_target_pairs={{0,16},{1,17},{2,18},{3,19},{4,20},{5,21},{6,22},{7,23},{8,24},{9,... | collective-permute-start | bytes 884744 | tf_op jit(solution)/shard_map/ppermute | solution.py:83
  290.7 11.2 %collective-permute-start.43 = (bf16[48,1536]{1,0:T(8,128)(2,1)}, bf16[48,1536]{1,0:T(8,128)(2,1)}, u32[]{:S(2)}, u32[]{:S(2)}) collective-permute-start(bf16[48,1536]{1,0:T(8,128)(2,1)} %get-tuple-element.181), channel_id=1, source_target_pairs={{0,16},{1,17},{2,18},{3,19},{4,20},{5,21},{6,22},{7,23},{8,24},{9,... | collective-permute-start | bytes 442376 | tf_op jit(solution)/shard_map/ppermute | solution.py:83
  (132 other events, 830.9 us)

commit v3 on v2

--- a/solution.py
+++ b/solution.py
@@ -31,8 +31,10 @@
 FFN_NEXT_MICROS = 8
 MIDDLE_MICROS = 10
 SELF_MICROS = 0
-ATTN_MICROS = 1
+ATTN_MICROS = 3
 TEXT_MICROS = 8
+TEXT_AFTER = 1
+PACK_MICROS = 16
 ATTN_FIRST_MICROS = 0
 
 RING = 4
@@ -420,23 +422,14 @@
     textvalue[...] = total[columns:].T
 
 
-def attn_second_kernel(rows, spot, riders, *refs):
+def attn_second_kernel(spot, riders, *refs):
     parts, outs = refs[:-RING], refs[-RING:]
-    size, count = SLOTS * rows, riders.shape[0]
+    rows = parts[0].shape[1]
     for offset in range(RING):
         for z in range(PAIR):
             slot = z * RING + (spot[2] + offset) % RING
-            index = (pl.ds(pl.multiple_of(slot * rows, 16), rows), slice(None))
-            outs[offset][z * rows : (z + 1) * rows, :] = add_up(parts, index).astype(jnp.bfloat16)
-    ahead, behind = parts[1], parts[2]
-    pairs = (
-        (riders[...], ahead[size : size + count, :]),
-        (behind[size : size + count, :], ahead[size + count : size + 2 * count, :]),
-    )
-    joined = [merge_rows(PAIR, first, second, rider_rows(2 * PAIR)) for first, second in pairs]
-    joined = merge_rows(2 * PAIR, joined[0], joined[1], rider_rows(4 * PAIR))
-    for out in outs:
-        out[PAIR * rows :, :] = joined
+            outs[offset][z * rows : (z + 1) * rows, :] = add_up(parts, slot).astype(jnp.bfloat16)
+        outs[offset][PAIR * rows :, :] = riders[...]
 
 
 def attn_third_kernel(spot, *refs):
@@ -937,8 +930,8 @@
     return jnp.concatenate(pieces, axis=0).astype(jnp.bfloat16)
 
 
-def merge_kernel(ours, theirs, out):
-    out[...] = merge_rows(1, ours[...], theirs[...], out.shape[0])
+def merge_kernel(count, ours, theirs, out):
+    out[...] = merge_rows(count, ours[...], theirs[...], out.shape[0])
 
 
 def ada_kernel(count, heads, dp, own, *refs):
@@ -1204,11 +1197,19 @@
         [((16, width), f32)],
         "stack_sums",
     )
-    sums_stacked = stacked
+    attn_pairs = [
+        (attn_rows_t, [query_grad, key_grad, value_grad]),
+        (turned(grad_attn, (halves_two[0],)), [mixed]),
+    ]
+    (halves_two,) = row_chunks(attn_pairs, (2,), spot, ties=(stacked,), micros=ATTN_FIRST_MICROS)
+    attn_passed = one_on(halves_two)
+    stacked = gather_tensor(stacked)
     text_one, text_three, text_kept = column_chunks(
-        text_lefts, caption_flat, (1, 3, 0), spot, extra=text_passed, ties=(sums_stacked,), micros=TEXT_MICROS
-    )
-    stacked = gather_tensor(stacked)
+        text_lefts, caption_flat, (1, 3, 0), spot, extra=text_passed, ties=(halves_two[0],), micros=TEXT_MICROS
+    )
+    attn_one, attn_three, attn_kept = row_chunks(
+        attn_pairs, (1, 3, 0), spot, extra=attn_passed, ties=(text_kept,), micros=ATTN_MICROS
+    )
     ffn_own, ffn_sent = tiled_call(
         ffn_middle_kernel,
         (),
@@ -1217,7 +1218,7 @@
         "ffn_middle",
         -1,
         2,
-        (text_kept,),
+        (attn_kept,),
     )
     (riders,) = whole_call(
         pack_kernel,
@@ -1226,21 +1227,21 @@
         [((rider_rows(1), width), b16)],
         "pack",
         (ffn_sent,),
-    )
-    theirs = dp_permute(riders, "z", 1)
-    (riders,) = whole_call(
-        merge_kernel, (), [riders, theirs], [((rider_rows(PAIR), width), b16)], "merge"
-    )
-    attn_pairs = [
-        (attn_rows_t, [query_grad, key_grad, value_grad]),
-        (turned(grad_attn, (halves_two[0],)), [mixed]),
-    ]
-    (halves_two,) = row_chunks(attn_pairs, (2,), spot, riders=(riders,), micros=ATTN_FIRST_MICROS)
-    attn_passed = one_on(halves_two)
+        micros=PACK_MICROS,
+    )
     text_rows = caption_flat.shape[1] // BLOCKS
-    attn_one, attn_three, attn_kept = row_chunks(
-        attn_pairs, (1, 3, 0), spot, extra=attn_passed, riders=(riders,), micros=ATTN_MICROS
-    )
+    count = 1
+    held = []
+    for axis, step in (("z", 1), ("first", 1), ("first", 2)):
+        (riders,) = whole_call(
+            functools.partial(merge_kernel, count),
+            (),
+            [riders, dp_permute(riders, axis, step)],
+            [((rider_rows(2 * count), width), b16)],
+            "merge",
+        )
+        held.append(riders)
+        count *= 2
     text_own, text_sent = tiled_call(
         text_second_kernel,
         (spot,),
@@ -1249,12 +1250,12 @@
         "text_second",
         0,
         4,
-        (attn_kept,),
+        (held[TEXT_AFTER],),
     )
     stage = tiled_call(
-        functools.partial(attn_second_kernel, block_rows),
+        attn_second_kernel,
         (spot,),
-        [riders] + to_neighbours(attn_kept, attn_one, attn_three),
+        [riders] + [by_slots(part) for part in to_neighbours(attn_kept, attn_one, attn_three)],
         [((PAIR * block_rows + rider_rows(4 * PAIR), width), b16)] * RING,
         "attn_second",
         -1,

time: 314 us -> 311 us (level)
    ppermute x23 -> x25, starting transfers between devices: 41.8 us -> 40.2 us  [dp_permute(): return lax.ppermute(values, ('dp', 'tensor'), dp_perm(axis, step))]
    unnamed x241 -> x239, local copies, waits for them, and re-layouts: 27 us -> 27.5 us
    ppermute x23 -> x25, waiting for transfers between devices: 37.9 us -> 38.1 us  [dp_permute(): return lax.ppermute(values, ('dp', 'tensor'), dp_perm(axis, step))]
    pallas_call x12 -> x14, Pallas kernels: 17.5 us -> 17.6 us  [whole_call(): pl.pallas_call(lambda *refs: kernel(*refs[:count], *refs[count + len(ties...]
  transfers between devices with their start and end apart: 49 -> 51, of which waited for: 23 -> 22; matrix products, arithmetic and copies ran while one was open for 3% -> 3% of each run, Pallas kernels for 25% -> 26%
where the time goes in v3:
time: 311 us; the launch traced here: 307 us
  Pallas kernels  105 us (34%)
  waiting for transfers between devices  92.7 us (30%)
  starting transfers between devices  58.9 us (19%)
  local copies, waits for them, and re-layouts  28.1 us (9%)
  matrix products  17.7 us (6%)
    ppermute x10, waiting for transfers between devices, swap_chip(): return lax.ppermute(values, 'tensor', CHIP_SWAP)  47.4 us
    ppermute x25, starting transfers between devices, dp_permute(): return lax.ppermute(values, ('dp', 'tensor'), dp_perm(axis, step))  40.2 us
    ppermute x25, waiting for transfers between devices, dp_permute(): return lax.ppermute(values, ('dp', 'tensor'), dp_perm(axis, step))  38.1 us
    unnamed x239, local copies, waits for them, and re-layouts  27.5 us
    pallas_call x3, Pallas kernels, pair_call(): pl.pallas_call(lambda *refs: kernel(*refs[:len(operands)], *refs[len(oper...  26 us
    pallas_call x6, Pallas kernels, chunk_call(): pl.pallas_call(kernel, grid_spec=pltpu.PrefetchScalarGridSpec(num_scalar_...  23.2 us
    pallas_call x9, Pallas kernels, tiled_call(): pl.pallas_call(lambda *refs: kernel(*refs[:count], *refs[count + len(ties...  23 us
    pallas_call x14, Pallas kernels, whole_call(): pl.pallas_call(lambda *refs: kernel(*refs[:count], *refs[count + len(ties...  17.6 us
  transfers between devices with their start and end apart: 51, of which 22 were waited for; matrix products, arithmetic and copies ran while one was open for 3% of the time, Pallas kernels for 26%

profile of v3, /device:TPU:0, one launch (start us, length us, event | category | flops | bytes accessed | tf_op | source)
XLA Modules:
  0.0 306.6 jit_solution(18382086766945545882)
XLA Ops:
  0.7 3.2 %fusion.16 = f32[3,1536]{1,0:T(4,128)} fusion(bf16[1024,1536]{1,0:T(8,128)(2,1)} %param.25, bf16[3,1024]{1,0:T(4,128)(2,1)} %param.21), kind=kOutput, calls=%fused_computation.46 | convolution fusion | flops 9455616 | bytes 3170304 | tf_op jit(solution)/shard_map/dot_general | solution.py:1039
  6.4 9.3 %text.1 = (f32[768,384]{1,0:T(8,128)S(1)}, bf16[768,384]{1,0:T(8,128)(2,1)S(1)}) custom-call(bf16[768,4096]{1,0:T(8,128)(2,1)} %bitcast.41, bf16[4096,384]{1,0:T(8,128)(2,1)} %key_weight.1, bf16[4096,384]{1,0:T(8,128)(2,1)} %value_weight.1), custom_call_target="tpu_custom_call" | custom-call | flops 8999999488 | tf_op jit(solution)/shard_map/text/pallas_call | solution.py:771
  23.9 4.9 %project.1 = (bf16[512,1536]{1,0:T(8,128)(2,1)S(1)}, f32[512,384]{1,0:T(8,128)S(1)}, f32[512,384]{1,0:T(8,128)S(1)}, bf16[512,384]{1,0:T(8,128)(2,1)S(1)}) custom-call(s32[1]{0:T(128)} %bitcast.refs_0_, bf16[128,1536]{1,0:T(8,128)(2,1)S(1)} %copy-done.24, bf16[128,1536]{1,0:T(8,128)(2,1)} %collective-permute-done.refs_2_, ...), custom_call_target="tpu_custom_call" | custom-call | flops 6000000000 | tf_op jit(solution)/shard_map/project/pallas_call | solution.py:453
  30.0 9.9 %attend.1 = (bf16[512,384]{1,0:T(8,128)(2,1)S(1)}, bf16[512,384]{1,0:T(8,128)(2,1)S(1)}, bf16[768,384]{1,0:T(8,128)(2,1)S(1)}, bf16[512,384]{1,0:T(8,128)(2,1)S(...) custom-call(f32[512,384]{1,0:T(8,128)S(1)} %get-tuple-element.109.refs_0_, ...), custom_call_target="tpu_custom_call" | custom-call | flops 11000000512 | tf_op jit(solution)/shard_map/attend/pallas_call | solution.py:663
  45.9 9.4 %collective-permute-done.7.refs_4_ = bf16[128,1536]{1,0:T(8,128)(2,1)S(1)} collective-permute-done((bf16[128,1536]{1,0:T(8,128)(2,1)S(1)}, bf16[128,1536]{1,0:T(8,128)(2,1)S(1)}, u32[]{:S(2)}, u32[]{:S(2)}) %collective-permute-start.7) | collective-permute-done | bytes 393248 | tf_op jit(solution)/shard_map/ppermute | solution.py:100
  58.0 8.8 %collective-permute-done.8 = bf16[128,1536]{1,0:T(8,128)(2,1)S(1)} collective-permute-done((bf16[128,1536]{1,0:T(8,128)(2,1)S(1)}, bf16[128,1536]{1,0:T(8,128)(2,1)S(1)}, u32[]{:S(2)}, u32[]{:S(2)}) %collective-permute-start.8) | collective-permute-done | bytes 393248 | tf_op jit(solution)/shard_map/ppermute | solution.py:100
  79.2 9.0 %collective-permute-done.12.refs_4_ = bf16[128,1536]{1,0:T(8,128)(2,1)S(1)} collective-permute-done((bf16[128,1536]{1,0:T(8,128)(2,1)S(1)}, bf16[128,1536]{1,0:T(8,128)(2,1)S(1)}, u32[]{:S(2)}, u32[]{:S(2)}) %collective-permute-start.12) | collective-permute-done | bytes 393248 | tf_op jit(solution)/shard_map/ppermute | solution.py:100
  91.2 8.8 %collective-permute-done.13 = bf16[128,1536]{1,0:T(8,128)(2,1)S(1)} collective-permute-done((bf16[128,1536]{1,0:T(8,128)(2,1)S(1)}, bf16[128,1536]{1,0:T(8,128)(2,1)S(1)}, u32[]{:S(2)}, u32[]{:S(2)}) %collective-permute-start.13) | collective-permute-done | bytes 393248 | tf_op jit(solution)/shard_map/ppermute | solution.py:100
  113.5 7.7 %collective-permute-done.17.refs_5_ = bf16[128,1536]{1,0:T(8,128)(2,1)} collective-permute-done((bf16[128,1536]{1,0:T(8,128)(2,1)S(1)}, bf16[128,1536]{1,0:T(8,128)(2,1)}, u32[]{:S(2)}, u32[]{:S(2)}) %collective-permute-start.17) | collective-permute-done | bytes 393248 | tf_op jit(solution)/shard_map/ppermute | solution.py:100
  121.3 2.5 middle_back.1
  130.8 3.6 %collective-permute-done.18 = bf16[128,1536]{1,0:T(8,128)(2,1)S(1)} collective-permute-done((bf16[128,1536]{1,0:T(8,128)(2,1)S(1)}, bf16[128,1536]{1,0:T(8,128)(2,1)S(1)}, u32[]{:S(2)}, u32[]{:S(2)}) %collective-permute-start.18) | collective-permute-done | bytes 393248 | tf_op jit(solution)/shard_map/ppermute | solution.py:100
  138.3 8.3 %cross_back.1 = (f32[512,384]{1,0:T(8,128)S(1)}, bf16[384,768]{1,0:T(8,128)(2,1)S(1)}, bf16[384,768]{1,0:T(8,128)(2,1)S(1)}, f32[1,384]{1,0:T(1,128)S(1)}, f32[1,384]{1,0:T(1,128)S(1)}) custom-call(bf16[512,384]{1,0:T(8,128)(2,1)S(1)} %copy-done.52, bf16[768,384]{1,0:T(8,128)(2,1)S(1)} %copy-done.94, bf16[768,384]{1,0:T(8,128)(2,1)S(1)} %copy-done.88, ...), custom_call_target="tpu_custom_call" | custom-call | flops 10000000000 | tf_op jit(solution)/shard_map/cross_back/pallas_call | solution.py:663
  146.7 5.5 %row_chunks.5 = (bf16[384,3072]{1,0:T(8,128)(2,1)S(1)}, bf16[384,3072]{1,0:T(8,128)(2,1)S(1)}, bf16[384,3072]{1,0:T(8,128)(2,1)S(1)}) custom-call(s32[4]{0:T(128)S(1)} %pad_add_fusion.spot_ref.refs_0_, bf16[32,48,512]{2,1,0:T(8,128)(2,1)S(1)} %bitcast.68, bf16[32,48,512]{2,1,0:T(8,128)(2,1)S(1)} %bitcast.69, bf16[32,48,512]{2,1,0:T(8,128)(2,1)S(1)} %bitcast.70, ...), custom_call_target="tpu_custom_call" | custom-call | flops 8000000000 | tf_op jit(solution)/shard_map/row_chunks/pallas_call | solution.py:204
  158.3 7.9 %self_back.1 = (bf16[512,384]{1,0:T(8,128)(2,1)S(1)}, bf16[512,384]{1,0:T(8,128)(2,1)S(1)}, bf16[512,384]{1,0:T(8,128)(2,1)S(1)}, f32[2,384]{1,0:T(2,128)S(1)}) custom-call(bf16[512,384]{1,0:T(8,128)(2,1)S(1)} %copy-done.52, bf16[512,384]{1,0:T(8,128)(2,1)S(1)} %copy-done.54, bf16[512,384]{1,0:T(8,128)(2,1)S(1)} %copy-done.50, f32[512,384]{1,0:T(8,128)S(1)} %copy-done.36, ...), custom_call_target="tpu_custom_call" | custom-call | tf_op jit(solution)/shard_map/self_back/pallas_call | solution.py:663
  166.1 3.1 %attn_back.1 = (bf16[256,1536]{1,0:T(8,128)(2,1)S(1)}, bf16[256,1536]{1,0:T(8,128)(2,1)S(1)}) custom-call(bf16[512,384]{1,0:T(8,128)(2,1)S(1)} %get-tuple-element.145.refs_0_.refs_4_.refs_16_, bf16[512,384]{1,0:T(8,128)(2,1)S(1)} %get-tuple-element.146.refs_1_.refs_17_, bf16[512,384]{1,0:T(8,128)(2,1)S(1)} %get-tuple-element.147.refs_2_.refs_18_, ...), custom_call_target="tpu_custom_call" | custom-call | tf_op jit(solution)/shard_map/attn_back/pallas_call | solution.py:991
  174.3 8.0 %collective-permute-done.25 = bf16[384,3072]{1,0:T(8,128)(2,1)S(1)} collective-permute-done((bf16[384,3072]{1,0:T(8,128)(2,1)S(1)}, bf16[384,3072]{1,0:T(8,128)(2,1)S(1)}, u32[]{:S(2)}, u32[]{:S(2)}) %collective-permute-start.25) | collective-permute-done | bytes 2359328 | tf_op jit(solution)/shard_map/ppermute | solution.py:85
  184.5 4.2 %ffn_second.1 = (bf16[4,48,3072]{2,1,0:T(8,128)(2,1)S(1)}, bf16[4,48,3072]{2,1,0:T(8,128)(2,1)S(1)}) custom-call(s32[4]{0:T(128)S(1)} %pad_add_fusion.spot_ref.refs_0_, bf16[8,48,3072]{2,1,0:T(8,128)(2,1)} %bitcast.124, bf16[8,48,3072]{2,1,0:T(8,128)(2,1)} %bitcast.127, bf16[8,48,3072]{2,1,0:T(8,128)(2,1)} %bitcast.128, ...), custom_call_target="tpu_custom_call" | custom-call | tf_op jit(solution)/shard_map/ffn_second/pallas_call | solution.py:476
  197.9 2.8 collective-permute-start.32
  201.0 7.0 %column_chunks.3 = (bf16[768,1024]{1,0:T(8,128)(2,1)S(1)}, bf16[768,1024]{1,0:T(8,128)(2,1)S(1)}, bf16[768,1024]{1,0:T(8,128)(2,1)S(1)}) custom-call(s32[4]{0:T(128)S(1)} %pad_add_fusion.spot_ref.refs_0_, bf16[384,768]{1,0:T(8,128)(2,1)S(1)} %get-tuple-element.139.refs_21_.refs_0_, bf16[384,768]{1,0:T(8,128)(2,1)S(1)} %get-tuple-element.140.refs_1_, ...), custom_call_target="tpu_custom_call" | custom-call | flops 8000000000 | tf_op jit(solution)/shard_map/column_chunks/pallas_call | solution.py:204
  213.3 4.6 %row_chunks.7 = (bf16[384,1536]{1,0:T(8,128)(2,1)S(1)}, bf16[384,1536]{1,0:T(8,128)(2,1)S(1)}, bf16[384,1536]{1,0:T(8,128)(2,1)S(1)}) custom-call(s32[4]{0:T(128)S(1)} %pad_add_fusion.spot_ref.refs_0_, bf16[32,48,512]{2,1,0:T(8,128)(2,1)S(1)} %bitcast.100, bf16[32,48,512]{2,1,0:T(8,128)(2,1)S(1)} %bitcast.101, bf16[32,48,512]{2,1,0:T(8,128)(2,1)S(1)} %bitcast.102, ...), custom_call_target="tpu_custom_call" | custom-call | flops 3000000000 | tf_op jit(solution)/shard_map/row_chunks/pallas_call | solution.py:204
  221.9 2.6 collective-permute-start.39
  224.6 3.6 %collective-permute-start.35 = (bf16[32,1536]{1,0:T(8,128)(2,1)S(1)}, bf16[32,1536]{1,0:T(8,128)(2,1)S(1)}, u32[]{:S(2)}, u32[]{:S(2)}) collective-permute-start(bf16[32,1536]{1,0:T(8,128)(2,1)S(1)} %pack.1.refs_0_), channel_id=1, source_target_pairs={{0,16},{1,17},{2,18},{3,19},{4,20},{5,21},{6,22},{7,23},{8,24},{9,... | collective-permute-start | bytes 294920 | tf_op jit(solution)/shard_map/ppermute | solution.py:85
  228.2 2.6 collective-permute-done.35.refs_1_
  231.0 12.4 %collective-permute-done.36.refs_1_ = bf16[32,1536]{1,0:T(8,128)(2,1)S(1)} collective-permute-done((bf16[32,1536]{1,0:T(8,128)(2,1)S(1)}, bf16[32,1536]{1,0:T(8,128)(2,1)S(1)}, u32[]{:S(2)}, u32[]{:S(2)}) %collective-permute-start.36) | collective-permute-done | bytes 98336 | tf_op jit(solution)/shard_map/ppermute | solution.py:85
  245.9 3.6 %text_second.1 = (bf16[768,512]{1,0:T(8,128)(2,1)S(1)}, bf16[768,512]{1,0:T(8,128)(2,1)S(1)}) custom-call(s32[4]{0:T(128)S(1)} %pad_add_fusion.spot_ref.refs_0_, bf16[768,1024]{1,0:T(8,128)(2,1)} %copy-done.8, bf16[768,1024]{1,0:T(8,128)(2,1)} %copy-done.104, bf16[768,1024]{1,0:T(8,128)(2,1)} %copy-done.105, bf16[48,1536]{1,0:T(8,128)(2,1)S(1)} %merge.4.refs_0_.refs_4_), custom_call_target="tpu_custom_call" | custom-call | tf_op jit(solution)/shard_map/text_second/pallas_call | solution.py:476
  250.8 3.0 collective-permute-start.49
  254.8 7.3 %collective-permute-done.37.refs_1_ = bf16[48,1536]{1,0:T(8,128)(2,1)S(1)} collective-permute-done((bf16[48,1536]{1,0:T(8,128)(2,1)S(1)}, bf16[48,1536]{1,0:T(8,128)(2,1)S(1)}, u32[]{:S(2)}, u32[]{:S(2)}) %collective-permute-start.37) | collective-permute-done | bytes 147488 | tf_op jit(solution)/shard_map/ppermute | solution.py:85
  264.2 3.1 %attn_second.1 = (bf16[160,1536]{1,0:T(8,128)(2,1)S(1)}, bf16[160,1536]{1,0:T(8,128)(2,1)S(1)}, bf16[160,1536]{1,0:T(8,128)(2,1)S(1)}, bf16[160,1536]{1,0:T(8,128)(2,1)S(1)}) custom-call(s32[4]{0:T(128)S(1)} %pad_add_fusion.spot_ref.refs_0_, bf16[64,1536]{1,0:T(8,128)(2,1)} %copy-done.34, bf16[8,48,1536]{2,1,0:T(8,128)(2,1)} %bitcast.125, ...), custom_call_target="tpu_custom_call" | custom-call | tf_op jit(solution)/shard_map/attn_second/pallas_call | solution.py:476
  277.6 3.7 %collective-permute-start.50 = (bf16[48,3072]{1,0:T(8,128)(2,1)S(1)}, bf16[48,3072]{1,0:T(8,128)(2,1)S(1)}, u32[]{:S(2)}, u32[]{:S(2)}) collective-permute-start(bf16[48,3072]{1,0:T(8,128)(2,1)S(1)} %get-tuple-element.197), channel_id=1, source_target_pairs={{0,16},{1,17},{2,18},{3,19},{4,20},{5,21},{6,22},{7,23},{8,24},{9,... | collective-permute-start | bytes 884744 | tf_op jit(solution)/shard_map/ppermute | solution.py:85
  286.8 3.7 %collective-permute-start.45 = (bf16[48,1536]{1,0:T(8,128)(2,1)}, bf16[48,1536]{1,0:T(8,128)(2,1)}, u32[]{:S(2)}, u32[]{:S(2)}) collective-permute-start(bf16[48,1536]{1,0:T(8,128)(2,1)} %get-tuple-element.181), channel_id=1, source_target_pairs={{0,16},{1,17},{2,18},{3,19},{4,20},{5,21},{6,22},{7,23},{8,24},{9,... | collective-permute-start | bytes 442376 | tf_op jit(solution)/shard_map/ppermute | solution.py:85
  292.3 2.7 ada.1
  301.4 3.0 collective-permute-done.48.refs_1_
  (372 shorter events, 124.2 us)
Async XLA Ops:
  3.9 13.7 %collective-permute-start.4 = (f32[3,1536]{1,0:T(4,128)}, f32[3,1536]{1,0:T(4,128)}, u32[]{:S(2)}, u32[]{:S(2)}) collective-permute-start(f32[3,1536]{1,0:T(4,128)} %fusion.16), channel_id=1, source_target_pairs={{0,2},{2,0},{1,3},{3,1},{4,6},{6,4},{5,7},{7,5},{8,10},{10,8},{9,1... | collective-permute-start | bytes 55304 | tf_op jit(solution)/shard_map/ppermute | solution.py:100
  5.9 17.0 %collective-permute-start.3 = (f32[3,1536]{1,0:T(4,128)}, f32[3,1536]{1,0:T(4,128)}, u32[]{:S(2)}, u32[]{:S(2)}) collective-permute-start(f32[3,1536]{1,0:T(4,128)} %fusion.16), channel_id=1, source_target_pairs={{0,1},{1,0},{2,3},{3,2},{4,5},{5,4},{6,7},{7,6},{8,9},{9,8},{10,11... | collective-permute-start | bytes 55304 | tf_op jit(solution)/shard_map/ppermute | solution.py:96
  5.9 17.9 %collective-permute-start.1 = (bf16[128,1536]{1,0:T(8,128)(2,1)S(1)}, bf16[128,1536]{1,0:T(8,128)(2,1)}, u32[]{:S(2)}, u32[]{:S(2)}) collective-permute-start(bf16[128,1536]{1,0:T(8,128)(2,1)S(1)} %copy-done.24), channel_id=1, source_target_pairs={{0,1},{1,0},{2,3},{3,2},{4,5},{5,4},{6,7},{7,6},{8,9},{9,8},{10,11... | collective-permute-start | bytes 1179656 | tf_op jit(solution)/shard_map/ppermute | solution.py:96
  6.4 11.2 %collective-permute-start = (bf16[128,1536]{1,0:T(8,128)(2,1)S(1)}, bf16[128,1536]{1,0:T(8,128)(2,1)}, u32[]{:S(2)}, u32[]{:S(2)}) collective-permute-start(bf16[128,1536]{1,0:T(8,128)(2,1)S(1)} %copy-done.24), channel_id=1, source_target_pairs={{0,2},{2,0},{1,3},{3,1},{4,6},{6,4},{5,7},{7,5},{8,10},{10,8},{9,1... | collective-permute-start | bytes 1179656 | tf_op jit(solution)/shard_map/ppermute | solution.py:100
  43.8 11.5 %collective-permute-start.7 = (bf16[128,1536]{1,0:T(8,128)(2,1)S(1)}, bf16[128,1536]{1,0:T(8,128)(2,1)S(1)}, u32[]{:S(2)}, u32[]{:S(2)}) collective-permute-start(bf16[128,1536]{1,0:T(8,128)(2,1)S(1)} %add_convert_fusion.3.rest_0_), channel_id=1, source_target_pairs={{0,2},{2,0},{1,3},{3,1},{4,6},{6,4},{5,7},{7,5},{8,10},{10,8},{9,1... | collective-permute-start | bytes 1179656 | tf_op jit(solution)/shard_map/ppermute | solution.py:100
  77.0 11.2 %collective-permute-start.12 = (bf16[128,1536]{1,0:T(8,128)(2,1)S(1)}, bf16[128,1536]{1,0:T(8,128)(2,1)S(1)}, u32[]{:S(2)}, u32[]{:S(2)}) collective-permute-start(bf16[128,1536]{1,0:T(8,128)(2,1)S(1)} %add_convert_fusion.2.rest_0_), channel_id=1, source_target_pairs={{0,2},{2,0},{1,3},{3,1},{4,6},{6,4},{5,7},{7,5},{8,10},{10,8},{9,1... | collective-permute-start | bytes 1179656 | tf_op jit(solution)/shard_map/ppermute | solution.py:100
  109.7 11.6 %collective-permute-start.17 = (bf16[128,1536]{1,0:T(8,128)(2,1)S(1)}, bf16[128,1536]{1,0:T(8,128)(2,1)}, u32[]{:S(2)}, u32[]{:S(2)}) collective-permute-start(bf16[128,1536]{1,0:T(8,128)(2,1)S(1)} %add_convert_fusion.1.rest_0_.refs_19_), channel_id=1, source_target_pairs={{0,2},{2,0},{1,3},{3,1},{4,6},{6,4},{5,7},{7,5},{8,10},{10,8},{9,1... | collective-permute-start | bytes 1179656 | tf_op jit(solution)/shard_map/ppermute | solution.py:100
  127.5 19.1 %collective-permute-start.21 = (bf16[384,1536]{1,0:T(8,128)(2,1)S(1)}, bf16[384,1536]{1,0:T(8,128)(2,1)S(1)}, u32[]{:S(2)}, u32[]{:S(2)}) collective-permute-start(bf16[384,1536]{1,0:T(8,128)(2,1)S(1)} %get-tuple-element.141), channel_id=1, source_target_pairs={{0,32},{1,5},{2,34},{3,7},{4,36},{5,9},{6,38},{7,11},{8,40},{9,13}... | collective-permute-start | bytes 3538952 | tf_op jit(solution)/shard_map/ppermute | solution.py:85
  129.0 17.6 %collective-permute-start.22 = (bf16[384,1536]{1,0:T(8,128)(2,1)S(1)}, bf16[384,1536]{1,0:T(8,128)(2,1)S(1)}, u32[]{:S(2)}, u32[]{:S(2)}) collective-permute-start(bf16[384,1536]{1,0:T(8,128)(2,1)S(1)} %get-tuple-element.142), channel_id=1, source_target_pairs={{0,96},{1,13},{2,98},{3,15},{4,100},{5,1},{6,102},{7,3},{8,104},{9... | collective-permute-start | bytes 3538952 | tf_op jit(solution)/shard_map/ppermute | solution.py:85
  152.2 30.1 %collective-permute-start.25 = (bf16[384,3072]{1,0:T(8,128)(2,1)S(1)}, bf16[384,3072]{1,0:T(8,128)(2,1)S(1)}, u32[]{:S(2)}, u32[]{:S(2)}) collective-permute-start(bf16[384,3072]{1,0:T(8,128)(2,1)S(1)} %get-tuple-element.150), channel_id=1, source_target_pairs={{0,32},{1,5},{2,34},{3,7},{4,36},{5,9},{6,38},{7,11},{8,40},{9,13}... | collective-permute-start | bytes 7077896 | tf_op jit(solution)/shard_map/ppermute | solution.py:85
  153.7 29.0 %collective-permute-start.26 = (bf16[384,3072]{1,0:T(8,128)(2,1)S(1)}, bf16[384,3072]{1,0:T(8,128)(2,1)S(1)}, u32[]{:S(2)}, u32[]{:S(2)}) collective-permute-start(bf16[384,3072]{1,0:T(8,128)(2,1)S(1)} %get-tuple-element.151), channel_id=1, source_target_pairs={{0,96},{1,13},{2,98},{3,15},{4,100},{5,1},{6,102},{7,3},{8,104},{9... | collective-permute-start | bytes 7077896 | tf_op jit(solution)/shard_map/ppermute | solution.py:85
  169.4 31.3 %collective-permute-start.33 = (bf16[384,1024]{1,0:T(8,128)(2,1)S(1)}, bf16[384,1024]{1,0:T(8,128)(2,1)S(1)}, u32[]{:S(2)}, u32[]{:S(2)}) collective-permute-start(bf16[384,1024]{1,0:T(8,128)(2,1)S(1)} %get-tuple-element.144.refs_14_.rest_0_), channel_id=1, source_target_pairs={{0,32},{1,5},{2,34},{3,7},{4,36},{5,9},{6,38},{7,11},{8,40},{9,13}... | collective-permute-start | bytes 2359304 | tf_op jit(solution)/shard_map/ppermute | solution.py:85
  170.5 27.4 %collective-permute-start.34 = (bf16[384,1024]{1,0:T(8,128)(2,1)S(1)}, bf16[384,1024]{1,0:T(8,128)(2,1)S(1)}, u32[]{:S(2)}, u32[]{:S(2)}) collective-permute-start(bf16[384,1024]{1,0:T(8,128)(2,1)S(1)} %get-tuple-element.165), channel_id=1, source_target_pairs={{0,96},{1,13},{2,98},{3,15},{4,100},{5,1},{6,102},{7,3},{8,104},{9... | collective-permute-start | bytes 2359304 | tf_op jit(solution)/shard_map/ppermute | solution.py:85
  172.8 20.0 %collective-permute-start.24 = (bf16[128,1536]{1,0:T(8,128)(2,1)S(1)}, bf16[128,1536]{1,0:T(8,128)(2,1)S(1)}, u32[]{:S(2)}, u32[]{:S(2)}) collective-permute-start(bf16[128,1536]{1,0:T(8,128)(2,1)S(1)} %add_convert_fusion), channel_id=1, source_target_pairs={{0,2},{2,0},{1,3},{3,1},{4,6},{6,4},{5,7},{7,5},{8,10},{10,8},{9,1... | collective-permute-start | bytes 1179656 | tf_op jit(solution)/shard_map/ppermute | solution.py:100
  189.8 28.2 %collective-permute-start.30 = (bf16[4,48,3072]{2,1,0:T(8,128)(2,1)S(1)}, bf16[4,48,3072]{2,1,0:T(8,128)(2,1)S(1)}, u32[]{:S(2)}, u32[]{:S(2)}) collective-permute-start(bf16[4,48,3072]{2,1,0:T(8,128)(2,1)S(1)} %get-tuple-element.152.refs_10_), channel_id=1, source_target_pairs={{0,4},{1,33},{2,6},{3,35},{4,0},{5,37},{6,2},{7,39},{8,12},{9,41},... | collective-permute-start | bytes 3538952 | tf_op jit(solution)/shard_map/ppermute | solution.py:85
  194.6 27.3 %collective-permute-start.28 = (f32[16,1536]{1,0:T(8,128)S(1)}, f32[16,1536]{1,0:T(8,128)S(1)}, u32[]{:S(2)}, u32[]{:S(2)}) collective-permute-start(f32[16,1536]{1,0:T(8,128)S(1)} %stack_sums.1.refs_20_.refs_1_), channel_id=1, source_target_pairs={{0,1},{1,0},{2,3},{3,2},{4,5},{5,4},{6,7},{7,6},{8,9},{9,8},{10,11... | collective-permute-start | bytes 294920 | tf_op jit(solution)/shard_map/ppermute | solution.py:96
  194.7 13.4 %collective-permute-start.27 = (f32[16,1536]{1,0:T(8,128)S(1)}, f32[16,1536]{1,0:T(8,128)S(1)}, u32[]{:S(2)}, u32[]{:S(2)}) collective-permute-start(f32[16,1536]{1,0:T(8,128)S(1)} %stack_sums.1.refs_20_.refs_1_), channel_id=1, source_target_pairs={{0,2},{2,0},{1,3},{3,1},{4,6},{6,4},{5,7},{7,5},{8,10},{10,8},{9,1... | collective-permute-start | bytes 294920 | tf_op jit(solution)/shard_map/ppermute | solution.py:100
  197.9 12.7 %collective-permute-start.32 = (bf16[384,768]{1,0:T(8,128)(2,1)S(1)}, bf16[384,768]{1,0:T(8,128)(2,1)S(1)}, u32[]{:S(2)}, u32[]{:S(2)}) collective-permute-start(bf16[384,768]{1,0:T(8,128)(2,1)S(1)} %get-tuple-element.164), channel_id=1, source_target_pairs={{0,96},{1,13},{2,98},{3,15},{4,100},{5,1},{6,102},{7,3},{8,104},{9... | collective-permute-start | bytes 1769480 | tf_op jit(solution)/shard_map/ppermute | solution.py:85
  200.7 11.3 %collective-permute-start.31 = (bf16[384,768]{1,0:T(8,128)(2,1)S(1)}, bf16[384,768]{1,0:T(8,128)(2,1)S(1)}, u32[]{:S(2)}, u32[]{:S(2)}) collective-permute-start(bf16[384,768]{1,0:T(8,128)(2,1)S(1)} %get-tuple-element.163.refs_12_), channel_id=1, source_target_pairs={{0,32},{1,5},{2,34},{3,7},{4,36},{5,9},{6,38},{7,11},{8,40},{9,13}... | collective-permute-start | bytes 1769480 | tf_op jit(solution)/shard_map/ppermute | solution.py:85
  208.0 35.5 %collective-permute-start.40 = (bf16[768,1024]{1,0:T(8,128)(2,1)S(1)}, bf16[768,1024]{1,0:T(8,128)(2,1)S(1)}, u32[]{:S(2)}, u32[]{:S(2)}) collective-permute-start(bf16[768,1024]{1,0:T(8,128)(2,1)S(1)} %get-tuple-element.171), channel_id=1, source_target_pairs={{0,32},{1,5},{2,34},{3,7},{4,36},{5,9},{6,38},{7,11},{8,40},{9,13}... | collective-permute-start | bytes 4718600 | tf_op jit(solution)/shard_map/ppermute | solution.py:85
  210.6 32.9 %collective-permute-start.41 = (bf16[768,1024]{1,0:T(8,128)(2,1)S(1)}, bf16[768,1024]{1,0:T(8,128)(2,1)S(1)}, u32[]{:S(2)}, u32[]{:S(2)}) collective-permute-start(bf16[768,1024]{1,0:T(8,128)(2,1)S(1)} %get-tuple-element.172), channel_id=1, source_target_pairs={{0,96},{1,13},{2,98},{3,15},{4,100},{5,1},{6,102},{7,3},{8,104},{9... | collective-permute-start | bytes 4718600 | tf_op jit(solution)/shard_map/ppermute | solution.py:85
  212.0 12.4 %collective-permute-start.29 = (f32[16,1536]{1,0:T(8,128)S(1)}, f32[16,1536]{1,0:T(8,128)S(1)}, u32[]{:S(2)}, u32[]{:S(2)}) collective-permute-start(f32[16,1536]{1,0:T(8,128)S(1)} %collective-permute-done.27.refs_2_), channel_id=1, source_target_pairs={{0,1},{1,0},{2,3},{3,2},{4,5},{5,4},{6,7},{7,6},{8,9},{9,8},{10,11... | collective-permute-start | bytes 294920 | tf_op jit(solution)/shard_map/ppermute | solution.py:96
  218.0 44.9 %collective-permute-start.38 = (bf16[384,1536]{1,0:T(8,128)(2,1)S(1)}, bf16[384,1536]{1,0:T(8,128)(2,1)S(1)}, u32[]{:S(2)}, u32[]{:S(2)}) collective-permute-start(bf16[384,1536]{1,0:T(8,128)(2,1)S(1)} %get-tuple-element.169), channel_id=1, source_target_pairs={{0,32},{1,5},{2,34},{3,7},{4,36},{5,9},{6,38},{7,11},{8,40},{9,13}... | collective-permute-start | bytes 3538952 | tf_op jit(solution)/shard_map/ppermute | solution.py:85
  221.9 41.0 %collective-permute-start.39 = (bf16[384,1536]{1,0:T(8,128)(2,1)S(1)}, bf16[384,1536]{1,0:T(8,128)(2,1)S(1)}, u32[]{:S(2)}, u32[]{:S(2)}) collective-permute-start(bf16[384,1536]{1,0:T(8,128)(2,1)S(1)} %get-tuple-element.170), channel_id=1, source_target_pairs={{0,96},{1,13},{2,98},{3,15},{4,100},{5,1},{6,102},{7,3},{8,104},{9... | collective-permute-start | bytes 3538952 | tf_op jit(solution)/shard_map/ppermute | solution.py:85
  230.9 12.5 %collective-permute-start.36 = (bf16[32,1536]{1,0:T(8,128)(2,1)S(1)}, bf16[32,1536]{1,0:T(8,128)(2,1)S(1)}, u32[]{:S(2)}, u32[]{:S(2)}) collective-permute-start(bf16[32,1536]{1,0:T(8,128)(2,1)S(1)} %merge.3.refs_0_), channel_id=1, source_target_pairs={{0,32},{1,5},{2,34},{3,7},{4,36},{5,9},{6,38},{7,11},{8,40},{9,13}... | collective-permute-start | bytes 294920 | tf_op jit(solution)/shard_map/ppermute | solution.py:85
  250.4 20.3 %collective-permute-start.46 = (bf16[768,512]{1,0:T(8,128)(2,1)S(1)}, bf16[768,512]{1,0:T(8,128)(2,1)S(1)}, u32[]{:S(2)}, u32[]{:S(2)}) collective-permute-start(bf16[768,512]{1,0:T(8,128)(2,1)S(1)} %get-tuple-element.173.refs_5_), channel_id=1, source_target_pairs={{0,4},{1,33},{2,6},{3,35},{4,0},{5,37},{6,2},{7,39},{8,12},{9,41},... | collective-permute-start | bytes 2359304 | tf_op jit(solution)/shard_map/ppermute | solution.py:85
  250.8 24.6 %collective-permute-start.49 = (bf16[2,48,3072]{2,1,0:T(8,128)(2,1)S(1)}, bf16[2,48,3072]{2,1,0:T(8,128)(2,1)S(1)}, u32[]{:S(2)}, u32[]{:S(2)}) collective-permute-start(bf16[2,48,3072]{2,1,0:T(8,128)(2,1)S(1)} %get-tuple-element.168.refs_8_), channel_id=1, source_target_pairs={{0,12},{1,97},{2,14},{3,99},{4,8},{5,101},{6,10},{7,103},{8,4},{9,... | collective-permute-start | bytes 1769480 | tf_op jit(solution)/shard_map/ppermute | solution.py:85
  267.3 15.4 %collective-permute-start.42 = (bf16[160,1536]{1,0:T(8,128)(2,1)S(1)}, bf16[160,1536]{1,0:T(8,128)(2,1)S(1)}, u32[]{:S(2)}, u32[]{:S(2)}) collective-permute-start(bf16[160,1536]{1,0:T(8,128)(2,1)S(1)} %get-tuple-element.175), channel_id=1, source_target_pairs={{0,4},{1,33},{2,6},{3,35},{4,8},{5,37},{6,10},{7,39},{8,12},{9,41}... | collective-permute-start | bytes 1474568 | tf_op jit(solution)/shard_map/ppermute | solution.py:85
  267.6 15.2 %collective-permute-start.43 = (bf16[160,1536]{1,0:T(8,128)(2,1)S(1)}, bf16[160,1536]{1,0:T(8,128)(2,1)S(1)}, u32[]{:S(2)}, u32[]{:S(2)}) collective-permute-start(bf16[160,1536]{1,0:T(8,128)(2,1)S(1)} %get-tuple-element.176), channel_id=1, source_target_pairs={{0,8},{1,65},{2,10},{3,67},{4,12},{5,69},{6,14},{7,71},{8,0},{9,73... | collective-permute-start | bytes 1474568 | tf_op jit(solution)/shard_map/ppermute | solution.py:85
  269.1 14.5 %collective-permute-start.44 = (bf16[160,1536]{1,0:T(8,128)(2,1)S(1)}, bf16[160,1536]{1,0:T(8,128)(2,1)S(1)}, u32[]{:S(2)}, u32[]{:S(2)}) collective-permute-start(bf16[160,1536]{1,0:T(8,128)(2,1)S(1)} %get-tuple-element.177), channel_id=1, source_target_pairs={{0,12},{1,97},{2,14},{3,99},{4,0},{5,101},{6,2},{7,103},{8,4},{9,1... | collective-permute-start | bytes 1474568 | tf_op jit(solution)/shard_map/ppermute | solution.py:85
  274.4 20.5 %collective-permute-start.47 = (bf16[768,256]{1,0:T(8,128)(2,1)}, bf16[768,256]{1,0:T(8,128)(2,1)}, u32[]{:S(2)}, u32[]{:S(2)}) collective-permute-start(bf16[768,256]{1,0:T(8,128)(2,1)} %get-tuple-element.188), channel_id=1, source_target_pairs={{0,12},{1,97},{2,14},{3,99},{4,8},{5,101},{6,10},{7,103},{8,4},{9,... | collective-permute-start | bytes 1179656 | tf_op jit(solution)/shard_map/ppermute | solution.py:85
  277.6 12.9 %collective-permute-start.50 = (bf16[48,3072]{1,0:T(8,128)(2,1)S(1)}, bf16[48,3072]{1,0:T(8,128)(2,1)S(1)}, u32[]{:S(2)}, u32[]{:S(2)}) collective-permute-start(bf16[48,3072]{1,0:T(8,128)(2,1)S(1)} %get-tuple-element.197), channel_id=1, source_target_pairs={{0,16},{1,17},{2,18},{3,19},{4,20},{5,21},{6,22},{7,23},{8,24},{9,... | collective-permute-start | bytes 884744 | tf_op jit(solution)/shard_map/ppermute | solution.py:85
  (133 other events, 821.3 us)

commit v4 on v3

--- a/solution.py
+++ b/solution.py
@@ -33,8 +33,8 @@
 SELF_MICROS = 0
 ATTN_MICROS = 3
 TEXT_MICROS = 8
-TEXT_AFTER = 1
 PACK_MICROS = 16
+SECOND_MICROS = 8
 ATTN_FIRST_MICROS = 0
 
 RING = 4
@@ -230,20 +230,7 @@
     lefts, rights = inputs[: SLOTS * len(groups)], inputs[SLOTS * len(groups) :]
     size = SLOTS * lefts[0].shape[1]
     if len(rights) > sum(groups):
-        riders = rights[-1][...]
-        count, half = riders.shape[0], riders.shape[1] // 2
-        first, second = slice(size, size + count), slice(size + count, size + 2 * count)
-        if offset == 2:
-            for side in (slice(0, half), slice(half, 2 * half)):
-                slot[first, side] = riders[:, :half]
-                slot[second, side] = riders[:, half:]
-        else:
-            slot[first, :] = riders
-            if offset == 1:
-                slot[second, :half] = added[1][first, :]
-                slot[second, half:] = added[1][second, :]
-            else:
-                slot[second, :] = riders
+        slot[size:, :] = rights[-1][...]
     column = place = 0
     for group, count in enumerate(groups):
         rows = jnp.concatenate(
@@ -287,7 +274,7 @@
             operands.append(left)
     specs += [pl.BlockSpec(right.shape, lambda step, spot: (0, 0)) for right in rights]
     specs += [pl.BlockSpec(part.shape, lambda step, spot: (0, 0)) for part in riders]
-    rows = SLOTS * lefts[0].shape[1] + sum(2 * part.shape[0] for part in riders)
+    rows = SLOTS * lefts[0].shape[1] + sum(part.shape[0] for part in riders)
     halves = [(slice(0, rows), slice(0, total // 2)), (slice(0, rows), slice(total // 2, total))]
     return chunk_call(
         functools.partial(make_rows, [len(group) for _, group in pairs]),
@@ -422,14 +409,19 @@
     textvalue[...] = total[columns:].T
 
 
-def attn_second_kernel(spot, riders, *refs):
+def attn_second_kernel(rows, spot, riders, opposite, *refs):
     parts, outs = refs[:-RING], refs[-RING:]
-    rows = parts[0].shape[1]
+    size = SLOTS * rows
     for offset in range(RING):
         for z in range(PAIR):
             slot = z * RING + (spot[2] + offset) % RING
-            outs[offset][z * rows : (z + 1) * rows, :] = add_up(parts, slot).astype(jnp.bfloat16)
-        outs[offset][PAIR * rows :, :] = riders[...]
+            index = (pl.ds(pl.multiple_of(slot * rows, 16), rows), slice(None))
+            outs[offset][z * rows : (z + 1) * rows, :] = add_up(parts, index).astype(jnp.bfloat16)
+    pairs = ((riders[...], parts[1][size:, :]), (opposite[...], parts[2][size:, :]))
+    joined = [merge_rows(PAIR, first, second, rider_rows(2 * PAIR)) for first, second in pairs]
+    joined = merge_rows(2 * PAIR, joined[0], joined[1], rider_rows(4 * PAIR))
+    for out in outs:
+        out[PAIR * rows :, :] = joined
 
 
 def attn_third_kernel(spot, *refs):
@@ -1207,9 +1199,6 @@
     text_one, text_three, text_kept = column_chunks(
         text_lefts, caption_flat, (1, 3, 0), spot, extra=text_passed, ties=(halves_two[0],), micros=TEXT_MICROS
     )
-    attn_one, attn_three, attn_kept = row_chunks(
-        attn_pairs, (1, 3, 0), spot, extra=attn_passed, ties=(text_kept,), micros=ATTN_MICROS
-    )
     ffn_own, ffn_sent = tiled_call(
         ffn_middle_kernel,
         (),
@@ -1218,7 +1207,7 @@
         "ffn_middle",
         -1,
         2,
-        (attn_kept,),
+        (text_kept,),
     )
     (riders,) = whole_call(
         pack_kernel,
@@ -1229,19 +1218,18 @@
         (ffn_sent,),
         micros=PACK_MICROS,
     )
+    (riders,) = whole_call(
+        functools.partial(merge_kernel, 1),
+        (),
+        [riders, dp_permute(riders, "z", 1)],
+        [((rider_rows(PAIR), width), b16)],
+        "merge",
+    )
+    opposite = dp_permute(riders, "first", 2)
+    attn_one, attn_three, attn_kept = row_chunks(
+        attn_pairs, (1, 3, 0), spot, extra=attn_passed, riders=(riders,), ties=(text_kept,), micros=ATTN_MICROS
+    )
     text_rows = caption_flat.shape[1] // BLOCKS
-    count = 1
-    held = []
-    for axis, step in (("z", 1), ("first", 1), ("first", 2)):
-        (riders,) = whole_call(
-            functools.partial(merge_kernel, count),
-            (),
-            [riders, dp_permute(riders, axis, step)],
-            [((rider_rows(2 * count), width), b16)],
-            "merge",
-        )
-        held.append(riders)
-        count *= 2
     text_own, text_sent = tiled_call(
         text_second_kernel,
         (spot,),
@@ -1250,12 +1238,13 @@
         "text_second",
         0,
         4,
-        (held[TEXT_AFTER],),
+        (opposite,),
+        micros=SECOND_MICROS,
     )
     stage = tiled_call(
-        attn_second_kernel,
+        functools.partial(attn_second_kernel, block_rows),
         (spot,),
-        [riders] + [by_slots(part) for part in to_neighbours(attn_kept, attn_one, attn_three)],
+        [riders, opposite] + to_neighbours(attn_kept, attn_one, attn_three),
         [((PAIR * block_rows + rider_rows(4 * PAIR), width), b16)] * RING,
         "attn_second",
         -1,

time: 311 us -> 310 us (level)
  the two profiles are of different devices: /device:TPU:0 before, /device:TPU:118 now
where the time goes in v4:
time: 310 us; the launch traced here: 305 us
  waiting for transfers between devices  119 us (38%)
  Pallas kernels  105 us (34%)
  starting transfers between devices  34.3 us (11%)
  local copies, waits for them, and re-layouts  25.1 us (8%)
  matrix products  17.6 us (6%)
    ppermute x24, waiting for transfers between devices, dp_permute(): return lax.ppermute(values, ('dp', 'tensor'), dp_perm(axis, step))  56.4 us
    ppermute x10, waiting for transfers between devices, swap_chip(): return lax.ppermute(values, 'tensor', CHIP_SWAP)  55.1 us
    pallas_call x3, Pallas kernels, pair_call(): pl.pallas_call(lambda *refs: kernel(*refs[:len(operands)], *refs[len(oper...  26 us
    ppermute x24, starting transfers between devices, dp_permute(): return lax.ppermute(values, ('dp', 'tensor'), dp_perm(axis, step))  25.7 us
    unnamed x241, local copies, waits for them, and re-layouts  24.5 us
    pallas_call x6, Pallas kernels, chunk_call(): pl.pallas_call(kernel, grid_spec=pltpu.PrefetchScalarGridSpec(num_scalar_...  23.7 us
    pallas_call x9, Pallas kernels, tiled_call(): pl.pallas_call(lambda *refs: kernel(*refs[:count], *refs[count + len(ties...  22.5 us
    pallas_call x12, Pallas kernels, whole_call(): pl.pallas_call(lambda *refs: kernel(*refs[:count], *refs[count + len(ties...  17.5 us
  transfers between devices with their start and end apart: 50, of which 23 were waited for; matrix products, arithmetic and copies ran while one was open for 3% of the time, Pallas kernels for 26%

profile of v4, /device:TPU:118, one launch (start us, length us, event | category | flops | bytes accessed | tf_op | source)
XLA Modules:
  0.0 305.1 jit_solution(1935645965121189917)
XLA Ops:
  0.7 3.2 %fusion.16 = f32[3,1536]{1,0:T(4,128)} fusion(bf16[1024,1536]{1,0:T(8,128)(2,1)} %param.25, bf16[3,1024]{1,0:T(4,128)(2,1)} %param.21), kind=kOutput, calls=%fused_computation.46 | convolution fusion | flops 9455616 | bytes 3170304 | tf_op jit(solution)/shard_map/dot_general | solution.py:1031
  6.4 9.3 %text.1 = (f32[768,384]{1,0:T(8,128)S(1)}, bf16[768,384]{1,0:T(8,128)(2,1)S(1)}) custom-call(bf16[768,4096]{1,0:T(8,128)(2,1)} %bitcast.38, bf16[4096,384]{1,0:T(8,128)(2,1)} %key_weight.1, bf16[4096,384]{1,0:T(8,128)(2,1)} %value_weight.1), custom_call_target="tpu_custom_call" | custom-call | flops 8999999488 | tf_op jit(solution)/shard_map/text/pallas_call | solution.py:763
  23.9 4.9 %project.1 = (bf16[512,1536]{1,0:T(8,128)(2,1)S(1)}, f32[512,384]{1,0:T(8,128)S(1)}, f32[512,384]{1,0:T(8,128)S(1)}, bf16[512,384]{1,0:T(8,128)(2,1)S(1)}) custom-call(s32[1]{0:T(128)} %bitcast.refs_0_, bf16[128,1536]{1,0:T(8,128)(2,1)S(1)} %copy-done.23, bf16[128,1536]{1,0:T(8,128)(2,1)} %collective-permute-done.refs_2_, ...), custom_call_target="tpu_custom_call" | custom-call | flops 6000000000 | tf_op jit(solution)/shard_map/project/pallas_call | solution.py:445
  30.0 9.9 %attend.1 = (bf16[512,384]{1,0:T(8,128)(2,1)S(1)}, bf16[512,384]{1,0:T(8,128)(2,1)S(1)}, bf16[768,384]{1,0:T(8,128)(2,1)S(1)}, bf16[512,384]{1,0:T(8,128)(2,1)S(...) custom-call(f32[512,384]{1,0:T(8,128)S(1)} %get-tuple-element.109.refs_0_, ...), custom_call_target="tpu_custom_call" | custom-call | flops 11000000512 | tf_op jit(solution)/shard_map/attend/pallas_call | solution.py:655
  44.3 10.7 %collective-permute-done.7.refs_4_ = bf16[128,1536]{1,0:T(8,128)(2,1)S(1)} collective-permute-done((bf16[128,1536]{1,0:T(8,128)(2,1)S(1)}, bf16[128,1536]{1,0:T(8,128)(2,1)S(1)}, u32[]{:S(2)}, u32[]{:S(2)}) %collective-permute-start.7) | collective-permute-done | bytes 393248 | tf_op jit(solution)/shard_map/ppermute | solution.py:100
  56.4 9.9 %collective-permute-done.8 = bf16[128,1536]{1,0:T(8,128)(2,1)S(1)} collective-permute-done((bf16[128,1536]{1,0:T(8,128)(2,1)S(1)}, bf16[128,1536]{1,0:T(8,128)(2,1)S(1)}, u32[]{:S(2)}, u32[]{:S(2)}) %collective-permute-start.8) | collective-permute-done | bytes 393248 | tf_op jit(solution)/shard_map/ppermute | solution.py:100
  77.6 10.0 %collective-permute-done.12.refs_4_ = bf16[128,1536]{1,0:T(8,128)(2,1)S(1)} collective-permute-done((bf16[128,1536]{1,0:T(8,128)(2,1)S(1)}, bf16[128,1536]{1,0:T(8,128)(2,1)S(1)}, u32[]{:S(2)}, u32[]{:S(2)}) %collective-permute-start.12) | collective-permute-done | bytes 393248 | tf_op jit(solution)/shard_map/ppermute | solution.py:100
  89.6 9.9 %collective-permute-done.13 = bf16[128,1536]{1,0:T(8,128)(2,1)S(1)} collective-permute-done((bf16[128,1536]{1,0:T(8,128)(2,1)S(1)}, bf16[128,1536]{1,0:T(8,128)(2,1)S(1)}, u32[]{:S(2)}, u32[]{:S(2)}) %collective-permute-start.13) | collective-permute-done | bytes 393248 | tf_op jit(solution)/shard_map/ppermute | solution.py:100
  101.2 2.4 multiply_convert_fusion
  112.0 8.8 %collective-permute-done.17.refs_5_ = bf16[128,1536]{1,0:T(8,128)(2,1)} collective-permute-done((bf16[128,1536]{1,0:T(8,128)(2,1)S(1)}, bf16[128,1536]{1,0:T(8,128)(2,1)}, u32[]{:S(2)}, u32[]{:S(2)}) %collective-permute-start.17) | collective-permute-done | bytes 393248 | tf_op jit(solution)/shard_map/ppermute | solution.py:100
  120.8 2.5 middle_back.1
  128.1 5.8 %collective-permute-done.18 = bf16[128,1536]{1,0:T(8,128)(2,1)S(1)} collective-permute-done((bf16[128,1536]{1,0:T(8,128)(2,1)S(1)}, bf16[128,1536]{1,0:T(8,128)(2,1)S(1)}, u32[]{:S(2)}, u32[]{:S(2)}) %collective-permute-start.18) | collective-permute-done | bytes 393248 | tf_op jit(solution)/shard_map/ppermute | solution.py:100
  137.9 8.3 %cross_back.1 = (f32[512,384]{1,0:T(8,128)S(1)}, bf16[384,768]{1,0:T(8,128)(2,1)S(1)}, bf16[384,768]{1,0:T(8,128)(2,1)S(1)}, f32[1,384]{1,0:T(1,128)S(1)}, f32[1,384]{1,0:T(1,128)S(1)}) custom-call(bf16[512,384]{1,0:T(8,128)(2,1)S(1)} %copy-done.52, bf16[768,384]{1,0:T(8,128)(2,1)S(1)} %copy-done.95, bf16[768,384]{1,0:T(8,128)(2,1)S(1)} %copy-done.89, ...), custom_call_target="tpu_custom_call" | custom-call | flops 10000000000 | tf_op jit(solution)/shard_map/cross_back/pallas_call | solution.py:655
  146.2 5.5 %row_chunks.5 = (bf16[384,3072]{1,0:T(8,128)(2,1)S(1)}, bf16[384,3072]{1,0:T(8,128)(2,1)S(1)}, bf16[384,3072]{1,0:T(8,128)(2,1)S(1)}) custom-call(s32[4]{0:T(128)S(1)} %pad_add_fusion.spot_ref.refs_0_, bf16[32,48,512]{2,1,0:T(8,128)(2,1)S(1)} %bitcast.97, bf16[32,48,512]{2,1,0:T(8,128)(2,1)S(1)} %bitcast.98, bf16[32,48,512]{2,1,0:T(8,128)(2,1)S(1)} %bitcast.99, ...), custom_call_target="tpu_custom_call" | custom-call | flops 8000000000 | tf_op jit(solution)/shard_map/row_chunks/pallas_call | solution.py:204
  156.6 7.8 %self_back.1 = (bf16[512,384]{1,0:T(8,128)(2,1)S(1)}, bf16[512,384]{1,0:T(8,128)(2,1)S(1)}, bf16[512,384]{1,0:T(8,128)(2,1)S(1)}, f32[2,384]{1,0:T(2,128)S(1)}) custom-call(bf16[512,384]{1,0:T(8,128)(2,1)S(1)} %copy-done.52, bf16[512,384]{1,0:T(8,128)(2,1)S(1)} %copy-done.54, bf16[512,384]{1,0:T(8,128)(2,1)S(1)} %copy-done.50, f32[512,384]{1,0:T(8,128)S(1)} %copy-done.36, ...), custom_call_target="tpu_custom_call" | custom-call | tf_op jit(solution)/shard_map/self_back/pallas_call | solution.py:655
  164.4 3.1 %attn_back.1 = (bf16[256,1536]{1,0:T(8,128)(2,1)S(1)}, bf16[256,1536]{1,0:T(8,128)(2,1)S(1)}) custom-call(bf16[512,384]{1,0:T(8,128)(2,1)S(1)} %get-tuple-element.145.refs_0_.refs_4_.refs_16_, bf16[512,384]{1,0:T(8,128)(2,1)S(1)} %get-tuple-element.146.refs_1_.refs_17_, bf16[512,384]{1,0:T(8,128)(2,1)S(1)} %get-tuple-element.147.refs_2_.refs_18_, ...), custom_call_target="tpu_custom_call" | custom-call | tf_op jit(solution)/shard_map/attn_back/pallas_call | solution.py:983
  170.5 10.1 %collective-permute-done.25 = bf16[384,3072]{1,0:T(8,128)(2,1)S(1)} collective-permute-done((bf16[384,3072]{1,0:T(8,128)(2,1)S(1)}, bf16[384,3072]{1,0:T(8,128)(2,1)S(1)}, u32[]{:S(2)}, u32[]{:S(2)}) %collective-permute-start.25) | collective-permute-done | bytes 2359328 | tf_op jit(solution)/shard_map/ppermute | solution.py:85
  184.0 4.1 %ffn_second.1 = (bf16[4,48,3072]{2,1,0:T(8,128)(2,1)S(1)}, bf16[4,48,3072]{2,1,0:T(8,128)(2,1)S(1)}) custom-call(s32[4]{0:T(128)S(1)} %pad_add_fusion.spot_ref.refs_0_, bf16[8,48,3072]{2,1,0:T(8,128)(2,1)} %bitcast.121, bf16[8,48,3072]{2,1,0:T(8,128)(2,1)} %bitcast.123, bf16[8,48,3072]{2,1,0:T(8,128)(2,1)} %bitcast.124, ...), custom_call_target="tpu_custom_call" | custom-call | tf_op jit(solution)/shard_map/ffn_second/pallas_call | solution.py:468
  196.2 2.9 collective-permute-start.35
  199.3 7.0 %column_chunks.3 = (bf16[768,1024]{1,0:T(8,128)(2,1)S(1)}, bf16[768,1024]{1,0:T(8,128)(2,1)S(1)}, bf16[768,1024]{1,0:T(8,128)(2,1)S(1)}) custom-call(s32[4]{0:T(128)S(1)} %pad_add_fusion.spot_ref.refs_0_, bf16[384,768]{1,0:T(8,128)(2,1)S(1)} %get-tuple-element.139.refs_21_.refs_0_, bf16[384,768]{1,0:T(8,128)(2,1)S(1)} %get-tuple-element.140.refs_1_, ...), custom_call_target="tpu_custom_call" | custom-call | flops 8000000000 | tf_op jit(solution)/shard_map/column_chunks/pallas_call | solution.py:204
  206.4 5.3 %collective-permute-done.30.refs_1_ = bf16[4,48,3072]{2,1,0:T(8,128)(2,1)S(1)} collective-permute-done((bf16[4,48,3072]{2,1,0:T(8,128)(2,1)S(1)}, bf16[4,48,3072]{2,1,0:T(8,128)(2,1)S(1)}, u32[]{:S(2)}, u32[]{:S(2)}) %collective-permute-start.30) | collective-permute-done | bytes 1179680 | tf_op jit(solution)/shard_map/ppermute | solution.py:85
  217.0 5.7 %collective-permute-done.33.refs_1_ = bf16[32,1536]{1,0:T(8,128)(2,1)S(1)} collective-permute-done((bf16[32,1536]{1,0:T(8,128)(2,1)S(1)}, bf16[32,1536]{1,0:T(8,128)(2,1)S(1)}, u32[]{:S(2)}, u32[]{:S(2)}) %collective-permute-start.33) | collective-permute-done | bytes 98336 | tf_op jit(solution)/shard_map/ppermute | solution.py:85
  224.0 5.1 %row_chunks.7 = (bf16[416,1536]{1,0:T(8,128)(2,1)S(1)}, bf16[416,1536]{1,0:T(8,128)(2,1)S(1)}, bf16[416,1536]{1,0:T(8,128)(2,1)S(1)}) custom-call(s32[4]{0:T(128)S(1)} %pad_add_fusion.spot_ref.refs_0_, bf16[32,48,512]{2,1,0:T(8,128)(2,1)S(1)} %bitcast.65, bf16[32,48,512]{2,1,0:T(8,128)(2,1)S(1)} %bitcast.66, bf16[32,48,512]{2,1,0:T(8,128)(2,1)S(1)} %bitcast.67, ...), custom_call_target="tpu_custom_call" | custom-call | flops 3000000000 | tf_op jit(solution)/shard_map/row_chunks/pallas_call | solution.py:204
  231.2 5.8 %collective-permute-done.34.refs_4_.refs_2_ = bf16[32,1536]{1,0:T(8,128)(2,1)S(1)} collective-permute-done((bf16[32,1536]{1,0:T(8,128)(2,1)S(1)}, bf16[32,1536]{1,0:T(8,128)(2,1)S(1)}, u32[]{:S(2)}, u32[]{:S(2)}) %collective-permute-start.34) | collective-permute-done | bytes 98336 | tf_op jit(solution)/shard_map/ppermute | solution.py:85
  239.5 3.6 %text_second.1 = (bf16[768,512]{1,0:T(8,128)(2,1)S(1)}, bf16[768,512]{1,0:T(8,128)(2,1)S(1)}) custom-call(s32[4]{0:T(128)S(1)} %pad_add_fusion.spot_ref.refs_0_, bf16[768,1024]{1,0:T(8,128)(2,1)} %copy-done.8, bf16[768,1024]{1,0:T(8,128)(2,1)} %copy-done.111, bf16[768,1024]{1,0:T(8,128)(2,1)} %copy-done.112, ...), custom_call_target="tpu_custom_call" | custom-call | flops 8000000000 | tf_op jit(solution)/shard_map/text_second/pallas_call | solution.py:468
  244.0 11.2 %collective-permute-done.37.refs_4_ = bf16[416,1536]{1,0:T(8,128)(2,1)S(1)} collective-permute-done((bf16[416,1536]{1,0:T(8,128)(2,1)S(1)}, bf16[416,1536]{1,0:T(8,128)(2,1)S(1)}, u32[]{:S(2)}, u32[]{:S(2)}) %collective-permute-start.37) | collective-permute-done | bytes 1277984 | tf_op jit(solution)/shard_map/ppermute | solution.py:85
  255.3 9.3 %collective-permute-done.38.refs_5_ = bf16[416,1536]{1,0:T(8,128)(2,1)S(1)} collective-permute-done((bf16[416,1536]{1,0:T(8,128)(2,1)S(1)}, bf16[416,1536]{1,0:T(8,128)(2,1)S(1)}, u32[]{:S(2)}, u32[]{:S(2)}) %collective-permute-start.38) | collective-permute-done | bytes 1277984 | tf_op jit(solution)/shard_map/ppermute | solution.py:85
  265.7 3.3 %attn_second.1 = (bf16[160,1536]{1,0:T(8,128)(2,1)S(1)}, bf16[160,1536]{1,0:T(8,128)(2,1)S(1)}, bf16[160,1536]{1,0:T(8,128)(2,1)S(1)}, bf16[160,1536]{1,0:T(8,128)(2,1)S(1)}) custom-call(s32[4]{0:T(128)S(1)} %pad_add_fusion.spot_ref.refs_0_, bf16[32,1536]{1,0:T(8,128)(2,1)} %copy-done.34, bf16[32,1536]{1,0:T(8,128)(2,1)} %copy-done.71, ...), custom_call_target="tpu_custom_call" | custom-call | tf_op jit(solution)/shard_map/attn_second/pallas_call | solution.py:468
  279.1 4.1 %collective-permute-done.41.refs_2_ = bf16[160,1536]{1,0:T(8,128)(2,1)S(1)} collective-permute-done((bf16[160,1536]{1,0:T(8,128)(2,1)S(1)}, bf16[160,1536]{1,0:T(8,128)(2,1)S(1)}, u32[]{:S(2)}, u32[]{:S(2)}) %collective-permute-start.41) | collective-permute-done | bytes 491552 | tf_op jit(solution)/shard_map/ppermute | solution.py:85
  286.1 2.3 attn_third.1
  292.7 3.1 %collective-permute-start.47 = (bf16[768,128]{1,0:T(8,128)(2,1)}, bf16[768,128]{1,0:T(8,128)(2,1)}, u32[]{:S(2)}, u32[]{:S(2)}) collective-permute-start(bf16[768,128]{1,0:T(8,128)(2,1)} %get-tuple-element.190), channel_id=1, source_target_pairs={{0,16},{1,17},{2,18},{3,19},{4,20},{5,21},{6,22},{7,23},{8,24},{9,... | collective-permute-start | bytes 589832 | tf_op jit(solution)/shard_map/ppermute | solution.py:85
  295.8 2.5 ada.1
  (370 shorter events, 104.9 us)
Async XLA Ops:
  3.9 13.7 %collective-permute-start.4 = (f32[3,1536]{1,0:T(4,128)}, f32[3,1536]{1,0:T(4,128)}, u32[]{:S(2)}, u32[]{:S(2)}) collective-permute-start(f32[3,1536]{1,0:T(4,128)} %fusion.16), channel_id=1, source_target_pairs={{0,2},{2,0},{1,3},{3,1},{4,6},{6,4},{5,7},{7,5},{8,10},{10,8},{9,1... | collective-permute-start | bytes 55304 | tf_op jit(solution)/shard_map/ppermute | solution.py:100
  4.3 18.6 %collective-permute-start.3 = (f32[3,1536]{1,0:T(4,128)}, f32[3,1536]{1,0:T(4,128)}, u32[]{:S(2)}, u32[]{:S(2)}) collective-permute-start(f32[3,1536]{1,0:T(4,128)} %fusion.16), channel_id=1, source_target_pairs={{0,1},{1,0},{2,3},{3,2},{4,5},{5,4},{6,7},{7,6},{8,9},{9,8},{10,11... | collective-permute-start | bytes 55304 | tf_op jit(solution)/shard_map/ppermute | solution.py:96
  4.3 19.5 %collective-permute-start.1 = (bf16[128,1536]{1,0:T(8,128)(2,1)S(1)}, bf16[128,1536]{1,0:T(8,128)(2,1)}, u32[]{:S(2)}, u32[]{:S(2)}) collective-permute-start(bf16[128,1536]{1,0:T(8,128)(2,1)S(1)} %copy-done.23), channel_id=1, source_target_pairs={{0,1},{1,0},{2,3},{3,2},{4,5},{5,4},{6,7},{7,6},{8,9},{9,8},{10,11... | collective-permute-start | bytes 1179656 | tf_op jit(solution)/shard_map/ppermute | solution.py:96
  4.8 12.8 %collective-permute-start = (bf16[128,1536]{1,0:T(8,128)(2,1)S(1)}, bf16[128,1536]{1,0:T(8,128)(2,1)}, u32[]{:S(2)}, u32[]{:S(2)}) collective-permute-start(bf16[128,1536]{1,0:T(8,128)(2,1)S(1)} %copy-done.23), channel_id=1, source_target_pairs={{0,2},{2,0},{1,3},{3,1},{4,6},{6,4},{5,7},{7,5},{8,10},{10,8},{9,1... | collective-permute-start | bytes 1179656 | tf_op jit(solution)/shard_map/ppermute | solution.py:100
  43.8 11.2 %collective-permute-start.7 = (bf16[128,1536]{1,0:T(8,128)(2,1)S(1)}, bf16[128,1536]{1,0:T(8,128)(2,1)S(1)}, u32[]{:S(2)}, u32[]{:S(2)}) collective-permute-start(bf16[128,1536]{1,0:T(8,128)(2,1)S(1)} %add_convert_fusion.3.rest_0_), channel_id=1, source_target_pairs={{0,2},{2,0},{1,3},{3,1},{4,6},{6,4},{5,7},{7,5},{8,10},{10,8},{9,1... | collective-permute-start | bytes 1179656 | tf_op jit(solution)/shard_map/ppermute | solution.py:100
  76.4 11.2 %collective-permute-start.12 = (bf16[128,1536]{1,0:T(8,128)(2,1)S(1)}, bf16[128,1536]{1,0:T(8,128)(2,1)S(1)}, u32[]{:S(2)}, u32[]{:S(2)}) collective-permute-start(bf16[128,1536]{1,0:T(8,128)(2,1)S(1)} %add_convert_fusion.2.rest_0_), channel_id=1, source_target_pairs={{0,2},{2,0},{1,3},{3,1},{4,6},{6,4},{5,7},{7,5},{8,10},{10,8},{9,1... | collective-permute-start | bytes 1179656 | tf_op jit(solution)/shard_map/ppermute | solution.py:100
  109.1 11.7 %collective-permute-start.17 = (bf16[128,1536]{1,0:T(8,128)(2,1)S(1)}, bf16[128,1536]{1,0:T(8,128)(2,1)}, u32[]{:S(2)}, u32[]{:S(2)}) collective-permute-start(bf16[128,1536]{1,0:T(8,128)(2,1)S(1)} %add_convert_fusion.1.rest_0_.refs_19_), channel_id=1, source_target_pairs={{0,2},{2,0},{1,3},{3,1},{4,6},{6,4},{5,7},{7,5},{8,10},{10,8},{9,1... | collective-permute-start | bytes 1179656 | tf_op jit(solution)/shard_map/ppermute | solution.py:100
  123.3 10.6 %collective-permute-start.18 = (bf16[128,1536]{1,0:T(8,128)(2,1)S(1)}, bf16[128,1536]{1,0:T(8,128)(2,1)S(1)}, u32[]{:S(2)}, u32[]{:S(2)}) collective-permute-start(bf16[128,1536]{1,0:T(8,128)(2,1)S(1)} %get-tuple-element.132), channel_id=1, source_target_pairs={{0,2},{2,0},{1,3},{3,1},{4,6},{6,4},{5,7},{7,5},{8,10},{10,8},{9,1... | collective-permute-start | bytes 1179656 | tf_op jit(solution)/shard_map/ppermute | solution.py:100
  126.0 20.2 %collective-permute-start.21 = (bf16[384,1536]{1,0:T(8,128)(2,1)S(1)}, bf16[384,1536]{1,0:T(8,128)(2,1)S(1)}, u32[]{:S(2)}, u32[]{:S(2)}) collective-permute-start(bf16[384,1536]{1,0:T(8,128)(2,1)S(1)} %get-tuple-element.141), channel_id=1, source_target_pairs={{0,32},{1,5},{2,34},{3,7},{4,36},{5,9},{6,38},{7,11},{8,40},{9,13}... | collective-permute-start | bytes 3538952 | tf_op jit(solution)/shard_map/ppermute | solution.py:85
  126.5 19.7 %collective-permute-start.22 = (bf16[384,1536]{1,0:T(8,128)(2,1)S(1)}, bf16[384,1536]{1,0:T(8,128)(2,1)S(1)}, u32[]{:S(2)}, u32[]{:S(2)}) collective-permute-start(bf16[384,1536]{1,0:T(8,128)(2,1)S(1)} %get-tuple-element.142), channel_id=1, source_target_pairs={{0,96},{1,13},{2,98},{3,15},{4,100},{5,1},{6,102},{7,3},{8,104},{9... | collective-permute-start | bytes 3538952 | tf_op jit(solution)/shard_map/ppermute | solution.py:85
  151.7 28.9 %collective-permute-start.25 = (bf16[384,3072]{1,0:T(8,128)(2,1)S(1)}, bf16[384,3072]{1,0:T(8,128)(2,1)S(1)}, u32[]{:S(2)}, u32[]{:S(2)}) collective-permute-start(bf16[384,3072]{1,0:T(8,128)(2,1)S(1)} %get-tuple-element.150), channel_id=1, source_target_pairs={{0,32},{1,5},{2,34},{3,7},{4,36},{5,9},{6,38},{7,11},{8,40},{9,13}... | collective-permute-start | bytes 7077896 | tf_op jit(solution)/shard_map/ppermute | solution.py:85
  152.3 30.2 %collective-permute-start.26 = (bf16[384,3072]{1,0:T(8,128)(2,1)S(1)}, bf16[384,3072]{1,0:T(8,128)(2,1)S(1)}, u32[]{:S(2)}, u32[]{:S(2)}) collective-permute-start(bf16[384,3072]{1,0:T(8,128)(2,1)S(1)} %get-tuple-element.151), channel_id=1, source_target_pairs={{0,96},{1,13},{2,98},{3,15},{4,100},{5,1},{6,102},{7,3},{8,104},{9... | collective-permute-start | bytes 7077896 | tf_op jit(solution)/shard_map/ppermute | solution.py:85
  167.7 28.5 %collective-permute-start.31 = (bf16[384,1024]{1,0:T(8,128)(2,1)S(1)}, bf16[384,1024]{1,0:T(8,128)(2,1)S(1)}, u32[]{:S(2)}, u32[]{:S(2)}) collective-permute-start(bf16[384,1024]{1,0:T(8,128)(2,1)S(1)} %get-tuple-element.144.refs_14_.rest_0_), channel_id=1, source_target_pairs={{0,32},{1,5},{2,34},{3,7},{4,36},{5,9},{6,38},{7,11},{8,40},{9,13}... | collective-permute-start | bytes 2359304 | tf_op jit(solution)/shard_map/ppermute | solution.py:85
  169.4 26.3 %collective-permute-start.32 = (bf16[384,1024]{1,0:T(8,128)(2,1)S(1)}, bf16[384,1024]{1,0:T(8,128)(2,1)S(1)}, u32[]{:S(2)}, u32[]{:S(2)}) collective-permute-start(bf16[384,1024]{1,0:T(8,128)(2,1)S(1)} %get-tuple-element.162), channel_id=1, source_target_pairs={{0,96},{1,13},{2,98},{3,15},{4,100},{5,1},{6,102},{7,3},{8,104},{9... | collective-permute-start | bytes 2359304 | tf_op jit(solution)/shard_map/ppermute | solution.py:85
  170.0 20.4 %collective-permute-start.24 = (bf16[128,1536]{1,0:T(8,128)(2,1)S(1)}, bf16[128,1536]{1,0:T(8,128)(2,1)S(1)}, u32[]{:S(2)}, u32[]{:S(2)}) collective-permute-start(bf16[128,1536]{1,0:T(8,128)(2,1)S(1)} %add_convert_fusion), channel_id=1, source_target_pairs={{0,2},{2,0},{1,3},{3,1},{4,6},{6,4},{5,7},{7,5},{8,10},{10,8},{9,1... | collective-permute-start | bytes 1179656 | tf_op jit(solution)/shard_map/ppermute | solution.py:100
  189.1 22.5 %collective-permute-start.30 = (bf16[4,48,3072]{2,1,0:T(8,128)(2,1)S(1)}, bf16[4,48,3072]{2,1,0:T(8,128)(2,1)S(1)}, u32[]{:S(2)}, u32[]{:S(2)}) collective-permute-start(bf16[4,48,3072]{2,1,0:T(8,128)(2,1)S(1)} %get-tuple-element.152.refs_10_), channel_id=1, source_target_pairs={{0,4},{1,33},{2,6},{3,35},{4,0},{5,37},{6,2},{7,39},{8,12},{9,41},... | collective-permute-start | bytes 3538952 | tf_op jit(solution)/shard_map/ppermute | solution.py:85
  194.0 21.3 %collective-permute-start.28 = (f32[16,1536]{1,0:T(8,128)S(1)}, f32[16,1536]{1,0:T(8,128)S(1)}, u32[]{:S(2)}, u32[]{:S(2)}) collective-permute-start(f32[16,1536]{1,0:T(8,128)S(1)} %stack_sums.1.refs_20_.refs_1_), channel_id=1, source_target_pairs={{0,1},{1,0},{2,3},{3,2},{4,5},{5,4},{6,7},{7,6},{8,9},{9,8},{10,11... | collective-permute-start | bytes 294920 | tf_op jit(solution)/shard_map/ppermute | solution.py:96
  195.7 28.3 %collective-permute-start.36 = (bf16[384,768]{1,0:T(8,128)(2,1)S(1)}, bf16[384,768]{1,0:T(8,128)(2,1)S(1)}, u32[]{:S(2)}, u32[]{:S(2)}) collective-permute-start(bf16[384,768]{1,0:T(8,128)(2,1)S(1)} %get-tuple-element.167), channel_id=1, source_target_pairs={{0,96},{1,13},{2,98},{3,15},{4,100},{5,1},{6,102},{7,3},{8,104},{9... | collective-permute-start | bytes 1769480 | tf_op jit(solution)/shard_map/ppermute | solution.py:85
  196.2 27.9 %collective-permute-start.35 = (bf16[384,768]{1,0:T(8,128)(2,1)S(1)}, bf16[384,768]{1,0:T(8,128)(2,1)S(1)}, u32[]{:S(2)}, u32[]{:S(2)}) collective-permute-start(bf16[384,768]{1,0:T(8,128)(2,1)S(1)} %get-tuple-element.164.refs_12_), channel_id=1, source_target_pairs={{0,32},{1,5},{2,34},{3,7},{4,36},{5,9},{6,38},{7,11},{8,40},{9,13}... | collective-permute-start | bytes 1769480 | tf_op jit(solution)/shard_map/ppermute | solution.py:85
  199.1 17.2 %collective-permute-start.29 = (f32[16,1536]{1,0:T(8,128)S(1)}, f32[16,1536]{1,0:T(8,128)S(1)}, u32[]{:S(2)}, u32[]{:S(2)}) collective-permute-start(f32[16,1536]{1,0:T(8,128)S(1)} %collective-permute-done.27.refs_2_), channel_id=1, source_target_pairs={{0,1},{1,0},{2,3},{3,2},{4,5},{5,4},{6,7},{7,6},{8,9},{9,8},{10,11... | collective-permute-start | bytes 294920 | tf_op jit(solution)/shard_map/ppermute | solution.py:96
  211.7 25.4 %collective-permute-start.39 = (bf16[768,1024]{1,0:T(8,128)(2,1)S(1)}, bf16[768,1024]{1,0:T(8,128)(2,1)S(1)}, u32[]{:S(2)}, u32[]{:S(2)}) collective-permute-start(bf16[768,1024]{1,0:T(8,128)(2,1)S(1)} %get-tuple-element.171), channel_id=1, source_target_pairs={{0,32},{1,5},{2,34},{3,7},{4,36},{5,9},{6,38},{7,11},{8,40},{9,13}... | collective-permute-start | bytes 4718600 | tf_op jit(solution)/shard_map/ppermute | solution.py:85
  215.3 22.7 %collective-permute-start.40 = (bf16[768,1024]{1,0:T(8,128)(2,1)S(1)}, bf16[768,1024]{1,0:T(8,128)(2,1)S(1)}, u32[]{:S(2)}, u32[]{:S(2)}) collective-permute-start(bf16[768,1024]{1,0:T(8,128)(2,1)S(1)} %get-tuple-element.172), channel_id=1, source_target_pairs={{0,96},{1,13},{2,98},{3,15},{4,100},{5,1},{6,102},{7,3},{8,104},{9... | collective-permute-start | bytes 4718600 | tf_op jit(solution)/shard_map/ppermute | solution.py:85
  222.8 14.3 %collective-permute-start.34 = (bf16[32,1536]{1,0:T(8,128)(2,1)S(1)}, bf16[32,1536]{1,0:T(8,128)(2,1)S(1)}, u32[]{:S(2)}, u32[]{:S(2)}) collective-permute-start(bf16[32,1536]{1,0:T(8,128)(2,1)S(1)} %merge.1.refs_20_.refs_1_), channel_id=1, source_target_pairs={{0,64},{1,9},{2,66},{3,11},{4,68},{5,13},{6,70},{7,15},{8,72},{9,1... | collective-permute-start | bytes 294920 | tf_op jit(solution)/shard_map/ppermute | solution.py:85
  229.2 26.1 %collective-permute-start.37 = (bf16[416,1536]{1,0:T(8,128)(2,1)S(1)}, bf16[416,1536]{1,0:T(8,128)(2,1)S(1)}, u32[]{:S(2)}, u32[]{:S(2)}) collective-permute-start(bf16[416,1536]{1,0:T(8,128)(2,1)S(1)} %get-tuple-element.169), channel_id=1, source_target_pairs={{0,32},{1,5},{2,34},{3,7},{4,36},{5,9},{6,38},{7,11},{8,40},{9,13}... | collective-permute-start | bytes 3833864 | tf_op jit(solution)/shard_map/ppermute | solution.py:85
  231.0 33.6 %collective-permute-start.38 = (bf16[416,1536]{1,0:T(8,128)(2,1)S(1)}, bf16[416,1536]{1,0:T(8,128)(2,1)S(1)}, u32[]{:S(2)}, u32[]{:S(2)}) collective-permute-start(bf16[416,1536]{1,0:T(8,128)(2,1)S(1)} %get-tuple-element.170), channel_id=1, source_target_pairs={{0,96},{1,13},{2,98},{3,15},{4,100},{5,1},{6,102},{7,3},{8,104},{9... | collective-permute-start | bytes 3833864 | tf_op jit(solution)/shard_map/ppermute | solution.py:85
  243.1 28.0 %collective-permute-start.45 = (bf16[768,512]{1,0:T(8,128)(2,1)S(1)}, bf16[768,512]{1,0:T(8,128)(2,1)S(1)}, u32[]{:S(2)}, u32[]{:S(2)}) collective-permute-start(bf16[768,512]{1,0:T(8,128)(2,1)S(1)} %get-tuple-element.173.refs_6_), channel_id=1, source_target_pairs={{0,4},{1,33},{2,6},{3,35},{4,0},{5,37},{6,2},{7,39},{8,12},{9,41},... | collective-permute-start | bytes 2359304 | tf_op jit(solution)/shard_map/ppermute | solution.py:85
  244.0 32.3 %collective-permute-start.48 = (bf16[2,48,3072]{2,1,0:T(8,128)(2,1)S(1)}, bf16[2,48,3072]{2,1,0:T(8,128)(2,1)S(1)}, u32[]{:S(2)}, u32[]{:S(2)}) collective-permute-start(bf16[2,48,3072]{2,1,0:T(8,128)(2,1)S(1)} %get-tuple-element.166.refs_8_), channel_id=1, source_target_pairs={{0,12},{1,97},{2,14},{3,99},{4,8},{5,101},{6,10},{7,103},{8,4},{9,... | collective-permute-start | bytes 1769480 | tf_op jit(solution)/shard_map/ppermute | solution.py:85
  269.0 14.2 %collective-permute-start.41 = (bf16[160,1536]{1,0:T(8,128)(2,1)S(1)}, bf16[160,1536]{1,0:T(8,128)(2,1)S(1)}, u32[]{:S(2)}, u32[]{:S(2)}) collective-permute-start(bf16[160,1536]{1,0:T(8,128)(2,1)S(1)} %get-tuple-element.175), channel_id=1, source_target_pairs={{0,4},{1,33},{2,6},{3,35},{4,8},{5,37},{6,10},{7,39},{8,12},{9,41}... | collective-permute-start | bytes 1474568 | tf_op jit(solution)/shard_map/ppermute | solution.py:85
  269.1 14.1 %collective-permute-start.42 = (bf16[160,1536]{1,0:T(8,128)(2,1)S(1)}, bf16[160,1536]{1,0:T(8,128)(2,1)S(1)}, u32[]{:S(2)}, u32[]{:S(2)}) collective-permute-start(bf16[160,1536]{1,0:T(8,128)(2,1)S(1)} %get-tuple-element.176), channel_id=1, source_target_pairs={{0,8},{1,65},{2,10},{3,67},{4,12},{5,69},{6,14},{7,71},{8,0},{9,73... | collective-permute-start | bytes 1474568 | tf_op jit(solution)/shard_map/ppermute | solution.py:85
  269.2 16.1 %collective-permute-start.43 = (bf16[160,1536]{1,0:T(8,128)(2,1)S(1)}, bf16[160,1536]{1,0:T(8,128)(2,1)S(1)}, u32[]{:S(2)}, u32[]{:S(2)}) collective-permute-start(bf16[160,1536]{1,0:T(8,128)(2,1)S(1)} %get-tuple-element.177), channel_id=1, source_target_pairs={{0,12},{1,97},{2,14},{3,99},{4,0},{5,101},{6,2},{7,103},{8,4},{9,1... | collective-permute-start | bytes 1474568 | tf_op jit(solution)/shard_map/ppermute | solution.py:85
  274.2 16.5 %collective-permute-start.46 = (bf16[768,256]{1,0:T(8,128)(2,1)S(1)}, bf16[768,256]{1,0:T(8,128)(2,1)}, u32[]{:S(2)}, u32[]{:S(2)}) collective-permute-start(bf16[768,256]{1,0:T(8,128)(2,1)S(1)} %get-tuple-element.188), channel_id=1, source_target_pairs={{0,12},{1,97},{2,14},{3,99},{4,8},{5,101},{6,10},{7,103},{8,4},{9,... | collective-permute-start | bytes 1179656 | tf_op jit(solution)/shard_map/ppermute | solution.py:85
  288.4 10.4 %collective-permute-start.44 = (bf16[48,1536]{1,0:T(8,128)(2,1)}, bf16[48,1536]{1,0:T(8,128)(2,1)}, u32[]{:S(2)}, u32[]{:S(2)}) collective-permute-start(bf16[48,1536]{1,0:T(8,128)(2,1)} %get-tuple-element.181), channel_id=1, source_target_pairs={{0,16},{1,17},{2,18},{3,19},{4,20},{5,21},{6,22},{7,23},{8,24},{9,... | collective-permute-start | bytes 442376 | tf_op jit(solution)/shard_map/ppermute | solution.py:85
  (133 other events, 865.6 us)

commit v5 on v4

--- a/solution.py
+++ b/solution.py
@@ -1207,7 +1207,7 @@
         "ffn_middle",
         -1,
         2,
-        (text_kept,),
+        (text_kept,) + tuple(attn_passed),
     )
     (riders,) = whole_call(
         pack_kernel,
@@ -1226,8 +1226,18 @@
         "merge",
     )
     opposite = dp_permute(riders, "first", 2)
+    ffn_own_kept, ffn_own_sent = tiled_call(
+        ffn_third_kernel,
+        (spot,),
+        [ffn_own, dp_permute(ffn_sent, "second", "mirror")],
+        [(shape[1:], b16)] * 2,
+        "ffn_third",
+        -1,
+        2,
+        (riders,),
+    )
     attn_one, attn_three, attn_kept = row_chunks(
-        attn_pairs, (1, 3, 0), spot, extra=attn_passed, riders=(riders,), ties=(text_kept,), micros=ATTN_MICROS
+        attn_pairs, (1, 3, 0), spot, extra=attn_passed, riders=(riders,), ties=(ffn_own_sent,), micros=ATTN_MICROS
     )
     text_rows = caption_flat.shape[1] // BLOCKS
     text_own, text_sent = tiled_call(
@@ -1250,16 +1260,6 @@
         -1,
         4,
         (text_sent,),
-    )
-    ffn_own_kept, ffn_own_sent = tiled_call(
-        ffn_third_kernel,
-        (spot,),
-        [ffn_own, dp_permute(ffn_sent, "second", "mirror")],
-        [(shape[1:], b16)] * 2,
-        "ffn_third",
-        -1,
-        2,
-        (stage[0],),
     )
     text_own, text_sent = tiled_call(
         text_middle_kernel,

time: 310 us -> 315 us (1.016)
  the two profiles are of different devices: /device:TPU:118 before, /device:TPU:0 now
where the time goes in v5:
time: 315 us; the launch traced here: 311 us
  Pallas kernels  105 us (33%)
  waiting for transfers between devices  96.8 us (31%)
  starting transfers between devices  59.2 us (19%)
  local copies, waits for them, and re-layouts  27.8 us (9%)
  matrix products  17.7 us (6%)
    ppermute x10, waiting for transfers between devices, swap_chip(): return lax.ppermute(values, 'tensor', CHIP_SWAP)  47.4 us
    ppermute x24, waiting for transfers between devices, dp_permute(): return lax.ppermute(values, ('dp', 'tensor'), dp_perm(axis, step))  42.3 us
    ppermute x24, starting transfers between devices, dp_permute(): return lax.ppermute(values, ('dp', 'tensor'), dp_perm(axis, step))  41.3 us
    unnamed x243, local copies, waits for them, and re-layouts  27.2 us
    pallas_call x3, Pallas kernels, pair_call(): pl.pallas_call(lambda *refs: kernel(*refs[:len(operands)], *refs[len(oper...  26 us
    pallas_call x6, Pallas kernels, chunk_call(): pl.pallas_call(kernel, grid_spec=pltpu.PrefetchScalarGridSpec(num_scalar_...  23.8 us
    pallas_call x9, Pallas kernels, tiled_call(): pl.pallas_call(lambda *refs: kernel(*refs[:count], *refs[count + len(ties...  22.5 us
    pallas_call x12, Pallas kernels, whole_call(): pl.pallas_call(lambda *refs: kernel(*refs[:count], *refs[count + len(ties...  17.5 us
  transfers between devices with their start and end apart: 50, of which 22 were waited for; matrix products, arithmetic and copies ran while one was open for 3% of the time, Pallas kernels for 25%

profile of v5, /device:TPU:0, one launch (start us, length us, event | category | flops | bytes accessed | tf_op | source)
XLA Modules:
  0.0 310.6 jit_solution(15697371325219041108)
XLA Ops:
  0.7 3.2 %fusion.16 = f32[3,1536]{1,0:T(4,128)} fusion(bf16[1024,1536]{1,0:T(8,128)(2,1)} %param.25, bf16[3,1024]{1,0:T(4,128)(2,1)} %param.21), kind=kOutput, calls=%fused_computation.46 | convolution fusion | flops 9455616 | bytes 3170304 | tf_op jit(solution)/shard_map/dot_general | solution.py:1031
  6.4 9.3 %text.1 = (f32[768,384]{1,0:T(8,128)S(1)}, bf16[768,384]{1,0:T(8,128)(2,1)S(1)}) custom-call(bf16[768,4096]{1,0:T(8,128)(2,1)} %bitcast.38, bf16[4096,384]{1,0:T(8,128)(2,1)} %key_weight.1, bf16[4096,384]{1,0:T(8,128)(2,1)} %value_weight.1), custom_call_target="tpu_custom_call" | custom-call | flops 8999999488 | tf_op jit(solution)/shard_map/text/pallas_call | solution.py:763
  23.9 4.9 %project.1 = (bf16[512,1536]{1,0:T(8,128)(2,1)S(1)}, f32[512,384]{1,0:T(8,128)S(1)}, f32[512,384]{1,0:T(8,128)S(1)}, bf16[512,384]{1,0:T(8,128)(2,1)S(1)}) custom-call(s32[1]{0:T(128)} %bitcast.refs_0_, bf16[128,1536]{1,0:T(8,128)(2,1)S(1)} %copy-done.23, bf16[128,1536]{1,0:T(8,128)(2,1)} %collective-permute-done.refs_2_, ...), custom_call_target="tpu_custom_call" | custom-call | flops 6000000000 | tf_op jit(solution)/shard_map/project/pallas_call | solution.py:445
  30.0 9.9 %attend.1 = (bf16[512,384]{1,0:T(8,128)(2,1)S(1)}, bf16[512,384]{1,0:T(8,128)(2,1)S(1)}, bf16[768,384]{1,0:T(8,128)(2,1)S(1)}, bf16[512,384]{1,0:T(8,128)(2,1)S(...) custom-call(f32[512,384]{1,0:T(8,128)S(1)} %get-tuple-element.109.refs_0_, ...), custom_call_target="tpu_custom_call" | custom-call | flops 11000000512 | tf_op jit(solution)/shard_map/attend/pallas_call | solution.py:655
  45.9 9.4 %collective-permute-done.7.refs_4_ = bf16[128,1536]{1,0:T(8,128)(2,1)S(1)} collective-permute-done((bf16[128,1536]{1,0:T(8,128)(2,1)S(1)}, bf16[128,1536]{1,0:T(8,128)(2,1)S(1)}, u32[]{:S(2)}, u32[]{:S(2)}) %collective-permute-start.7) | collective-permute-done | bytes 393248 | tf_op jit(solution)/shard_map/ppermute | solution.py:100
  58.0 8.8 %collective-permute-done.8 = bf16[128,1536]{1,0:T(8,128)(2,1)S(1)} collective-permute-done((bf16[128,1536]{1,0:T(8,128)(2,1)S(1)}, bf16[128,1536]{1,0:T(8,128)(2,1)S(1)}, u32[]{:S(2)}, u32[]{:S(2)}) %collective-permute-start.8) | collective-permute-done | bytes 393248 | tf_op jit(solution)/shard_map/ppermute | solution.py:100
  79.2 9.0 %collective-permute-done.12.refs_4_ = bf16[128,1536]{1,0:T(8,128)(2,1)S(1)} collective-permute-done((bf16[128,1536]{1,0:T(8,128)(2,1)S(1)}, bf16[128,1536]{1,0:T(8,128)(2,1)S(1)}, u32[]{:S(2)}, u32[]{:S(2)}) %collective-permute-start.12) | collective-permute-done | bytes 393248 | tf_op jit(solution)/shard_map/ppermute | solution.py:100
  91.2 8.8 %collective-permute-done.13 = bf16[128,1536]{1,0:T(8,128)(2,1)S(1)} collective-permute-done((bf16[128,1536]{1,0:T(8,128)(2,1)S(1)}, bf16[128,1536]{1,0:T(8,128)(2,1)S(1)}, u32[]{:S(2)}, u32[]{:S(2)}) %collective-permute-start.13) | collective-permute-done | bytes 393248 | tf_op jit(solution)/shard_map/ppermute | solution.py:100
  113.5 7.7 %collective-permute-done.17.refs_5_ = bf16[128,1536]{1,0:T(8,128)(2,1)} collective-permute-done((bf16[128,1536]{1,0:T(8,128)(2,1)S(1)}, bf16[128,1536]{1,0:T(8,128)(2,1)}, u32[]{:S(2)}, u32[]{:S(2)}) %collective-permute-start.17) | collective-permute-done | bytes 393248 | tf_op jit(solution)/shard_map/ppermute | solution.py:100
  130.8 3.6 %collective-permute-done.18 = bf16[128,1536]{1,0:T(8,128)(2,1)S(1)} collective-permute-done((bf16[128,1536]{1,0:T(8,128)(2,1)S(1)}, bf16[128,1536]{1,0:T(8,128)(2,1)S(1)}, u32[]{:S(2)}, u32[]{:S(2)}) %collective-permute-start.18) | collective-permute-done | bytes 393248 | tf_op jit(solution)/shard_map/ppermute | solution.py:100
  138.4 8.3 %cross_back.1 = (f32[512,384]{1,0:T(8,128)S(1)}, bf16[384,768]{1,0:T(8,128)(2,1)S(1)}, bf16[384,768]{1,0:T(8,128)(2,1)S(1)}, f32[1,384]{1,0:T(1,128)S(1)}, f32[1,384]{1,0:T(1,128)S(1)}) custom-call(bf16[512,384]{1,0:T(8,128)(2,1)S(1)} %copy-done.52, bf16[768,384]{1,0:T(8,128)(2,1)S(1)} %copy-done.95, bf16[768,384]{1,0:T(8,128)(2,1)S(1)} %copy-done.89, ...), custom_call_target="tpu_custom_call" | custom-call | flops 10000000000 | tf_op jit(solution)/shard_map/cross_back/pallas_call | solution.py:655
  146.7 5.5 %row_chunks.5 = (bf16[384,3072]{1,0:T(8,128)(2,1)S(1)}, bf16[384,3072]{1,0:T(8,128)(2,1)S(1)}, bf16[384,3072]{1,0:T(8,128)(2,1)S(1)}) custom-call(s32[4]{0:T(128)S(1)} %pad_add_fusion.spot_ref.refs_0_, bf16[32,48,512]{2,1,0:T(8,128)(2,1)S(1)} %bitcast.65, bf16[32,48,512]{2,1,0:T(8,128)(2,1)S(1)} %bitcast.66, bf16[32,48,512]{2,1,0:T(8,128)(2,1)S(1)} %bitcast.67, ...), custom_call_target="tpu_custom_call" | custom-call | flops 8000000000 | tf_op jit(solution)/shard_map/row_chunks/pallas_call | solution.py:204
  158.3 7.8 %self_back.1 = (bf16[512,384]{1,0:T(8,128)(2,1)S(1)}, bf16[512,384]{1,0:T(8,128)(2,1)S(1)}, bf16[512,384]{1,0:T(8,128)(2,1)S(1)}, f32[2,384]{1,0:T(2,128)S(1)}) custom-call(bf16[512,384]{1,0:T(8,128)(2,1)S(1)} %copy-done.52, bf16[512,384]{1,0:T(8,128)(2,1)S(1)} %copy-done.54, bf16[512,384]{1,0:T(8,128)(2,1)S(1)} %copy-done.50, f32[512,384]{1,0:T(8,128)S(1)} %copy-done.36, ...), custom_call_target="tpu_custom_call" | custom-call | tf_op jit(solution)/shard_map/self_back/pallas_call | solution.py:655
  166.1 3.1 %attn_back.1 = (bf16[256,1536]{1,0:T(8,128)(2,1)S(1)}, bf16[256,1536]{1,0:T(8,128)(2,1)S(1)}) custom-call(bf16[512,384]{1,0:T(8,128)(2,1)S(1)} %get-tuple-element.145.refs_0_.refs_4_.refs_16_, bf16[512,384]{1,0:T(8,128)(2,1)S(1)} %get-tuple-element.146.refs_1_.refs_17_, bf16[512,384]{1,0:T(8,128)(2,1)S(1)} %get-tuple-element.147.refs_2_.refs_18_, ...), custom_call_target="tpu_custom_call" | custom-call | tf_op jit(solution)/shard_map/attn_back/pallas_call | solution.py:983
  174.3 8.0 %collective-permute-done.25 = bf16[384,3072]{1,0:T(8,128)(2,1)S(1)} collective-permute-done((bf16[384,3072]{1,0:T(8,128)(2,1)S(1)}, bf16[384,3072]{1,0:T(8,128)(2,1)S(1)}, u32[]{:S(2)}, u32[]{:S(2)}) %collective-permute-start.25) | collective-permute-done | bytes 2359328 | tf_op jit(solution)/shard_map/ppermute | solution.py:85
  184.5 4.1 %ffn_second.1 = (bf16[4,48,3072]{2,1,0:T(8,128)(2,1)S(1)}, bf16[4,48,3072]{2,1,0:T(8,128)(2,1)S(1)}) custom-call(s32[4]{0:T(128)S(1)} %pad_add_fusion.spot_ref.refs_0_, bf16[8,48,3072]{2,1,0:T(8,128)(2,1)} %bitcast.121, bf16[8,48,3072]{2,1,0:T(8,128)(2,1)} %bitcast.123, bf16[8,48,3072]{2,1,0:T(8,128)(2,1)} %bitcast.124, ...), custom_call_target="tpu_custom_call" | custom-call | tf_op jit(solution)/shard_map/ffn_second/pallas_call | solution.py:468
  197.7 2.8 collective-permute-start.34
  200.8 7.0 %column_chunks.3 = (bf16[768,1024]{1,0:T(8,128)(2,1)S(1)}, bf16[768,1024]{1,0:T(8,128)(2,1)S(1)}, bf16[768,1024]{1,0:T(8,128)(2,1)S(1)}) custom-call(s32[4]{0:T(128)S(1)} %pad_add_fusion.spot_ref.refs_0_, bf16[384,768]{1,0:T(8,128)(2,1)S(1)} %get-tuple-element.139.refs_21_.refs_0_, bf16[384,768]{1,0:T(8,128)(2,1)S(1)} %get-tuple-element.140.refs_1_, ...), custom_call_target="tpu_custom_call" | custom-call | flops 8000000000 | tf_op jit(solution)/shard_map/column_chunks/pallas_call | solution.py:204
  207.9 2.7 collective-permute-done.34.refs_4_.refs_22_
  219.5 3.6 %collective-permute-start.35 = (bf16[32,1536]{1,0:T(8,128)(2,1)S(1)}, bf16[32,1536]{1,0:T(8,128)(2,1)S(1)}, u32[]{:S(2)}, u32[]{:S(2)}) collective-permute-start(bf16[32,1536]{1,0:T(8,128)(2,1)S(1)} %pack.1.refs_0_), channel_id=1, source_target_pairs={{0,16},{1,17},{2,18},{3,19},{4,20},{5,21},{6,22},{7,23},{8,24},{9,... | collective-permute-start | bytes 294920 | tf_op jit(solution)/shard_map/ppermute | solution.py:85
  223.1 3.6 %collective-permute-done.35.refs_1_ = bf16[32,1536]{1,0:T(8,128)(2,1)S(1)} collective-permute-done((bf16[32,1536]{1,0:T(8,128)(2,1)S(1)}, bf16[32,1536]{1,0:T(8,128)(2,1)S(1)}, u32[]{:S(2)}, u32[]{:S(2)}) %collective-permute-start.35) | collective-permute-done | bytes 98336 | tf_op jit(solution)/shard_map/ppermute | solution.py:85
  227.6 7.6 %collective-permute-done.37.refs_2_ = bf16[2,48,3072]{2,1,0:T(8,128)(2,1)S(1)} collective-permute-done((bf16[2,48,3072]{2,1,0:T(8,128)(2,1)S(1)}, bf16[2,48,3072]{2,1,0:T(8,128)(2,1)S(1)}, u32[]{:S(2)}, u32[]{:S(2)}) %collective-permute-start.37) | collective-permute-done | bytes 589856 | tf_op jit(solution)/shard_map/ppermute | solution.py:85
  237.5 5.1 %row_chunks.7 = (bf16[416,1536]{1,0:T(8,128)(2,1)S(1)}, bf16[416,1536]{1,0:T(8,128)(2,1)S(1)}, bf16[416,1536]{1,0:T(8,128)(2,1)S(1)}) custom-call(s32[4]{0:T(128)S(1)} %pad_add_fusion.spot_ref.refs_0_, bf16[32,48,512]{2,1,0:T(8,128)(2,1)S(1)} %bitcast.97, bf16[32,48,512]{2,1,0:T(8,128)(2,1)S(1)} %bitcast.98, bf16[32,48,512]{2,1,0:T(8,128)(2,1)S(1)} %bitcast.99, ...), custom_call_target="tpu_custom_call" | custom-call | flops 3000000000 | tf_op jit(solution)/shard_map/row_chunks/pallas_call | solution.py:204
  242.7 3.2 %collective-permute-start.39 = (bf16[416,1536]{1,0:T(8,128)(2,1)S(1)}, bf16[416,1536]{1,0:T(8,128)(2,1)S(1)}, u32[]{:S(2)}, u32[]{:S(2)}) collective-permute-start(bf16[416,1536]{1,0:T(8,128)(2,1)S(1)} %get-tuple-element.172), channel_id=1, source_target_pairs={{0,96},{1,13},{2,98},{3,15},{4,100},{5,1},{6,102},{7,3},{8,104},{9... | collective-permute-start | bytes 3833864 | tf_op jit(solution)/shard_map/ppermute | solution.py:85
  248.4 3.6 %text_second.1 = (bf16[768,512]{1,0:T(8,128)(2,1)S(1)}, bf16[768,512]{1,0:T(8,128)(2,1)S(1)}) custom-call(s32[4]{0:T(128)S(1)} %pad_add_fusion.spot_ref.refs_0_, bf16[768,1024]{1,0:T(8,128)(2,1)} %copy-done.22, bf16[768,1024]{1,0:T(8,128)(2,1)} %copy-done.112, bf16[768,1024]{1,0:T(8,128)(2,1)} %copy-done.113, ...), custom_call_target="tpu_custom_call" | custom-call | flops 8000000000 | tf_op jit(solution)/shard_map/text_second/pallas_call | solution.py:468
  252.1 10.8 %collective-permute-done.38.refs_4_ = bf16[416,1536]{1,0:T(8,128)(2,1)S(1)} collective-permute-done((bf16[416,1536]{1,0:T(8,128)(2,1)S(1)}, bf16[416,1536]{1,0:T(8,128)(2,1)S(1)}, u32[]{:S(2)}, u32[]{:S(2)}) %collective-permute-start.38) | collective-permute-done | bytes 1277984 | tf_op jit(solution)/shard_map/ppermute | solution.py:85
  262.8 2.9 collective-permute-done.39.refs_5_
  266.8 3.3 %attn_second.1 = (bf16[160,1536]{1,0:T(8,128)(2,1)S(1)}, bf16[160,1536]{1,0:T(8,128)(2,1)S(1)}, bf16[160,1536]{1,0:T(8,128)(2,1)S(1)}, bf16[160,1536]{1,0:T(8,128)(2,1)S(1)}) custom-call(s32[4]{0:T(128)S(1)} %pad_add_fusion.spot_ref.refs_0_, bf16[32,1536]{1,0:T(8,128)(2,1)} %copy-done.26, bf16[32,1536]{1,0:T(8,128)(2,1)} %copy-done.71, ...), custom_call_target="tpu_custom_call" | custom-call | tf_op jit(solution)/shard_map/attn_second/pallas_call | solution.py:468
  270.3 6.3 %collective-permute-start.43 = (bf16[160,1536]{1,0:T(8,128)(2,1)S(1)}, bf16[160,1536]{1,0:T(8,128)(2,1)S(1)}, u32[]{:S(2)}, u32[]{:S(2)}) collective-permute-start(bf16[160,1536]{1,0:T(8,128)(2,1)S(1)} %get-tuple-element.178), channel_id=1, source_target_pairs={{0,8},{1,65},{2,10},{3,67},{4,12},{5,69},{6,14},{7,71},{8,0},{9,73... | collective-permute-start | bytes 1474568 | tf_op jit(solution)/shard_map/ppermute | solution.py:85
  280.3 3.6 %collective-permute-start.49 = (bf16[48,3072]{1,0:T(8,128)(2,1)S(1)}, bf16[48,3072]{1,0:T(8,128)(2,1)S(1)}, u32[]{:S(2)}, u32[]{:S(2)}) collective-permute-start(bf16[48,3072]{1,0:T(8,128)(2,1)S(1)} %get-tuple-element.169.refs_23_), channel_id=1, source_target_pairs={{0,16},{1,17},{2,18},{3,19},{4,20},{5,21},{6,22},{7,23},{8,24},{9,... | collective-permute-start | bytes 884744 | tf_op jit(solution)/shard_map/ppermute | solution.py:85
  283.9 4.9 %collective-permute-done.43.refs_3_ = bf16[160,1536]{1,0:T(8,128)(2,1)S(1)} collective-permute-done((bf16[160,1536]{1,0:T(8,128)(2,1)S(1)}, bf16[160,1536]{1,0:T(8,128)(2,1)S(1)}, u32[]{:S(2)}, u32[]{:S(2)}) %collective-permute-start.43) | collective-permute-done | bytes 491552 | tf_op jit(solution)/shard_map/ppermute | solution.py:85
  292.7 3.6 %collective-permute-start.45 = (bf16[48,1536]{1,0:T(8,128)(2,1)}, bf16[48,1536]{1,0:T(8,128)(2,1)}, u32[]{:S(2)}, u32[]{:S(2)}) collective-permute-start(bf16[48,1536]{1,0:T(8,128)(2,1)} %get-tuple-element.183), channel_id=1, source_target_pairs={{0,16},{1,17},{2,18},{3,19},{4,20},{5,21},{6,22},{7,23},{8,24},{9,... | collective-permute-start | bytes 442376 | tf_op jit(solution)/shard_map/ppermute | solution.py:85
  (372 shorter events, 121.7 us)
Async XLA Ops:
  3.9 13.7 %collective-permute-start.4 = (f32[3,1536]{1,0:T(4,128)}, f32[3,1536]{1,0:T(4,128)}, u32[]{:S(2)}, u32[]{:S(2)}) collective-permute-start(f32[3,1536]{1,0:T(4,128)} %fusion.16), channel_id=1, source_target_pairs={{0,2},{2,0},{1,3},{3,1},{4,6},{6,4},{5,7},{7,5},{8,10},{10,8},{9,1... | collective-permute-start | bytes 55304 | tf_op jit(solution)/shard_map/ppermute | solution.py:100
  5.9 17.0 %collective-permute-start.3 = (f32[3,1536]{1,0:T(4,128)}, f32[3,1536]{1,0:T(4,128)}, u32[]{:S(2)}, u32[]{:S(2)}) collective-permute-start(f32[3,1536]{1,0:T(4,128)} %fusion.16), channel_id=1, source_target_pairs={{0,1},{1,0},{2,3},{3,2},{4,5},{5,4},{6,7},{7,6},{8,9},{9,8},{10,11... | collective-permute-start | bytes 55304 | tf_op jit(solution)/shard_map/ppermute | solution.py:96
  5.9 17.9 %collective-permute-start.1 = (bf16[128,1536]{1,0:T(8,128)(2,1)S(1)}, bf16[128,1536]{1,0:T(8,128)(2,1)}, u32[]{:S(2)}, u32[]{:S(2)}) collective-permute-start(bf16[128,1536]{1,0:T(8,128)(2,1)S(1)} %copy-done.23), channel_id=1, source_target_pairs={{0,1},{1,0},{2,3},{3,2},{4,5},{5,4},{6,7},{7,6},{8,9},{9,8},{10,11... | collective-permute-start | bytes 1179656 | tf_op jit(solution)/shard_map/ppermute | solution.py:96
  6.4 11.2 %collective-permute-start = (bf16[128,1536]{1,0:T(8,128)(2,1)S(1)}, bf16[128,1536]{1,0:T(8,128)(2,1)}, u32[]{:S(2)}, u32[]{:S(2)}) collective-permute-start(bf16[128,1536]{1,0:T(8,128)(2,1)S(1)} %copy-done.23), channel_id=1, source_target_pairs={{0,2},{2,0},{1,3},{3,1},{4,6},{6,4},{5,7},{7,5},{8,10},{10,8},{9,1... | collective-permute-start | bytes 1179656 | tf_op jit(solution)/shard_map/ppermute | solution.py:100
  43.8 11.5 %collective-permute-start.7 = (bf16[128,1536]{1,0:T(8,128)(2,1)S(1)}, bf16[128,1536]{1,0:T(8,128)(2,1)S(1)}, u32[]{:S(2)}, u32[]{:S(2)}) collective-permute-start(bf16[128,1536]{1,0:T(8,128)(2,1)S(1)} %add_convert_fusion.3.rest_0_), channel_id=1, source_target_pairs={{0,2},{2,0},{1,3},{3,1},{4,6},{6,4},{5,7},{7,5},{8,10},{10,8},{9,1... | collective-permute-start | bytes 1179656 | tf_op jit(solution)/shard_map/ppermute | solution.py:100
  77.0 11.2 %collective-permute-start.12 = (bf16[128,1536]{1,0:T(8,128)(2,1)S(1)}, bf16[128,1536]{1,0:T(8,128)(2,1)S(1)}, u32[]{:S(2)}, u32[]{:S(2)}) collective-permute-start(bf16[128,1536]{1,0:T(8,128)(2,1)S(1)} %add_convert_fusion.2.rest_0_), channel_id=1, source_target_pairs={{0,2},{2,0},{1,3},{3,1},{4,6},{6,4},{5,7},{7,5},{8,10},{10,8},{9,1... | collective-permute-start | bytes 1179656 | tf_op jit(solution)/shard_map/ppermute | solution.py:100
  109.7 11.6 %collective-permute-start.17 = (bf16[128,1536]{1,0:T(8,128)(2,1)S(1)}, bf16[128,1536]{1,0:T(8,128)(2,1)}, u32[]{:S(2)}, u32[]{:S(2)}) collective-permute-start(bf16[128,1536]{1,0:T(8,128)(2,1)S(1)} %add_convert_fusion.1.rest_0_.refs_19_), channel_id=1, source_target_pairs={{0,2},{2,0},{1,3},{3,1},{4,6},{6,4},{5,7},{7,5},{8,10},{10,8},{9,1... | collective-permute-start | bytes 1179656 | tf_op jit(solution)/shard_map/ppermute | solution.py:100
  127.5 19.2 %collective-permute-start.21 = (bf16[384,1536]{1,0:T(8,128)(2,1)S(1)}, bf16[384,1536]{1,0:T(8,128)(2,1)S(1)}, u32[]{:S(2)}, u32[]{:S(2)}) collective-permute-start(bf16[384,1536]{1,0:T(8,128)(2,1)S(1)} %get-tuple-element.141), channel_id=1, source_target_pairs={{0,32},{1,5},{2,34},{3,7},{4,36},{5,9},{6,38},{7,11},{8,40},{9,13}... | collective-permute-start | bytes 3538952 | tf_op jit(solution)/shard_map/ppermute | solution.py:85
  129.1 17.6 %collective-permute-start.22 = (bf16[384,1536]{1,0:T(8,128)(2,1)S(1)}, bf16[384,1536]{1,0:T(8,128)(2,1)S(1)}, u32[]{:S(2)}, u32[]{:S(2)}) collective-permute-start(bf16[384,1536]{1,0:T(8,128)(2,1)S(1)} %get-tuple-element.142), channel_id=1, source_target_pairs={{0,96},{1,13},{2,98},{3,15},{4,100},{5,1},{6,102},{7,3},{8,104},{9... | collective-permute-start | bytes 3538952 | tf_op jit(solution)/shard_map/ppermute | solution.py:85
  152.2 30.1 %collective-permute-start.25 = (bf16[384,3072]{1,0:T(8,128)(2,1)S(1)}, bf16[384,3072]{1,0:T(8,128)(2,1)S(1)}, u32[]{:S(2)}, u32[]{:S(2)}) collective-permute-start(bf16[384,3072]{1,0:T(8,128)(2,1)S(1)} %get-tuple-element.150), channel_id=1, source_target_pairs={{0,32},{1,5},{2,34},{3,7},{4,36},{5,9},{6,38},{7,11},{8,40},{9,13}... | collective-permute-start | bytes 7077896 | tf_op jit(solution)/shard_map/ppermute | solution.py:85
  153.7 29.0 %collective-permute-start.26 = (bf16[384,3072]{1,0:T(8,128)(2,1)S(1)}, bf16[384,3072]{1,0:T(8,128)(2,1)S(1)}, u32[]{:S(2)}, u32[]{:S(2)}) collective-permute-start(bf16[384,3072]{1,0:T(8,128)(2,1)S(1)} %get-tuple-element.151), channel_id=1, source_target_pairs={{0,96},{1,13},{2,98},{3,15},{4,100},{5,1},{6,102},{7,3},{8,104},{9... | collective-permute-start | bytes 7077896 | tf_op jit(solution)/shard_map/ppermute | solution.py:85
  169.4 31.1 %collective-permute-start.31 = (bf16[384,1024]{1,0:T(8,128)(2,1)S(1)}, bf16[384,1024]{1,0:T(8,128)(2,1)S(1)}, u32[]{:S(2)}, u32[]{:S(2)}) collective-permute-start(bf16[384,1024]{1,0:T(8,128)(2,1)S(1)} %get-tuple-element.144.refs_14_.rest_0_), channel_id=1, source_target_pairs={{0,32},{1,5},{2,34},{3,7},{4,36},{5,9},{6,38},{7,11},{8,40},{9,13}... | collective-permute-start | bytes 2359304 | tf_op jit(solution)/shard_map/ppermute | solution.py:85
  170.5 27.1 %collective-permute-start.32 = (bf16[384,1024]{1,0:T(8,128)(2,1)S(1)}, bf16[384,1024]{1,0:T(8,128)(2,1)S(1)}, u32[]{:S(2)}, u32[]{:S(2)}) collective-permute-start(bf16[384,1024]{1,0:T(8,128)(2,1)S(1)} %get-tuple-element.162), channel_id=1, source_target_pairs={{0,96},{1,13},{2,98},{3,15},{4,100},{5,1},{6,102},{7,3},{8,104},{9... | collective-permute-start | bytes 2359304 | tf_op jit(solution)/shard_map/ppermute | solution.py:85
  172.8 18.4 %collective-permute-start.24 = (bf16[128,1536]{1,0:T(8,128)(2,1)S(1)}, bf16[128,1536]{1,0:T(8,128)(2,1)S(1)}, u32[]{:S(2)}, u32[]{:S(2)}) collective-permute-start(bf16[128,1536]{1,0:T(8,128)(2,1)S(1)} %add_convert_fusion), channel_id=1, source_target_pairs={{0,2},{2,0},{1,3},{3,1},{4,6},{6,4},{5,7},{7,5},{8,10},{10,8},{9,1... | collective-permute-start | bytes 1179656 | tf_op jit(solution)/shard_map/ppermute | solution.py:100
  189.7 24.1 %collective-permute-start.30 = (bf16[4,48,3072]{2,1,0:T(8,128)(2,1)S(1)}, bf16[4,48,3072]{2,1,0:T(8,128)(2,1)S(1)}, u32[]{:S(2)}, u32[]{:S(2)}) collective-permute-start(bf16[4,48,3072]{2,1,0:T(8,128)(2,1)S(1)} %get-tuple-element.152.refs_10_), channel_id=1, source_target_pairs={{0,4},{1,33},{2,6},{3,35},{4,0},{5,37},{6,2},{7,39},{8,12},{9,41},... | collective-permute-start | bytes 3538952 | tf_op jit(solution)/shard_map/ppermute | solution.py:85
  195.9 23.4 %collective-permute-start.28 = (f32[16,1536]{1,0:T(8,128)S(1)}, f32[16,1536]{1,0:T(8,128)S(1)}, u32[]{:S(2)}, u32[]{:S(2)}) collective-permute-start(f32[16,1536]{1,0:T(8,128)S(1)} %stack_sums.1.refs_20_.refs_1_), channel_id=1, source_target_pairs={{0,1},{1,0},{2,3},{3,2},{4,5},{5,4},{6,7},{7,6},{8,9},{9,8},{10,11... | collective-permute-start | bytes 294920 | tf_op jit(solution)/shard_map/ppermute | solution.py:96
  197.7 12.9 %collective-permute-start.34 = (bf16[384,768]{1,0:T(8,128)(2,1)S(1)}, bf16[384,768]{1,0:T(8,128)(2,1)S(1)}, u32[]{:S(2)}, u32[]{:S(2)}) collective-permute-start(bf16[384,768]{1,0:T(8,128)(2,1)S(1)} %get-tuple-element.166), channel_id=1, source_target_pairs={{0,96},{1,13},{2,98},{3,15},{4,100},{5,1},{6,102},{7,3},{8,104},{9... | collective-permute-start | bytes 1769480 | tf_op jit(solution)/shard_map/ppermute | solution.py:85
  200.5 11.1 %collective-permute-start.33 = (bf16[384,768]{1,0:T(8,128)(2,1)S(1)}, bf16[384,768]{1,0:T(8,128)(2,1)S(1)}, u32[]{:S(2)}, u32[]{:S(2)}) collective-permute-start(bf16[384,768]{1,0:T(8,128)(2,1)S(1)} %get-tuple-element.164.refs_12_), channel_id=1, source_target_pairs={{0,32},{1,5},{2,34},{3,7},{4,36},{5,9},{6,38},{7,11},{8,40},{9,13}... | collective-permute-start | bytes 1769480 | tf_op jit(solution)/shard_map/ppermute | solution.py:85
  200.5 18.8 %collective-permute-start.29 = (f32[16,1536]{1,0:T(8,128)S(1)}, f32[16,1536]{1,0:T(8,128)S(1)}, u32[]{:S(2)}, u32[]{:S(2)}) collective-permute-start(f32[16,1536]{1,0:T(8,128)S(1)} %collective-permute-done.27.refs_2_), channel_id=1, source_target_pairs={{0,1},{1,0},{2,3},{3,2},{4,5},{5,4},{6,7},{7,6},{8,9},{9,8},{10,11... | collective-permute-start | bytes 294920 | tf_op jit(solution)/shard_map/ppermute | solution.py:96
  210.5 35.4 %collective-permute-start.40 = (bf16[768,1024]{1,0:T(8,128)(2,1)S(1)}, bf16[768,1024]{1,0:T(8,128)(2,1)S(1)}, u32[]{:S(2)}, u32[]{:S(2)}) collective-permute-start(bf16[768,1024]{1,0:T(8,128)(2,1)S(1)} %get-tuple-element.173), channel_id=1, source_target_pairs={{0,32},{1,5},{2,34},{3,7},{4,36},{5,9},{6,38},{7,11},{8,40},{9,13}... | collective-permute-start | bytes 4718600 | tf_op jit(solution)/shard_map/ppermute | solution.py:85
  211.6 34.4 %collective-permute-start.41 = (bf16[768,1024]{1,0:T(8,128)(2,1)S(1)}, bf16[768,1024]{1,0:T(8,128)(2,1)S(1)}, u32[]{:S(2)}, u32[]{:S(2)}) collective-permute-start(bf16[768,1024]{1,0:T(8,128)(2,1)S(1)} %get-tuple-element.174), channel_id=1, source_target_pairs={{0,96},{1,13},{2,98},{3,15},{4,100},{5,1},{6,102},{7,3},{8,104},{9... | collective-permute-start | bytes 4718600 | tf_op jit(solution)/shard_map/ppermute | solution.py:85
  216.6 18.6 %collective-permute-start.37 = (bf16[2,48,3072]{2,1,0:T(8,128)(2,1)S(1)}, bf16[2,48,3072]{2,1,0:T(8,128)(2,1)S(1)}, u32[]{:S(2)}, u32[]{:S(2)}) collective-permute-start(bf16[2,48,3072]{2,1,0:T(8,128)(2,1)S(1)} %get-tuple-element.167.refs_8_), channel_id=1, source_target_pairs={{0,12},{1,97},{2,14},{3,99},{4,8},{5,101},{6,10},{7,103},{8,4},{9,... | collective-permute-start | bytes 1769480 | tf_op jit(solution)/shard_map/ppermute | solution.py:85
  226.8 19.1 %collective-permute-start.36 = (bf16[32,1536]{1,0:T(8,128)(2,1)S(1)}, bf16[32,1536]{1,0:T(8,128)(2,1)S(1)}, u32[]{:S(2)}, u32[]{:S(2)}) collective-permute-start(bf16[32,1536]{1,0:T(8,128)(2,1)S(1)} %merge.1.refs_3_.refs_20_.refs_1_), channel_id=1, source_target_pairs={{0,64},{1,9},{2,66},{3,11},{4,68},{5,13},{6,70},{7,15},{8,72},{9,1... | collective-permute-start | bytes 294920 | tf_op jit(solution)/shard_map/ppermute | solution.py:85
  242.6 20.2 %collective-permute-start.38 = (bf16[416,1536]{1,0:T(8,128)(2,1)S(1)}, bf16[416,1536]{1,0:T(8,128)(2,1)S(1)}, u32[]{:S(2)}, u32[]{:S(2)}) collective-permute-start(bf16[416,1536]{1,0:T(8,128)(2,1)S(1)} %get-tuple-element.171), channel_id=1, source_target_pairs={{0,32},{1,5},{2,34},{3,7},{4,36},{5,9},{6,38},{7,11},{8,40},{9,13}... | collective-permute-start | bytes 3833864 | tf_op jit(solution)/shard_map/ppermute | solution.py:85
  242.7 23.1 %collective-permute-start.39 = (bf16[416,1536]{1,0:T(8,128)(2,1)S(1)}, bf16[416,1536]{1,0:T(8,128)(2,1)S(1)}, u32[]{:S(2)}, u32[]{:S(2)}) collective-permute-start(bf16[416,1536]{1,0:T(8,128)(2,1)S(1)} %get-tuple-element.172), channel_id=1, source_target_pairs={{0,96},{1,13},{2,98},{3,15},{4,100},{5,1},{6,102},{7,3},{8,104},{9... | collective-permute-start | bytes 3833864 | tf_op jit(solution)/shard_map/ppermute | solution.py:85
  252.0 24.6 %collective-permute-start.46 = (bf16[768,512]{1,0:T(8,128)(2,1)S(1)}, bf16[768,512]{1,0:T(8,128)(2,1)S(1)}, u32[]{:S(2)}, u32[]{:S(2)}) collective-permute-start(bf16[768,512]{1,0:T(8,128)(2,1)S(1)} %get-tuple-element.175.refs_6_), channel_id=1, source_target_pairs={{0,4},{1,33},{2,6},{3,35},{4,0},{5,37},{6,2},{7,39},{8,12},{9,41},... | collective-permute-start | bytes 2359304 | tf_op jit(solution)/shard_map/ppermute | solution.py:85
  270.2 13.7 %collective-permute-start.42 = (bf16[160,1536]{1,0:T(8,128)(2,1)S(1)}, bf16[160,1536]{1,0:T(8,128)(2,1)S(1)}, u32[]{:S(2)}, u32[]{:S(2)}) collective-permute-start(bf16[160,1536]{1,0:T(8,128)(2,1)S(1)} %get-tuple-element.177), channel_id=1, source_target_pairs={{0,4},{1,33},{2,6},{3,35},{4,8},{5,37},{6,10},{7,39},{8,12},{9,41}... | collective-permute-start | bytes 1474568 | tf_op jit(solution)/shard_map/ppermute | solution.py:85
  270.3 18.5 %collective-permute-start.43 = (bf16[160,1536]{1,0:T(8,128)(2,1)S(1)}, bf16[160,1536]{1,0:T(8,128)(2,1)S(1)}, u32[]{:S(2)}, u32[]{:S(2)}) collective-permute-start(bf16[160,1536]{1,0:T(8,128)(2,1)S(1)} %get-tuple-element.178), channel_id=1, source_target_pairs={{0,8},{1,65},{2,10},{3,67},{4,12},{5,69},{6,14},{7,71},{8,0},{9,73... | collective-permute-start | bytes 1474568 | tf_op jit(solution)/shard_map/ppermute | solution.py:85
  276.6 12.2 %collective-permute-start.44 = (bf16[160,1536]{1,0:T(8,128)(2,1)S(1)}, bf16[160,1536]{1,0:T(8,128)(2,1)S(1)}, u32[]{:S(2)}, u32[]{:S(2)}) collective-permute-start(bf16[160,1536]{1,0:T(8,128)(2,1)S(1)} %get-tuple-element.179), channel_id=1, source_target_pairs={{0,12},{1,97},{2,14},{3,99},{4,0},{5,101},{6,2},{7,103},{8,4},{9,1... | collective-permute-start | bytes 1474568 | tf_op jit(solution)/shard_map/ppermute | solution.py:85
  279.7 18.3 %collective-permute-start.47 = (bf16[768,256]{1,0:T(8,128)(2,1)S(1)}, bf16[768,256]{1,0:T(8,128)(2,1)S(1)}, u32[]{:S(2)}, u32[]{:S(2)}) collective-permute-start(bf16[768,256]{1,0:T(8,128)(2,1)S(1)} %get-tuple-element.190), channel_id=1, source_target_pairs={{0,12},{1,97},{2,14},{3,99},{4,8},{5,101},{6,10},{7,103},{8,4},{9,... | collective-permute-start | bytes 1179656 | tf_op jit(solution)/shard_map/ppermute | solution.py:85
  280.3 16.0 %collective-permute-start.49 = (bf16[48,3072]{1,0:T(8,128)(2,1)S(1)}, bf16[48,3072]{1,0:T(8,128)(2,1)S(1)}, u32[]{:S(2)}, u32[]{:S(2)}) collective-permute-start(bf16[48,3072]{1,0:T(8,128)(2,1)S(1)} %get-tuple-element.169.refs_23_), channel_id=1, source_target_pairs={{0,16},{1,17},{2,18},{3,19},{4,20},{5,21},{6,22},{7,23},{8,24},{9,... | collective-permute-start | bytes 884744 | tf_op jit(solution)/shard_map/ppermute | solution.py:85
  292.7 11.2 %collective-permute-start.45 = (bf16[48,1536]{1,0:T(8,128)(2,1)}, bf16[48,1536]{1,0:T(8,128)(2,1)}, u32[]{:S(2)}, u32[]{:S(2)}) collective-permute-start(bf16[48,1536]{1,0:T(8,128)(2,1)} %get-tuple-element.183), channel_id=1, source_target_pairs={{0,16},{1,17},{2,18},{3,19},{4,20},{5,21},{6,22},{7,23},{8,24},{9,... | collective-permute-start | bytes 442376 | tf_op jit(solution)/shard_map/ppermute | solution.py:85
  (134 other events, 863.4 us)

commit v6 on v4

--- a/solution.py
+++ b/solution.py
@@ -26,14 +26,14 @@
 
 SUM_ROWS = 6
 CROSS_MICROS = 10
-BLOCK_IN_MICROS = 0
+BLOCK_IN_MICROS = 10
 FFN_MICROS = 3
 FFN_NEXT_MICROS = 8
 MIDDLE_MICROS = 10
 SELF_MICROS = 0
 ATTN_MICROS = 3
 TEXT_MICROS = 8
-PACK_MICROS = 16
+PACK_MICROS = 0
 SECOND_MICROS = 8
 ATTN_FIRST_MICROS = 0
 
@@ -1156,6 +1156,13 @@
 
     hidden_cols = hidden.shape[1]
     block_rows = width // BLOCKS
+    upper, lower = back_call(
+        [query_grad, key_grad, value_grad], [query_weight, key_weight, value_weight], "attn_back"
+    )
+    sums, sent = scatter_tensor(upper, lower)
+    text_one, text_three, text_kept = column_chunks(
+        text_lefts, caption_flat, (1, 3, 0), spot, extra=text_passed, ties=(sent,), micros=TEXT_MICROS
+    )
     got = [by_slots(part) for part in to_neighbours(ffn_kept, ffn_one, ffn_three)]
     shape = (PAIR, block_rows, 3 * hidden_cols)
     ffn_kept, ffn_sent = tiled_call(
@@ -1166,12 +1173,8 @@
         "ffn_second",
         -1,
         4,
-        (query_grad,),
-    )
-    upper, lower = back_call(
-        [query_grad, key_grad, value_grad], [query_weight, key_weight, value_weight], "attn_back"
-    )
-    sums, sent = scatter_tensor(upper, lower)
+        (text_kept,),
+    )
     in_grad, sum_scale_attn = whole_call(
         block_in_kernel,
         (here,),
@@ -1196,9 +1199,6 @@
     (halves_two,) = row_chunks(attn_pairs, (2,), spot, ties=(stacked,), micros=ATTN_FIRST_MICROS)
     attn_passed = one_on(halves_two)
     stacked = gather_tensor(stacked)
-    text_one, text_three, text_kept = column_chunks(
-        text_lefts, caption_flat, (1, 3, 0), spot, extra=text_passed, ties=(halves_two[0],), micros=TEXT_MICROS
-    )
     ffn_own, ffn_sent = tiled_call(
         ffn_middle_kernel,
         (),

time: 310 us -> 331 us (1.068)
  the two profiles are of different devices: /device:TPU:118 before, /device:TPU:0 now
where the time goes in v6:
time: 331 us; the launch traced here: 325 us
  waiting for transfers between devices  107 us (32%)
  Pallas kernels  105 us (32%)
  starting transfers between devices  61.3 us (19%)
  local copies, waits for them, and re-layouts  29.5 us (9%)
  matrix products  17.7 us (5%)
    ppermute x24, waiting for transfers between devices, dp_permute(): return lax.ppermute(values, ('dp', 'tensor'), dp_perm(axis, step))  52.8 us
    ppermute x10, waiting for transfers between devices, swap_chip(): return lax.ppermute(values, 'tensor', CHIP_SWAP)  47.5 us
    ppermute x24, starting transfers between devices, dp_permute(): return lax.ppermute(values, ('dp', 'tensor'), dp_perm(axis, step))  43.6 us
    unnamed x241, local copies, waits for them, and re-layouts  28.9 us
    pallas_call x3, Pallas kernels, pair_call(): pl.pallas_call(lambda *refs: kernel(*refs[:len(operands)], *refs[len(oper...  26 us
    pallas_call x6, Pallas kernels, chunk_call(): pl.pallas_call(kernel, grid_spec=pltpu.PrefetchScalarGridSpec(num_scalar_...  23.7 us
    pallas_call x9, Pallas kernels, tiled_call(): pl.pallas_call(lambda *refs: kernel(*refs[:count], *refs[count + len(ties...  22.4 us
    pallas_call x12, Pallas kernels, whole_call(): pl.pallas_call(lambda *refs: kernel(*refs[:count], *refs[count + len(ties...  17.5 us
  transfers between devices with their start and end apart: 50, of which 19 were waited for; matrix products, arithmetic and copies ran while one was open for 3% of the time, Pallas kernels for 24%

profile of v6, /device:TPU:0, one launch (start us, length us, event | category | flops | bytes accessed | tf_op | source)
XLA Modules:
  0.0 325.0 jit_solution(9691870485002903311)
XLA Ops:
  0.7 3.2 fusion.16
  6.4 9.3 %text.1 = (f32[768,384]{1,0:T(8,128)S(1)}, bf16[768,384]{1,0:T(8,128)(2,1)S(1)}) custom-call(bf16[768,4096]{1,0:T(8,128)(2,1)} %bitcast.38, bf16[4096,384]{1,0:T(8,128)(2,1)} %key_weight.1, bf16[4096,384]{1,0:T(8,128)(2,1)} %value_weight.1), custom_call_target="tpu_custom_call" | custom-call | flops 8999999488 | tf_op jit(solution)/shard_map/text/pallas_call | solution.py:763
  23.9 4.9 %project.1 = (bf16[512,1536]{1,0:T(8,128)(2,1)S(1)}, f32[512,384]{1,0:T(8,128)S(1)}, f32[512,384]{1,0:T(8,128)S(1)}, bf16[512,384]{1,0:T(8,128)(2,1)S(1)}) custom-call(s32[1]{0:T(128)} %bitcast.refs_0_, bf16[128,1536]{1,0:T(8,128)(2,1)S(1)} %copy-done.54, bf16[128,1536]{1,0:T(8,128)(2,1)} %collective-permute-done.refs_2_, ...), custom_call_target="tpu_custom_call" | custom-call | flops 6000000000 | tf_op jit(solution)/shard_map/project/pallas_call | solution.py:445
  30.0 9.9 %attend.1 = (bf16[512,384]{1,0:T(8,128)(2,1)S(1)}, bf16[512,384]{1,0:T(8,128)(2,1)S(1)}, bf16[768,384]{1,0:T(8,128)(2,1)S(1)}, bf16[512,384]{1,0:T(8,128)(2,1)S(...) custom-call(f32[512,384]{1,0:T(8,128)S(1)} %get-tuple-element.109.refs_0_, ...), custom_call_target="tpu_custom_call" | custom-call | flops 11000000512 | tf_op jit(solution)/shard_map/attend/pallas_call | solution.py:655
  45.9 9.4 %collective-permute-done.7.refs_4_ = bf16[128,1536]{1,0:T(8,128)(2,1)S(1)} collective-permute-done((bf16[128,1536]{1,0:T(8,128)(2,1)S(1)}, bf16[128,1536]{1,0:T(8,128)(2,1)S(1)}, u32[]{:S(2)}, u32[]{:S(2)}) %collective-permute-start.7) | collective-permute-done | bytes 393248 | tf_op jit(solution)/shard_map/ppermute | solution.py:100
  58.0 8.8 %collective-permute-done.8 = bf16[128,1536]{1,0:T(8,128)(2,1)S(1)} collective-permute-done((bf16[128,1536]{1,0:T(8,128)(2,1)S(1)}, bf16[128,1536]{1,0:T(8,128)(2,1)S(1)}, u32[]{:S(2)}, u32[]{:S(2)}) %collective-permute-start.8) | collective-permute-done | bytes 393248 | tf_op jit(solution)/shard_map/ppermute | solution.py:100
  79.2 9.0 %collective-permute-done.12.refs_4_ = bf16[128,1536]{1,0:T(8,128)(2,1)S(1)} collective-permute-done((bf16[128,1536]{1,0:T(8,128)(2,1)S(1)}, bf16[128,1536]{1,0:T(8,128)(2,1)S(1)}, u32[]{:S(2)}, u32[]{:S(2)}) %collective-permute-start.12) | collective-permute-done | bytes 393248 | tf_op jit(solution)/shard_map/ppermute | solution.py:100
  91.2 8.8 %collective-permute-done.13 = bf16[128,1536]{1,0:T(8,128)(2,1)S(1)} collective-permute-done((bf16[128,1536]{1,0:T(8,128)(2,1)S(1)}, bf16[128,1536]{1,0:T(8,128)(2,1)S(1)}, u32[]{:S(2)}, u32[]{:S(2)}) %collective-permute-start.13) | collective-permute-done | bytes 393248 | tf_op jit(solution)/shard_map/ppermute | solution.py:100
  101.8 2.4 multiply_convert_fusion
  113.5 7.7 %collective-permute-done.17.refs_5_ = bf16[128,1536]{1,0:T(8,128)(2,1)} collective-permute-done((bf16[128,1536]{1,0:T(8,128)(2,1)S(1)}, bf16[128,1536]{1,0:T(8,128)(2,1)}, u32[]{:S(2)}, u32[]{:S(2)}) %collective-permute-start.17) | collective-permute-done | bytes 393248 | tf_op jit(solution)/shard_map/ppermute | solution.py:100
  121.4 2.5 middle_back.1
  130.8 3.6 %collective-permute-done.18 = bf16[128,1536]{1,0:T(8,128)(2,1)S(1)} collective-permute-done((bf16[128,1536]{1,0:T(8,128)(2,1)S(1)}, bf16[128,1536]{1,0:T(8,128)(2,1)S(1)}, u32[]{:S(2)}, u32[]{:S(2)}) %collective-permute-start.18) | collective-permute-done | bytes 393248 | tf_op jit(solution)/shard_map/ppermute | solution.py:100
  138.4 8.3 %cross_back.1 = (f32[512,384]{1,0:T(8,128)S(1)}, bf16[384,768]{1,0:T(8,128)(2,1)S(1)}, bf16[384,768]{1,0:T(8,128)(2,1)S(1)}, f32[1,384]{1,0:T(1,128)S(1)}, f32[1,384]{1,0:T(1,128)S(1)}) custom-call(bf16[512,384]{1,0:T(8,128)(2,1)S(1)} %copy-done.48, bf16[768,384]{1,0:T(8,128)(2,1)S(1)} %copy-done.94, bf16[768,384]{1,0:T(8,128)(2,1)S(1)} %copy-done.88, ...), custom_call_target="tpu_custom_call" | custom-call | flops 10000000000 | tf_op jit(solution)/shard_map/cross_back/pallas_call | solution.py:655
  146.7 5.5 %row_chunks.5 = (bf16[384,3072]{1,0:T(8,128)(2,1)S(1)}, bf16[384,3072]{1,0:T(8,128)(2,1)S(1)}, bf16[384,3072]{1,0:T(8,128)(2,1)S(1)}) custom-call(s32[4]{0:T(128)S(1)} %pad_add_fusion.spot_ref.refs_0_, bf16[32,48,512]{2,1,0:T(8,128)(2,1)S(1)} %bitcast.97, bf16[32,48,512]{2,1,0:T(8,128)(2,1)S(1)} %bitcast.98, bf16[32,48,512]{2,1,0:T(8,128)(2,1)S(1)} %bitcast.99, ...), custom_call_target="tpu_custom_call" | custom-call | flops 8000000000 | tf_op jit(solution)/shard_map/row_chunks/pallas_call | solution.py:204
  158.3 7.8 %self_back.1 = (bf16[512,384]{1,0:T(8,128)(2,1)S(1)}, bf16[512,384]{1,0:T(8,128)(2,1)S(1)}, bf16[512,384]{1,0:T(8,128)(2,1)S(1)}, f32[2,384]{1,0:T(2,128)S(1)}) custom-call(bf16[512,384]{1,0:T(8,128)(2,1)S(1)} %copy-done.48, bf16[512,384]{1,0:T(8,128)(2,1)S(1)} %copy-done.50, bf16[512,384]{1,0:T(8,128)(2,1)S(1)} %copy-done.46, f32[512,384]{1,0:T(8,128)S(1)} %copy-done.33, ...), custom_call_target="tpu_custom_call" | custom-call | tf_op jit(solution)/shard_map/self_back/pallas_call | solution.py:655
  166.2 3.1 attn_back.1
  173.5 17.6 %collective-permute-done.28.refs_11_ = bf16[384,1024]{1,0:T(8,128)(2,1)S(1)} collective-permute-done((bf16[384,1024]{1,0:T(8,128)(2,1)S(1)}, bf16[384,1024]{1,0:T(8,128)(2,1)S(1)}, u32[]{:S(2)}, u32[]{:S(2)}) %collective-permute-start.28) | collective-permute-done | bytes 786464 | tf_op jit(solution)/shard_map/ppermute | solution.py:85
  191.2 7.0 %column_chunks.3 = (bf16[768,1024]{1,0:T(8,128)(2,1)S(1)}, bf16[768,1024]{1,0:T(8,128)(2,1)S(1)}, bf16[768,1024]{1,0:T(8,128)(2,1)S(1)}) custom-call(s32[4]{0:T(128)S(1)} %pad_add_fusion.spot_ref.refs_0_, bf16[384,768]{1,0:T(8,128)(2,1)S(1)} %get-tuple-element.139.refs_21_.refs_0_, bf16[384,768]{1,0:T(8,128)(2,1)S(1)} %get-tuple-element.140.refs_1_, ...), custom_call_target="tpu_custom_call" | custom-call | flops 8000000000 | tf_op jit(solution)/shard_map/column_chunks/pallas_call | solution.py:204
  203.7 4.1 %ffn_second.1 = (bf16[4,48,3072]{2,1,0:T(8,128)(2,1)S(1)}, bf16[4,48,3072]{2,1,0:T(8,128)(2,1)S(1)}) custom-call(s32[4]{0:T(128)S(1)} %pad_add_fusion.spot_ref.refs_0_, bf16[8,48,3072]{2,1,0:T(8,128)(2,1)} %bitcast.121, bf16[8,48,3072]{2,1,0:T(8,128)(2,1)} %bitcast.123, bf16[8,48,3072]{2,1,0:T(8,128)(2,1)} %bitcast.124, ...), custom_call_target="tpu_custom_call" | custom-call | tf_op jit(solution)/shard_map/ffn_second/pallas_call | solution.py:468
  217.5 2.9 collective-permute-start.36
  220.4 16.6 %collective-permute-done.32.refs_1_ = bf16[4,48,3072]{2,1,0:T(8,128)(2,1)S(1)} collective-permute-done((bf16[4,48,3072]{2,1,0:T(8,128)(2,1)S(1)}, bf16[4,48,3072]{2,1,0:T(8,128)(2,1)S(1)}, u32[]{:S(2)}, u32[]{:S(2)}) %collective-permute-start.32) | collective-permute-done | bytes 1179680 | tf_op jit(solution)/shard_map/ppermute | solution.py:85
  240.9 3.6 %collective-permute-start.33 = (bf16[32,1536]{1,0:T(8,128)(2,1)S(1)}, bf16[32,1536]{1,0:T(8,128)(2,1)S(1)}, u32[]{:S(2)}, u32[]{:S(2)}) collective-permute-start(bf16[32,1536]{1,0:T(8,128)(2,1)S(1)} %pack.1.refs_0_), channel_id=1, source_target_pairs={{0,16},{1,17},{2,18},{3,19},{4,20},{5,21},{6,22},{7,23},{8,24},{9,... | collective-permute-start | bytes 294920 | tf_op jit(solution)/shard_map/ppermute | solution.py:85
  244.5 2.6 collective-permute-done.33.refs_1_
  249.5 5.1 %row_chunks.7 = (bf16[416,1536]{1,0:T(8,128)(2,1)S(1)}, bf16[416,1536]{1,0:T(8,128)(2,1)S(1)}, bf16[416,1536]{1,0:T(8,128)(2,1)S(1)}) custom-call(s32[4]{0:T(128)S(1)} %pad_add_fusion.spot_ref.refs_0_, bf16[32,48,512]{2,1,0:T(8,128)(2,1)S(1)} %bitcast.65, bf16[32,48,512]{2,1,0:T(8,128)(2,1)S(1)} %bitcast.66, bf16[32,48,512]{2,1,0:T(8,128)(2,1)S(1)} %bitcast.67, ...), custom_call_target="tpu_custom_call" | custom-call | flops 3000000000 | tf_op jit(solution)/shard_map/row_chunks/pallas_call | solution.py:204
  259.6 3.6 %text_second.1 = (bf16[768,512]{1,0:T(8,128)(2,1)S(1)}, bf16[768,512]{1,0:T(8,128)(2,1)S(1)}) custom-call(s32[4]{0:T(128)S(1)} %pad_add_fusion.spot_ref.refs_0_, bf16[768,1024]{1,0:T(8,128)(2,1)} %copy-done.2, bf16[768,1024]{1,0:T(8,128)(2,1)} %copy-done.111, bf16[768,1024]{1,0:T(8,128)(2,1)} %copy-done.112, ...), custom_call_target="tpu_custom_call" | custom-call | flops 8000000000 | tf_op jit(solution)/shard_map/text_second/pallas_call | solution.py:468
  264.5 2.7 collective-permute-start.48
  267.1 12.3 %collective-permute-done.37.refs_4_ = bf16[416,1536]{1,0:T(8,128)(2,1)S(1)} collective-permute-done((bf16[416,1536]{1,0:T(8,128)(2,1)S(1)}, bf16[416,1536]{1,0:T(8,128)(2,1)S(1)}, u32[]{:S(2)}, u32[]{:S(2)}) %collective-permute-start.37) | collective-permute-done | bytes 1277984 | tf_op jit(solution)/shard_map/ppermute | solution.py:85
  282.6 3.3 %attn_second.1 = (bf16[160,1536]{1,0:T(8,128)(2,1)S(1)}, bf16[160,1536]{1,0:T(8,128)(2,1)S(1)}, bf16[160,1536]{1,0:T(8,128)(2,1)S(1)}, bf16[160,1536]{1,0:T(8,128)(2,1)S(1)}) custom-call(s32[4]{0:T(128)S(1)} %pad_add_fusion.spot_ref.refs_0_, bf16[32,1536]{1,0:T(8,128)(2,1)} %copy-done.31, bf16[32,1536]{1,0:T(8,128)(2,1)} %copy-done.72, ...), custom_call_target="tpu_custom_call" | custom-call | tf_op jit(solution)/shard_map/attn_second/pallas_call | solution.py:468
  286.5 2.9 collective-permute-start.42
  297.1 3.6 %collective-permute-start.49 = (bf16[48,3072]{1,0:T(8,128)(2,1)S(1)}, bf16[48,3072]{1,0:T(8,128)(2,1)S(1)}, u32[]{:S(2)}, u32[]{:S(2)}) collective-permute-start(bf16[48,3072]{1,0:T(8,128)(2,1)S(1)} %get-tuple-element.197), channel_id=1, source_target_pairs={{0,16},{1,17},{2,18},{3,19},{4,20},{5,21},{6,22},{7,23},{8,24},{9,... | collective-permute-start | bytes 884744 | tf_op jit(solution)/shard_map/ppermute | solution.py:85
  305.6 3.5 %collective-permute-start.44 = (bf16[48,1536]{1,0:T(8,128)(2,1)}, bf16[48,1536]{1,0:T(8,128)(2,1)}, u32[]{:S(2)}, u32[]{:S(2)}) collective-permute-start(bf16[48,1536]{1,0:T(8,128)(2,1)} %get-tuple-element.181), channel_id=1, source_target_pairs={{0,16},{1,17},{2,18},{3,19},{4,20},{5,21},{6,22},{7,23},{8,24},{9,... | collective-permute-start | bytes 442376 | tf_op jit(solution)/shard_map/ppermute | solution.py:85
  315.7 2.5 ada.1
  (370 shorter events, 123.8 us)
Async XLA Ops:
  3.9 13.7 %collective-permute-start.4 = (f32[3,1536]{1,0:T(4,128)}, f32[3,1536]{1,0:T(4,128)}, u32[]{:S(2)}, u32[]{:S(2)}) collective-permute-start(f32[3,1536]{1,0:T(4,128)} %fusion.16), channel_id=1, source_target_pairs={{0,2},{2,0},{1,3},{3,1},{4,6},{6,4},{5,7},{7,5},{8,10},{10,8},{9,1... | collective-permute-start | bytes 55304 | tf_op jit(solution)/shard_map/ppermute | solution.py:100
  5.9 17.0 %collective-permute-start.3 = (f32[3,1536]{1,0:T(4,128)}, f32[3,1536]{1,0:T(4,128)}, u32[]{:S(2)}, u32[]{:S(2)}) collective-permute-start(f32[3,1536]{1,0:T(4,128)} %fusion.16), channel_id=1, source_target_pairs={{0,1},{1,0},{2,3},{3,2},{4,5},{5,4},{6,7},{7,6},{8,9},{9,8},{10,11... | collective-permute-start | bytes 55304 | tf_op jit(solution)/shard_map/ppermute | solution.py:96
  5.9 17.9 %collective-permute-start.1 = (bf16[128,1536]{1,0:T(8,128)(2,1)S(1)}, bf16[128,1536]{1,0:T(8,128)(2,1)}, u32[]{:S(2)}, u32[]{:S(2)}) collective-permute-start(bf16[128,1536]{1,0:T(8,128)(2,1)S(1)} %copy-done.54), channel_id=1, source_target_pairs={{0,1},{1,0},{2,3},{3,2},{4,5},{5,4},{6,7},{7,6},{8,9},{9,8},{10,11... | collective-permute-start | bytes 1179656 | tf_op jit(solution)/shard_map/ppermute | solution.py:96
  6.4 11.2 %collective-permute-start = (bf16[128,1536]{1,0:T(8,128)(2,1)S(1)}, bf16[128,1536]{1,0:T(8,128)(2,1)}, u32[]{:S(2)}, u32[]{:S(2)}) collective-permute-start(bf16[128,1536]{1,0:T(8,128)(2,1)S(1)} %copy-done.54), channel_id=1, source_target_pairs={{0,2},{2,0},{1,3},{3,1},{4,6},{6,4},{5,7},{7,5},{8,10},{10,8},{9,1... | collective-permute-start | bytes 1179656 | tf_op jit(solution)/shard_map/ppermute | solution.py:100
  43.8 11.5 %collective-permute-start.7 = (bf16[128,1536]{1,0:T(8,128)(2,1)S(1)}, bf16[128,1536]{1,0:T(8,128)(2,1)S(1)}, u32[]{:S(2)}, u32[]{:S(2)}) collective-permute-start(bf16[128,1536]{1,0:T(8,128)(2,1)S(1)} %add_convert_fusion.3.rest_0_), channel_id=1, source_target_pairs={{0,2},{2,0},{1,3},{3,1},{4,6},{6,4},{5,7},{7,5},{8,10},{10,8},{9,1... | collective-permute-start | bytes 1179656 | tf_op jit(solution)/shard_map/ppermute | solution.py:100
  56.1 10.7 %collective-permute-start.8 = (bf16[128,1536]{1,0:T(8,128)(2,1)S(1)}, bf16[128,1536]{1,0:T(8,128)(2,1)S(1)}, u32[]{:S(2)}, u32[]{:S(2)}) collective-permute-start(bf16[128,1536]{1,0:T(8,128)(2,1)S(1)} %get-tuple-element.124), channel_id=1, source_target_pairs={{0,2},{2,0},{1,3},{3,1},{4,6},{6,4},{5,7},{7,5},{8,10},{10,8},{9,1... | collective-permute-start | bytes 1179656 | tf_op jit(solution)/shard_map/ppermute | solution.py:100
  77.0 11.2 %collective-permute-start.12 = (bf16[128,1536]{1,0:T(8,128)(2,1)S(1)}, bf16[128,1536]{1,0:T(8,128)(2,1)S(1)}, u32[]{:S(2)}, u32[]{:S(2)}) collective-permute-start(bf16[128,1536]{1,0:T(8,128)(2,1)S(1)} %add_convert_fusion.2.rest_0_), channel_id=1, source_target_pairs={{0,2},{2,0},{1,3},{3,1},{4,6},{6,4},{5,7},{7,5},{8,10},{10,8},{9,1... | collective-permute-start | bytes 1179656 | tf_op jit(solution)/shard_map/ppermute | solution.py:100
  109.7 11.6 %collective-permute-start.17 = (bf16[128,1536]{1,0:T(8,128)(2,1)S(1)}, bf16[128,1536]{1,0:T(8,128)(2,1)}, u32[]{:S(2)}, u32[]{:S(2)}) collective-permute-start(bf16[128,1536]{1,0:T(8,128)(2,1)S(1)} %add_convert_fusion.1.rest_0_.refs_19_), channel_id=1, source_target_pairs={{0,2},{2,0},{1,3},{3,1},{4,6},{6,4},{5,7},{7,5},{8,10},{10,8},{9,1... | collective-permute-start | bytes 1179656 | tf_op jit(solution)/shard_map/ppermute | solution.py:100
  127.5 19.2 %collective-permute-start.21 = (bf16[384,1536]{1,0:T(8,128)(2,1)S(1)}, bf16[384,1536]{1,0:T(8,128)(2,1)S(1)}, u32[]{:S(2)}, u32[]{:S(2)}) collective-permute-start(bf16[384,1536]{1,0:T(8,128)(2,1)S(1)} %get-tuple-element.141), channel_id=1, source_target_pairs={{0,32},{1,5},{2,34},{3,7},{4,36},{5,9},{6,38},{7,11},{8,40},{9,13}... | collective-permute-start | bytes 3538952 | tf_op jit(solution)/shard_map/ppermute | solution.py:85
  129.0 17.6 %collective-permute-start.22 = (bf16[384,1536]{1,0:T(8,128)(2,1)S(1)}, bf16[384,1536]{1,0:T(8,128)(2,1)S(1)}, u32[]{:S(2)}, u32[]{:S(2)}) collective-permute-start(bf16[384,1536]{1,0:T(8,128)(2,1)S(1)} %get-tuple-element.142), channel_id=1, source_target_pairs={{0,96},{1,13},{2,98},{3,15},{4,100},{5,1},{6,102},{7,3},{8,104},{9... | collective-permute-start | bytes 3538952 | tf_op jit(solution)/shard_map/ppermute | solution.py:85
  152.3 49.2 %collective-permute-start.25 = (bf16[384,3072]{1,0:T(8,128)(2,1)S(1)}, bf16[384,3072]{1,0:T(8,128)(2,1)S(1)}, u32[]{:S(2)}, u32[]{:S(2)}) collective-permute-start(bf16[384,3072]{1,0:T(8,128)(2,1)S(1)} %get-tuple-element.150), channel_id=1, source_target_pairs={{0,32},{1,5},{2,34},{3,7},{4,36},{5,9},{6,38},{7,11},{8,40},{9,13}... | collective-permute-start | bytes 7077896 | tf_op jit(solution)/shard_map/ppermute | solution.py:85
  153.7 47.8 %collective-permute-start.26 = (bf16[384,3072]{1,0:T(8,128)(2,1)S(1)}, bf16[384,3072]{1,0:T(8,128)(2,1)S(1)}, u32[]{:S(2)}, u32[]{:S(2)}) collective-permute-start(bf16[384,3072]{1,0:T(8,128)(2,1)S(1)} %get-tuple-element.151), channel_id=1, source_target_pairs={{0,96},{1,13},{2,98},{3,15},{4,100},{5,1},{6,102},{7,3},{8,104},{9... | collective-permute-start | bytes 7077896 | tf_op jit(solution)/shard_map/ppermute | solution.py:85
  169.4 21.7 %collective-permute-start.28 = (bf16[384,1024]{1,0:T(8,128)(2,1)S(1)}, bf16[384,1024]{1,0:T(8,128)(2,1)S(1)}, u32[]{:S(2)}, u32[]{:S(2)}) collective-permute-start(bf16[384,1024]{1,0:T(8,128)(2,1)S(1)} %get-tuple-element.152), channel_id=1, source_target_pairs={{0,96},{1,13},{2,98},{3,15},{4,100},{5,1},{6,102},{7,3},{8,104},{9... | collective-permute-start | bytes 2359304 | tf_op jit(solution)/shard_map/ppermute | solution.py:85
  171.8 19.4 %collective-permute-start.27 = (bf16[384,1024]{1,0:T(8,128)(2,1)S(1)}, bf16[384,1024]{1,0:T(8,128)(2,1)S(1)}, u32[]{:S(2)}, u32[]{:S(2)}) collective-permute-start(bf16[384,1024]{1,0:T(8,128)(2,1)S(1)} %get-tuple-element.144.refs_14_.rest_0_), channel_id=1, source_target_pairs={{0,32},{1,5},{2,34},{3,7},{4,36},{5,9},{6,38},{7,11},{8,40},{9,13}... | collective-permute-start | bytes 2359304 | tf_op jit(solution)/shard_map/ppermute | solution.py:85
  171.9 38.5 %collective-permute-start.24 = (bf16[128,1536]{1,0:T(8,128)(2,1)S(1)}, bf16[128,1536]{1,0:T(8,128)(2,1)S(1)}, u32[]{:S(2)}, u32[]{:S(2)}) collective-permute-start(bf16[128,1536]{1,0:T(8,128)(2,1)S(1)} %add_convert_fusion.refs_12_), channel_id=1, source_target_pairs={{0,2},{2,0},{1,3},{3,1},{4,6},{6,4},{5,7},{7,5},{8,10},{10,8},{9,1... | collective-permute-start | bytes 1179656 | tf_op jit(solution)/shard_map/ppermute | solution.py:100
  198.2 59.7 %collective-permute-start.39 = (bf16[768,1024]{1,0:T(8,128)(2,1)S(1)}, bf16[768,1024]{1,0:T(8,128)(2,1)S(1)}, u32[]{:S(2)}, u32[]{:S(2)}) collective-permute-start(bf16[768,1024]{1,0:T(8,128)(2,1)S(1)} %get-tuple-element.171), channel_id=1, source_target_pairs={{0,32},{1,5},{2,34},{3,7},{4,36},{5,9},{6,38},{7,11},{8,40},{9,13}... | collective-permute-start | bytes 4718600 | tf_op jit(solution)/shard_map/ppermute | solution.py:85
  199.8 58.2 %collective-permute-start.40 = (bf16[768,1024]{1,0:T(8,128)(2,1)S(1)}, bf16[768,1024]{1,0:T(8,128)(2,1)S(1)}, u32[]{:S(2)}, u32[]{:S(2)}) collective-permute-start(bf16[768,1024]{1,0:T(8,128)(2,1)S(1)} %get-tuple-element.172), channel_id=1, source_target_pairs={{0,96},{1,13},{2,98},{3,15},{4,100},{5,1},{6,102},{7,3},{8,104},{9... | collective-permute-start | bytes 4718600 | tf_op jit(solution)/shard_map/ppermute | solution.py:85
  208.9 28.2 %collective-permute-start.32 = (bf16[4,48,3072]{2,1,0:T(8,128)(2,1)S(1)}, bf16[4,48,3072]{2,1,0:T(8,128)(2,1)S(1)}, u32[]{:S(2)}, u32[]{:S(2)}) collective-permute-start(bf16[4,48,3072]{2,1,0:T(8,128)(2,1)S(1)} %get-tuple-element.154.refs_10_), channel_id=1, source_target_pairs={{0,4},{1,33},{2,6},{3,35},{4,0},{5,37},{6,2},{7,39},{8,12},{9,41},... | collective-permute-start | bytes 3538952 | tf_op jit(solution)/shard_map/ppermute | solution.py:85
  217.1 32.4 %collective-permute-start.35 = (bf16[384,768]{1,0:T(8,128)(2,1)S(1)}, bf16[384,768]{1,0:T(8,128)(2,1)S(1)}, u32[]{:S(2)}, u32[]{:S(2)}) collective-permute-start(bf16[384,768]{1,0:T(8,128)(2,1)S(1)} %get-tuple-element.166), channel_id=1, source_target_pairs={{0,32},{1,5},{2,34},{3,7},{4,36},{5,9},{6,38},{7,11},{8,40},{9,13}... | collective-permute-start | bytes 1769480 | tf_op jit(solution)/shard_map/ppermute | solution.py:85
  217.5 32.0 %collective-permute-start.36 = (bf16[384,768]{1,0:T(8,128)(2,1)S(1)}, bf16[384,768]{1,0:T(8,128)(2,1)S(1)}, u32[]{:S(2)}, u32[]{:S(2)}) collective-permute-start(bf16[384,768]{1,0:T(8,128)(2,1)S(1)} %get-tuple-element.167), channel_id=1, source_target_pairs={{0,96},{1,13},{2,98},{3,15},{4,100},{5,1},{6,102},{7,3},{8,104},{9... | collective-permute-start | bytes 1769480 | tf_op jit(solution)/shard_map/ppermute | solution.py:85
  247.2 10.8 %collective-permute-start.34 = (bf16[32,1536]{1,0:T(8,128)(2,1)S(1)}, bf16[32,1536]{1,0:T(8,128)(2,1)S(1)}, u32[]{:S(2)}, u32[]{:S(2)}) collective-permute-start(bf16[32,1536]{1,0:T(8,128)(2,1)S(1)} %merge.1.refs_20_.refs_1_), channel_id=1, source_target_pairs={{0,64},{1,9},{2,66},{3,11},{4,68},{5,13},{6,70},{7,15},{8,72},{9,1... | collective-permute-start | bytes 294920 | tf_op jit(solution)/shard_map/ppermute | solution.py:85
  254.6 24.9 %collective-permute-start.37 = (bf16[416,1536]{1,0:T(8,128)(2,1)S(1)}, bf16[416,1536]{1,0:T(8,128)(2,1)S(1)}, u32[]{:S(2)}, u32[]{:S(2)}) collective-permute-start(bf16[416,1536]{1,0:T(8,128)(2,1)S(1)} %get-tuple-element.169), channel_id=1, source_target_pairs={{0,32},{1,5},{2,34},{3,7},{4,36},{5,9},{6,38},{7,11},{8,40},{9,13}... | collective-permute-start | bytes 3833864 | tf_op jit(solution)/shard_map/ppermute | solution.py:85
  255.9 25.7 %collective-permute-start.38 = (bf16[416,1536]{1,0:T(8,128)(2,1)S(1)}, bf16[416,1536]{1,0:T(8,128)(2,1)S(1)}, u32[]{:S(2)}, u32[]{:S(2)}) collective-permute-start(bf16[416,1536]{1,0:T(8,128)(2,1)S(1)} %get-tuple-element.170), channel_id=1, source_target_pairs={{0,96},{1,13},{2,98},{3,15},{4,100},{5,1},{6,102},{7,3},{8,104},{9... | collective-permute-start | bytes 3833864 | tf_op jit(solution)/shard_map/ppermute | solution.py:85
  263.3 28.5 %collective-permute-start.45 = (bf16[768,512]{1,0:T(8,128)(2,1)S(1)}, bf16[768,512]{1,0:T(8,128)(2,1)S(1)}, u32[]{:S(2)}, u32[]{:S(2)}) collective-permute-start(bf16[768,512]{1,0:T(8,128)(2,1)S(1)} %get-tuple-element.173.refs_6_), channel_id=1, source_target_pairs={{0,4},{1,33},{2,6},{3,35},{4,0},{5,37},{6,2},{7,39},{8,12},{9,41},... | collective-permute-start | bytes 2359304 | tf_op jit(solution)/shard_map/ppermute | solution.py:85
  264.5 30.4 %collective-permute-start.48 = (bf16[2,48,3072]{2,1,0:T(8,128)(2,1)S(1)}, bf16[2,48,3072]{2,1,0:T(8,128)(2,1)S(1)}, u32[]{:S(2)}, u32[]{:S(2)}) collective-permute-start(bf16[2,48,3072]{2,1,0:T(8,128)(2,1)S(1)} %get-tuple-element.164.refs_8_), channel_id=1, source_target_pairs={{0,12},{1,97},{2,14},{3,99},{4,8},{5,101},{6,10},{7,103},{8,4},{9,... | collective-permute-start | bytes 1769480 | tf_op jit(solution)/shard_map/ppermute | solution.py:85
  285.9 14.8 %collective-permute-start.41 = (bf16[160,1536]{1,0:T(8,128)(2,1)S(1)}, bf16[160,1536]{1,0:T(8,128)(2,1)S(1)}, u32[]{:S(2)}, u32[]{:S(2)}) collective-permute-start(bf16[160,1536]{1,0:T(8,128)(2,1)S(1)} %get-tuple-element.175), channel_id=1, source_target_pairs={{0,4},{1,33},{2,6},{3,35},{4,8},{5,37},{6,10},{7,39},{8,12},{9,41}... | collective-permute-start | bytes 1474568 | tf_op jit(solution)/shard_map/ppermute | solution.py:85
  286.5 15.1 %collective-permute-start.42 = (bf16[160,1536]{1,0:T(8,128)(2,1)S(1)}, bf16[160,1536]{1,0:T(8,128)(2,1)S(1)}, u32[]{:S(2)}, u32[]{:S(2)}) collective-permute-start(bf16[160,1536]{1,0:T(8,128)(2,1)S(1)} %get-tuple-element.176), channel_id=1, source_target_pairs={{0,8},{1,65},{2,10},{3,67},{4,12},{5,69},{6,14},{7,71},{8,0},{9,73... | collective-permute-start | bytes 1474568 | tf_op jit(solution)/shard_map/ppermute | solution.py:85
  289.4 12.8 %collective-permute-start.43 = (bf16[160,1536]{1,0:T(8,128)(2,1)S(1)}, bf16[160,1536]{1,0:T(8,128)(2,1)S(1)}, u32[]{:S(2)}, u32[]{:S(2)}) collective-permute-start(bf16[160,1536]{1,0:T(8,128)(2,1)S(1)} %get-tuple-element.177), channel_id=1, source_target_pairs={{0,12},{1,97},{2,14},{3,99},{4,0},{5,101},{6,2},{7,103},{8,4},{9,1... | collective-permute-start | bytes 1474568 | tf_op jit(solution)/shard_map/ppermute | solution.py:85
  294.9 14.2 %collective-permute-start.46 = (bf16[768,256]{1,0:T(8,128)(2,1)S(1)}, bf16[768,256]{1,0:T(8,128)(2,1)S(1)}, u32[]{:S(2)}, u32[]{:S(2)}) collective-permute-start(bf16[768,256]{1,0:T(8,128)(2,1)S(1)} %get-tuple-element.188), channel_id=1, source_target_pairs={{0,12},{1,97},{2,14},{3,99},{4,8},{5,101},{6,10},{7,103},{8,4},{9,... | collective-permute-start | bytes 1179656 | tf_op jit(solution)/shard_map/ppermute | solution.py:85
  297.1 14.8 %collective-permute-start.49 = (bf16[48,3072]{1,0:T(8,128)(2,1)S(1)}, bf16[48,3072]{1,0:T(8,128)(2,1)S(1)}, u32[]{:S(2)}, u32[]{:S(2)}) collective-permute-start(bf16[48,3072]{1,0:T(8,128)(2,1)S(1)} %get-tuple-element.197), channel_id=1, source_target_pairs={{0,16},{1,17},{2,18},{3,19},{4,20},{5,21},{6,22},{7,23},{8,24},{9,... | collective-permute-start | bytes 884744 | tf_op jit(solution)/shard_map/ppermute | solution.py:85
  305.6 13.2 %collective-permute-start.44 = (bf16[48,1536]{1,0:T(8,128)(2,1)}, bf16[48,1536]{1,0:T(8,128)(2,1)}, u32[]{:S(2)}, u32[]{:S(2)}) collective-permute-start(bf16[48,1536]{1,0:T(8,128)(2,1)} %get-tuple-element.181), channel_id=1, source_target_pairs={{0,16},{1,17},{2,18},{3,19},{4,20},{5,21},{6,22},{7,23},{8,24},{9,... | collective-permute-start | bytes 442376 | tf_op jit(solution)/shard_map/ppermute | solution.py:85
  311.8 11.0 %collective-permute-start.47 = (bf16[768,128]{1,0:T(8,128)(2,1)}, bf16[768,128]{1,0:T(8,128)(2,1)}, u32[]{:S(2)}, u32[]{:S(2)}) collective-permute-start(bf16[768,128]{1,0:T(8,128)(2,1)} %get-tuple-element.190), channel_id=1, source_target_pairs={{0,16},{1,17},{2,18},{3,19},{4,20},{5,21},{6,22},{7,23},{8,24},{9,... | collective-permute-start | bytes 589832 | tf_op jit(solution)/shard_map/ppermute | solution.py:85
  (133 other events, 883.6 us)

commit v7 on v4

--- a/solution.py
+++ b/solution.py
@@ -35,6 +35,7 @@
 TEXT_MICROS = 8
 PACK_MICROS = 16
 SECOND_MICROS = 8
+STAGE_MICROS = 0
 ATTN_FIRST_MICROS = 0
 
 RING = 4
@@ -1230,6 +1231,16 @@
         attn_pairs, (1, 3, 0), spot, extra=attn_passed, riders=(riders,), ties=(text_kept,), micros=ATTN_MICROS
     )
     text_rows = caption_flat.shape[1] // BLOCKS
+    stage = tiled_call(
+        functools.partial(attn_second_kernel, block_rows),
+        (spot,),
+        [riders, opposite] + to_neighbours(attn_kept, attn_one, attn_three),
+        [((PAIR * block_rows + rider_rows(4 * PAIR), width), b16)] * RING,
+        "attn_second",
+        -1,
+        4,
+        micros=STAGE_MICROS,
+    )
     text_own, text_sent = tiled_call(
         text_second_kernel,
         (spot,),
@@ -1238,18 +1249,8 @@
         "text_second",
         0,
         4,
-        (opposite,),
+        (stage[0],),
         micros=SECOND_MICROS,
-    )
-    stage = tiled_call(
-        functools.partial(attn_second_kernel, block_rows),
-        (spot,),
-        [riders, opposite] + to_neighbours(attn_kept, attn_one, attn_three),
-        [((PAIR * block_rows + rider_rows(4 * PAIR), width), b16)] * RING,
-        "attn_second",
-        -1,
-        4,
-        (text_sent,),
     )
     ffn_own_kept, ffn_own_sent = tiled_call(
         ffn_third_kernel,

time: 310 us -> 318 us (1.026)
  the two profiles are of different devices: /device:TPU:118 before, /device:TPU:0 now
where the time goes in v7:
time: 318 us; the launch traced here: 312 us
  Pallas kernels  106 us (33%)
  waiting for transfers between devices  99.2 us (31%)
  starting transfers between devices  56.6 us (18%)
  local copies, waits for them, and re-layouts  28.7 us (9%)
  matrix products  17.7 us (6%)
    ppermute x10, waiting for transfers between devices, swap_chip(): return lax.ppermute(values, 'tensor', CHIP_SWAP)  47.4 us
    ppermute x24, waiting for transfers between devices, dp_permute(): return lax.ppermute(values, ('dp', 'tensor'), dp_perm(axis, step))  44.7 us
    ppermute x24, starting transfers between devices, dp_permute(): return lax.ppermute(values, ('dp', 'tensor'), dp_perm(axis, step))  38.8 us
    unnamed x241, local copies, waits for them, and re-layouts  28.1 us
    pallas_call x3, Pallas kernels, pair_call(): pl.pallas_call(lambda *refs: kernel(*refs[:len(operands)], *refs[len(oper...  26 us
    pallas_call x6, Pallas kernels, chunk_call(): pl.pallas_call(kernel, grid_spec=pltpu.PrefetchScalarGridSpec(num_scalar_...  23.7 us
    pallas_call x9, Pallas kernels, tiled_call(): pl.pallas_call(lambda *refs: kernel(*refs[:count], *refs[count + len(ties...  23.2 us
    pallas_call x12, Pallas kernels, whole_call(): pl.pallas_call(lambda *refs: kernel(*refs[:count], *refs[count + len(ties...  17.5 us
  transfers between devices with their start and end apart: 50, of which 18 were waited for; matrix products, arithmetic and copies ran while one was open for 3% of the time, Pallas kernels for 24%

profile of v7, /device:TPU:0, one launch (start us, length us, event | category | flops | bytes accessed | tf_op | source)
XLA Modules:
  0.0 312.0 jit_solution(65948086457683917)
XLA Ops:
  0.7 3.2 %fusion.16 = f32[3,1536]{1,0:T(4,128)} fusion(bf16[1024,1536]{1,0:T(8,128)(2,1)} %param.25, bf16[3,1024]{1,0:T(4,128)(2,1)} %param.21), kind=kOutput, calls=%fused_computation.46 | convolution fusion | flops 9455616 | bytes 3170304 | tf_op jit(solution)/shard_map/dot_general | solution.py:1032
  6.4 9.3 %text.1 = (f32[768,384]{1,0:T(8,128)S(1)}, bf16[768,384]{1,0:T(8,128)(2,1)S(1)}) custom-call(bf16[768,4096]{1,0:T(8,128)(2,1)} %bitcast.38, bf16[4096,384]{1,0:T(8,128)(2,1)} %key_weight.1, bf16[4096,384]{1,0:T(8,128)(2,1)} %value_weight.1), custom_call_target="tpu_custom_call" | custom-call | flops 8999999488 | tf_op jit(solution)/shard_map/text/pallas_call | solution.py:764
  23.9 4.9 %project.1 = (bf16[512,1536]{1,0:T(8,128)(2,1)S(1)}, f32[512,384]{1,0:T(8,128)S(1)}, f32[512,384]{1,0:T(8,128)S(1)}, bf16[512,384]{1,0:T(8,128)(2,1)S(1)}) custom-call(s32[1]{0:T(128)} %bitcast.refs_0_, bf16[128,1536]{1,0:T(8,128)(2,1)S(1)} %copy-done.23, bf16[128,1536]{1,0:T(8,128)(2,1)} %collective-permute-done.refs_2_, ...), custom_call_target="tpu_custom_call" | custom-call | flops 6000000000 | tf_op jit(solution)/shard_map/project/pallas_call | solution.py:446
  30.0 9.9 %attend.1 = (bf16[512,384]{1,0:T(8,128)(2,1)S(1)}, bf16[512,384]{1,0:T(8,128)(2,1)S(1)}, bf16[768,384]{1,0:T(8,128)(2,1)S(1)}, bf16[512,384]{1,0:T(8,128)(2,1)S(...) custom-call(f32[512,384]{1,0:T(8,128)S(1)} %get-tuple-element.109.refs_0_, ...), custom_call_target="tpu_custom_call" | custom-call | flops 11000000512 | tf_op jit(solution)/shard_map/attend/pallas_call | solution.py:656
  45.9 9.4 %collective-permute-done.7.refs_4_ = bf16[128,1536]{1,0:T(8,128)(2,1)S(1)} collective-permute-done((bf16[128,1536]{1,0:T(8,128)(2,1)S(1)}, bf16[128,1536]{1,0:T(8,128)(2,1)S(1)}, u32[]{:S(2)}, u32[]{:S(2)}) %collective-permute-start.7) | collective-permute-done | bytes 393248 | tf_op jit(solution)/shard_map/ppermute | solution.py:101
  58.0 8.8 %collective-permute-done.8 = bf16[128,1536]{1,0:T(8,128)(2,1)S(1)} collective-permute-done((bf16[128,1536]{1,0:T(8,128)(2,1)S(1)}, bf16[128,1536]{1,0:T(8,128)(2,1)S(1)}, u32[]{:S(2)}, u32[]{:S(2)}) %collective-permute-start.8) | collective-permute-done | bytes 393248 | tf_op jit(solution)/shard_map/ppermute | solution.py:101
  79.2 9.0 %collective-permute-done.12.refs_4_ = bf16[128,1536]{1,0:T(8,128)(2,1)S(1)} collective-permute-done((bf16[128,1536]{1,0:T(8,128)(2,1)S(1)}, bf16[128,1536]{1,0:T(8,128)(2,1)S(1)}, u32[]{:S(2)}, u32[]{:S(2)}) %collective-permute-start.12) | collective-permute-done | bytes 393248 | tf_op jit(solution)/shard_map/ppermute | solution.py:101
  91.2 8.8 %collective-permute-done.13 = bf16[128,1536]{1,0:T(8,128)(2,1)S(1)} collective-permute-done((bf16[128,1536]{1,0:T(8,128)(2,1)S(1)}, bf16[128,1536]{1,0:T(8,128)(2,1)S(1)}, u32[]{:S(2)}, u32[]{:S(2)}) %collective-permute-start.13) | collective-permute-done | bytes 393248 | tf_op jit(solution)/shard_map/ppermute | solution.py:101
  113.5 7.7 %collective-permute-done.17.refs_5_ = bf16[128,1536]{1,0:T(8,128)(2,1)} collective-permute-done((bf16[128,1536]{1,0:T(8,128)(2,1)S(1)}, bf16[128,1536]{1,0:T(8,128)(2,1)}, u32[]{:S(2)}, u32[]{:S(2)}) %collective-permute-start.17) | collective-permute-done | bytes 393248 | tf_op jit(solution)/shard_map/ppermute | solution.py:101
  121.3 2.5 middle_back.1
  130.8 3.6 %collective-permute-done.18 = bf16[128,1536]{1,0:T(8,128)(2,1)S(1)} collective-permute-done((bf16[128,1536]{1,0:T(8,128)(2,1)S(1)}, bf16[128,1536]{1,0:T(8,128)(2,1)S(1)}, u32[]{:S(2)}, u32[]{:S(2)}) %collective-permute-start.18) | collective-permute-done | bytes 393248 | tf_op jit(solution)/shard_map/ppermute | solution.py:101
  138.4 8.3 %cross_back.1 = (f32[512,384]{1,0:T(8,128)S(1)}, bf16[384,768]{1,0:T(8,128)(2,1)S(1)}, bf16[384,768]{1,0:T(8,128)(2,1)S(1)}, f32[1,384]{1,0:T(1,128)S(1)}, f32[1,384]{1,0:T(1,128)S(1)}) custom-call(bf16[512,384]{1,0:T(8,128)(2,1)S(1)} %copy-done.52, bf16[768,384]{1,0:T(8,128)(2,1)S(1)} %copy-done.94, bf16[768,384]{1,0:T(8,128)(2,1)S(1)} %copy-done.88, ...), custom_call_target="tpu_custom_call" | custom-call | flops 10000000000 | tf_op jit(solution)/shard_map/cross_back/pallas_call | solution.py:656
  146.7 5.5 %row_chunks.5 = (bf16[384,3072]{1,0:T(8,128)(2,1)S(1)}, bf16[384,3072]{1,0:T(8,128)(2,1)S(1)}, bf16[384,3072]{1,0:T(8,128)(2,1)S(1)}) custom-call(s32[4]{0:T(128)S(1)} %pad_add_fusion.spot_ref.refs_0_, bf16[32,48,512]{2,1,0:T(8,128)(2,1)S(1)} %bitcast.97, bf16[32,48,512]{2,1,0:T(8,128)(2,1)S(1)} %bitcast.98, bf16[32,48,512]{2,1,0:T(8,128)(2,1)S(1)} %bitcast.99, ...), custom_call_target="tpu_custom_call" | custom-call | flops 8000000000 | tf_op jit(solution)/shard_map/row_chunks/pallas_call | solution.py:205
  158.3 7.8 %self_back.1 = (bf16[512,384]{1,0:T(8,128)(2,1)S(1)}, bf16[512,384]{1,0:T(8,128)(2,1)S(1)}, bf16[512,384]{1,0:T(8,128)(2,1)S(1)}, f32[2,384]{1,0:T(2,128)S(1)}) custom-call(bf16[512,384]{1,0:T(8,128)(2,1)S(1)} %copy-done.52, bf16[512,384]{1,0:T(8,128)(2,1)S(1)} %copy-done.54, bf16[512,384]{1,0:T(8,128)(2,1)S(1)} %copy-done.50, f32[512,384]{1,0:T(8,128)S(1)} %copy-done.36, ...), custom_call_target="tpu_custom_call" | custom-call | tf_op jit(solution)/shard_map/self_back/pallas_call | solution.py:656
  166.1 3.1 %attn_back.1 = (bf16[256,1536]{1,0:T(8,128)(2,1)S(1)}, bf16[256,1536]{1,0:T(8,128)(2,1)S(1)}) custom-call(bf16[512,384]{1,0:T(8,128)(2,1)S(1)} %get-tuple-element.145.refs_0_.refs_4_.refs_16_, bf16[512,384]{1,0:T(8,128)(2,1)S(1)} %get-tuple-element.146.refs_1_.refs_17_, bf16[512,384]{1,0:T(8,128)(2,1)S(1)} %get-tuple-element.147.refs_2_.refs_18_, ...), custom_call_target="tpu_custom_call" | custom-call | tf_op jit(solution)/shard_map/attn_back/pallas_call | solution.py:984
  174.3 8.0 %collective-permute-done.25 = bf16[384,3072]{1,0:T(8,128)(2,1)S(1)} collective-permute-done((bf16[384,3072]{1,0:T(8,128)(2,1)S(1)}, bf16[384,3072]{1,0:T(8,128)(2,1)S(1)}, u32[]{:S(2)}, u32[]{:S(2)}) %collective-permute-start.25) | collective-permute-done | bytes 2359328 | tf_op jit(solution)/shard_map/ppermute | solution.py:86
  184.5 4.1 %ffn_second.1 = (bf16[4,48,3072]{2,1,0:T(8,128)(2,1)S(1)}, bf16[4,48,3072]{2,1,0:T(8,128)(2,1)S(1)}) custom-call(s32[4]{0:T(128)S(1)} %pad_add_fusion.spot_ref.refs_0_, bf16[8,48,3072]{2,1,0:T(8,128)(2,1)} %bitcast.121, bf16[8,48,3072]{2,1,0:T(8,128)(2,1)} %bitcast.123, bf16[8,48,3072]{2,1,0:T(8,128)(2,1)} %bitcast.124, ...), custom_call_target="tpu_custom_call" | custom-call | tf_op jit(solution)/shard_map/ffn_second/pallas_call | solution.py:469
  197.7 2.8 collective-permute-start.36
  200.8 7.0 %column_chunks.3 = (bf16[768,1024]{1,0:T(8,128)(2,1)S(1)}, bf16[768,1024]{1,0:T(8,128)(2,1)S(1)}, bf16[768,1024]{1,0:T(8,128)(2,1)S(1)}) custom-call(s32[4]{0:T(128)S(1)} %pad_add_fusion.spot_ref.refs_0_, bf16[384,768]{1,0:T(8,128)(2,1)S(1)} %get-tuple-element.139.refs_21_.refs_0_, bf16[384,768]{1,0:T(8,128)(2,1)S(1)} %get-tuple-element.140.refs_1_, ...), custom_call_target="tpu_custom_call" | custom-call | flops 8000000000 | tf_op jit(solution)/shard_map/column_chunks/pallas_call | solution.py:205
  207.9 3.1 collective-permute-done.30.refs_1_
  214.7 3.4 %collective-permute-start.33 = (bf16[32,1536]{1,0:T(8,128)(2,1)S(1)}, bf16[32,1536]{1,0:T(8,128)(2,1)S(1)}, u32[]{:S(2)}, u32[]{:S(2)}) collective-permute-start(bf16[32,1536]{1,0:T(8,128)(2,1)S(1)} %pack.1.refs_0_), channel_id=1, source_target_pairs={{0,16},{1,17},{2,18},{3,19},{4,20},{5,21},{6,22},{7,23},{8,24},{9,... | collective-permute-start | bytes 294920 | tf_op jit(solution)/shard_map/ppermute | solution.py:86
  221.4 5.1 %row_chunks.7 = (bf16[416,1536]{1,0:T(8,128)(2,1)S(1)}, bf16[416,1536]{1,0:T(8,128)(2,1)S(1)}, bf16[416,1536]{1,0:T(8,128)(2,1)S(1)}) custom-call(s32[4]{0:T(128)S(1)} %pad_add_fusion.spot_ref.refs_0_, bf16[32,48,512]{2,1,0:T(8,128)(2,1)S(1)} %bitcast.65, bf16[32,48,512]{2,1,0:T(8,128)(2,1)S(1)} %bitcast.66, bf16[32,48,512]{2,1,0:T(8,128)(2,1)S(1)} %bitcast.67, ...), custom_call_target="tpu_custom_call" | custom-call | flops 3000000000 | tf_op jit(solution)/shard_map/row_chunks/pallas_call | solution.py:205
  228.2 2.6 collective-permute-start.38
  231.6 23.8 %collective-permute-done.34.refs_2_ = bf16[32,1536]{1,0:T(8,128)(2,1)S(1)} collective-permute-done((bf16[32,1536]{1,0:T(8,128)(2,1)S(1)}, bf16[32,1536]{1,0:T(8,128)(2,1)S(1)}, u32[]{:S(2)}, u32[]{:S(2)}) %collective-permute-start.34) | collective-permute-done | bytes 98336 | tf_op jit(solution)/shard_map/ppermute | solution.py:86
  257.0 3.3 %attn_second.1 = (bf16[160,1536]{1,0:T(8,128)(2,1)S(1)}, bf16[160,1536]{1,0:T(8,128)(2,1)S(1)}, bf16[160,1536]{1,0:T(8,128)(2,1)S(1)}, bf16[160,1536]{1,0:T(8,128)(2,1)S(1)}) custom-call(s32[4]{0:T(128)S(1)} %pad_add_fusion.spot_ref.refs_0_, bf16[32,1536]{1,0:T(8,128)(2,1)} %copy-done.34, bf16[32,1536]{1,0:T(8,128)(2,1)} %copy-done.109, ...), custom_call_target="tpu_custom_call" | custom-call | tf_op jit(solution)/shard_map/attn_second/pallas_call | solution.py:469
  262.1 3.6 %text_second.1 = (bf16[768,512]{1,0:T(8,128)(2,1)S(1)}, bf16[768,512]{1,0:T(8,128)(2,1)S(1)}) custom-call(s32[4]{0:T(128)S(1)} %pad_add_fusion.spot_ref.refs_0_, bf16[768,1024]{1,0:T(8,128)(2,1)} %copy-done.8, bf16[768,1024]{1,0:T(8,128)(2,1)} %copy-done.111, bf16[768,1024]{1,0:T(8,128)(2,1)} %copy-done.112, ...), custom_call_target="tpu_custom_call" | custom-call | flops 8000000000 | tf_op jit(solution)/shard_map/text_second/pallas_call | solution.py:469
  267.5 3.1 collective-permute-start.48
  273.8 4.7 %collective-permute-done.45.refs_1_ = bf16[768,512]{1,0:T(8,128)(2,1)S(1)} collective-permute-done((bf16[768,512]{1,0:T(8,128)(2,1)S(1)}, bf16[768,512]{1,0:T(8,128)(2,1)S(1)}, u32[]{:S(2)}, u32[]{:S(2)}) %collective-permute-start.45) | collective-permute-done | bytes 786464 | tf_op jit(solution)/shard_map/ppermute | solution.py:86
  281.6 2.8 collective-permute-start.46
  286.8 4.7 %collective-permute-done.40.refs_3_ = bf16[160,1536]{1,0:T(8,128)(2,1)S(1)} collective-permute-done((bf16[160,1536]{1,0:T(8,128)(2,1)S(1)}, bf16[160,1536]{1,0:T(8,128)(2,1)S(1)}, u32[]{:S(2)}, u32[]{:S(2)}) %collective-permute-start.40) | collective-permute-done | bytes 491552 | tf_op jit(solution)/shard_map/ppermute | solution.py:86
  297.2 2.7 ada.1
  301.8 3.4 %collective-permute-start.47 = (bf16[768,128]{1,0:T(8,128)(2,1)}, bf16[768,128]{1,0:T(8,128)(2,1)}, u32[]{:S(2)}, u32[]{:S(2)}) collective-permute-start(bf16[768,128]{1,0:T(8,128)(2,1)} %get-tuple-element.190), channel_id=1, source_target_pairs={{0,16},{1,17},{2,18},{3,19},{4,20},{5,21},{6,22},{7,23},{8,24},{9,... | collective-permute-start | bytes 589832 | tf_op jit(solution)/shard_map/ppermute | solution.py:86
  (370 shorter events, 119.2 us)
Async XLA Ops:
  3.9 13.7 %collective-permute-start.4 = (f32[3,1536]{1,0:T(4,128)}, f32[3,1536]{1,0:T(4,128)}, u32[]{:S(2)}, u32[]{:S(2)}) collective-permute-start(f32[3,1536]{1,0:T(4,128)} %fusion.16), channel_id=1, source_target_pairs={{0,2},{2,0},{1,3},{3,1},{4,6},{6,4},{5,7},{7,5},{8,10},{10,8},{9,1... | collective-permute-start | bytes 55304 | tf_op jit(solution)/shard_map/ppermute | solution.py:101
  5.9 17.0 %collective-permute-start.3 = (f32[3,1536]{1,0:T(4,128)}, f32[3,1536]{1,0:T(4,128)}, u32[]{:S(2)}, u32[]{:S(2)}) collective-permute-start(f32[3,1536]{1,0:T(4,128)} %fusion.16), channel_id=1, source_target_pairs={{0,1},{1,0},{2,3},{3,2},{4,5},{5,4},{6,7},{7,6},{8,9},{9,8},{10,11... | collective-permute-start | bytes 55304 | tf_op jit(solution)/shard_map/ppermute | solution.py:97
  5.9 17.9 %collective-permute-start.1 = (bf16[128,1536]{1,0:T(8,128)(2,1)S(1)}, bf16[128,1536]{1,0:T(8,128)(2,1)}, u32[]{:S(2)}, u32[]{:S(2)}) collective-permute-start(bf16[128,1536]{1,0:T(8,128)(2,1)S(1)} %copy-done.23), channel_id=1, source_target_pairs={{0,1},{1,0},{2,3},{3,2},{4,5},{5,4},{6,7},{7,6},{8,9},{9,8},{10,11... | collective-permute-start | bytes 1179656 | tf_op jit(solution)/shard_map/ppermute | solution.py:97
  6.4 11.2 %collective-permute-start = (bf16[128,1536]{1,0:T(8,128)(2,1)S(1)}, bf16[128,1536]{1,0:T(8,128)(2,1)}, u32[]{:S(2)}, u32[]{:S(2)}) collective-permute-start(bf16[128,1536]{1,0:T(8,128)(2,1)S(1)} %copy-done.23), channel_id=1, source_target_pairs={{0,2},{2,0},{1,3},{3,1},{4,6},{6,4},{5,7},{7,5},{8,10},{10,8},{9,1... | collective-permute-start | bytes 1179656 | tf_op jit(solution)/shard_map/ppermute | solution.py:101
  43.8 11.5 %collective-permute-start.7 = (bf16[128,1536]{1,0:T(8,128)(2,1)S(1)}, bf16[128,1536]{1,0:T(8,128)(2,1)S(1)}, u32[]{:S(2)}, u32[]{:S(2)}) collective-permute-start(bf16[128,1536]{1,0:T(8,128)(2,1)S(1)} %add_convert_fusion.3.rest_0_), channel_id=1, source_target_pairs={{0,2},{2,0},{1,3},{3,1},{4,6},{6,4},{5,7},{7,5},{8,10},{10,8},{9,1... | collective-permute-start | bytes 1179656 | tf_op jit(solution)/shard_map/ppermute | solution.py:101
  56.1 10.7 %collective-permute-start.8 = (bf16[128,1536]{1,0:T(8,128)(2,1)S(1)}, bf16[128,1536]{1,0:T(8,128)(2,1)S(1)}, u32[]{:S(2)}, u32[]{:S(2)}) collective-permute-start(bf16[128,1536]{1,0:T(8,128)(2,1)S(1)} %get-tuple-element.124), channel_id=1, source_target_pairs={{0,2},{2,0},{1,3},{3,1},{4,6},{6,4},{5,7},{7,5},{8,10},{10,8},{9,1... | collective-permute-start | bytes 1179656 | tf_op jit(solution)/shard_map/ppermute | solution.py:101
  77.0 11.2 %collective-permute-start.12 = (bf16[128,1536]{1,0:T(8,128)(2,1)S(1)}, bf16[128,1536]{1,0:T(8,128)(2,1)S(1)}, u32[]{:S(2)}, u32[]{:S(2)}) collective-permute-start(bf16[128,1536]{1,0:T(8,128)(2,1)S(1)} %add_convert_fusion.2.rest_0_), channel_id=1, source_target_pairs={{0,2},{2,0},{1,3},{3,1},{4,6},{6,4},{5,7},{7,5},{8,10},{10,8},{9,1... | collective-permute-start | bytes 1179656 | tf_op jit(solution)/shard_map/ppermute | solution.py:101
  109.7 11.6 %collective-permute-start.17 = (bf16[128,1536]{1,0:T(8,128)(2,1)S(1)}, bf16[128,1536]{1,0:T(8,128)(2,1)}, u32[]{:S(2)}, u32[]{:S(2)}) collective-permute-start(bf16[128,1536]{1,0:T(8,128)(2,1)S(1)} %add_convert_fusion.1.rest_0_.refs_19_), channel_id=1, source_target_pairs={{0,2},{2,0},{1,3},{3,1},{4,6},{6,4},{5,7},{7,5},{8,10},{10,8},{9,1... | collective-permute-start | bytes 1179656 | tf_op jit(solution)/shard_map/ppermute | solution.py:101
  123.8 10.6 %collective-permute-start.18 = (bf16[128,1536]{1,0:T(8,128)(2,1)S(1)}, bf16[128,1536]{1,0:T(8,128)(2,1)S(1)}, u32[]{:S(2)}, u32[]{:S(2)}) collective-permute-start(bf16[128,1536]{1,0:T(8,128)(2,1)S(1)} %get-tuple-element.132), channel_id=1, source_target_pairs={{0,2},{2,0},{1,3},{3,1},{4,6},{6,4},{5,7},{7,5},{8,10},{10,8},{9,1... | collective-permute-start | bytes 1179656 | tf_op jit(solution)/shard_map/ppermute | solution.py:101
  127.5 19.2 %collective-permute-start.21 = (bf16[384,1536]{1,0:T(8,128)(2,1)S(1)}, bf16[384,1536]{1,0:T(8,128)(2,1)S(1)}, u32[]{:S(2)}, u32[]{:S(2)}) collective-permute-start(bf16[384,1536]{1,0:T(8,128)(2,1)S(1)} %get-tuple-element.141), channel_id=1, source_target_pairs={{0,32},{1,5},{2,34},{3,7},{4,36},{5,9},{6,38},{7,11},{8,40},{9,13}... | collective-permute-start | bytes 3538952 | tf_op jit(solution)/shard_map/ppermute | solution.py:86
  129.0 17.6 %collective-permute-start.22 = (bf16[384,1536]{1,0:T(8,128)(2,1)S(1)}, bf16[384,1536]{1,0:T(8,128)(2,1)S(1)}, u32[]{:S(2)}, u32[]{:S(2)}) collective-permute-start(bf16[384,1536]{1,0:T(8,128)(2,1)S(1)} %get-tuple-element.142), channel_id=1, source_target_pairs={{0,96},{1,13},{2,98},{3,15},{4,100},{5,1},{6,102},{7,3},{8,104},{9... | collective-permute-start | bytes 3538952 | tf_op jit(solution)/shard_map/ppermute | solution.py:86
  152.2 30.1 %collective-permute-start.25 = (bf16[384,3072]{1,0:T(8,128)(2,1)S(1)}, bf16[384,3072]{1,0:T(8,128)(2,1)S(1)}, u32[]{:S(2)}, u32[]{:S(2)}) collective-permute-start(bf16[384,3072]{1,0:T(8,128)(2,1)S(1)} %get-tuple-element.150), channel_id=1, source_target_pairs={{0,32},{1,5},{2,34},{3,7},{4,36},{5,9},{6,38},{7,11},{8,40},{9,13}... | collective-permute-start | bytes 7077896 | tf_op jit(solution)/shard_map/ppermute | solution.py:86
  153.7 29.0 %collective-permute-start.26 = (bf16[384,3072]{1,0:T(8,128)(2,1)S(1)}, bf16[384,3072]{1,0:T(8,128)(2,1)S(1)}, u32[]{:S(2)}, u32[]{:S(2)}) collective-permute-start(bf16[384,3072]{1,0:T(8,128)(2,1)S(1)} %get-tuple-element.151), channel_id=1, source_target_pairs={{0,96},{1,13},{2,98},{3,15},{4,100},{5,1},{6,102},{7,3},{8,104},{9... | collective-permute-start | bytes 7077896 | tf_op jit(solution)/shard_map/ppermute | solution.py:86
  169.4 31.1 %collective-permute-start.31 = (bf16[384,1024]{1,0:T(8,128)(2,1)S(1)}, bf16[384,1024]{1,0:T(8,128)(2,1)S(1)}, u32[]{:S(2)}, u32[]{:S(2)}) collective-permute-start(bf16[384,1024]{1,0:T(8,128)(2,1)S(1)} %get-tuple-element.144.refs_14_.rest_0_), channel_id=1, source_target_pairs={{0,32},{1,5},{2,34},{3,7},{4,36},{5,9},{6,38},{7,11},{8,40},{9,13}... | collective-permute-start | bytes 2359304 | tf_op jit(solution)/shard_map/ppermute | solution.py:86
  170.5 27.1 %collective-permute-start.32 = (bf16[384,1024]{1,0:T(8,128)(2,1)S(1)}, bf16[384,1024]{1,0:T(8,128)(2,1)S(1)}, u32[]{:S(2)}, u32[]{:S(2)}) collective-permute-start(bf16[384,1024]{1,0:T(8,128)(2,1)S(1)} %get-tuple-element.162), channel_id=1, source_target_pairs={{0,96},{1,13},{2,98},{3,15},{4,100},{5,1},{6,102},{7,3},{8,104},{9... | collective-permute-start | bytes 2359304 | tf_op jit(solution)/shard_map/ppermute | solution.py:86
  172.8 18.4 %collective-permute-start.24 = (bf16[128,1536]{1,0:T(8,128)(2,1)S(1)}, bf16[128,1536]{1,0:T(8,128)(2,1)S(1)}, u32[]{:S(2)}, u32[]{:S(2)}) collective-permute-start(bf16[128,1536]{1,0:T(8,128)(2,1)S(1)} %add_convert_fusion), channel_id=1, source_target_pairs={{0,2},{2,0},{1,3},{3,1},{4,6},{6,4},{5,7},{7,5},{8,10},{10,8},{9,1... | collective-permute-start | bytes 1179656 | tf_op jit(solution)/shard_map/ppermute | solution.py:101
  189.7 21.2 %collective-permute-start.30 = (bf16[4,48,3072]{2,1,0:T(8,128)(2,1)S(1)}, bf16[4,48,3072]{2,1,0:T(8,128)(2,1)S(1)}, u32[]{:S(2)}, u32[]{:S(2)}) collective-permute-start(bf16[4,48,3072]{2,1,0:T(8,128)(2,1)S(1)} %get-tuple-element.152.refs_10_), channel_id=1, source_target_pairs={{0,4},{1,33},{2,6},{3,35},{4,0},{5,37},{6,2},{7,39},{8,12},{9,41},... | collective-permute-start | bytes 3538952 | tf_op jit(solution)/shard_map/ppermute | solution.py:86
  195.9 18.6 %collective-permute-start.28 = (f32[16,1536]{1,0:T(8,128)S(1)}, f32[16,1536]{1,0:T(8,128)S(1)}, u32[]{:S(2)}, u32[]{:S(2)}) collective-permute-start(f32[16,1536]{1,0:T(8,128)S(1)} %stack_sums.1.refs_20_.refs_1_), channel_id=1, source_target_pairs={{0,1},{1,0},{2,3},{3,2},{4,5},{5,4},{6,7},{7,6},{8,9},{9,8},{10,11... | collective-permute-start | bytes 294920 | tf_op jit(solution)/shard_map/ppermute | solution.py:97
  197.7 23.8 %collective-permute-start.36 = (bf16[384,768]{1,0:T(8,128)(2,1)S(1)}, bf16[384,768]{1,0:T(8,128)(2,1)S(1)}, u32[]{:S(2)}, u32[]{:S(2)}) collective-permute-start(bf16[384,768]{1,0:T(8,128)(2,1)S(1)} %get-tuple-element.167), channel_id=1, source_target_pairs={{0,96},{1,13},{2,98},{3,15},{4,100},{5,1},{6,102},{7,3},{8,104},{9... | collective-permute-start | bytes 1769480 | tf_op jit(solution)/shard_map/ppermute | solution.py:86
  200.4 21.0 %collective-permute-start.35 = (bf16[384,768]{1,0:T(8,128)(2,1)S(1)}, bf16[384,768]{1,0:T(8,128)(2,1)S(1)}, u32[]{:S(2)}, u32[]{:S(2)}) collective-permute-start(bf16[384,768]{1,0:T(8,128)(2,1)S(1)} %get-tuple-element.164.refs_12_), channel_id=1, source_target_pairs={{0,32},{1,5},{2,34},{3,7},{4,36},{5,9},{6,38},{7,11},{8,40},{9,13}... | collective-permute-start | bytes 1769480 | tf_op jit(solution)/shard_map/ppermute | solution.py:86
  200.5 14.1 %collective-permute-start.29 = (f32[16,1536]{1,0:T(8,128)S(1)}, f32[16,1536]{1,0:T(8,128)S(1)}, u32[]{:S(2)}, u32[]{:S(2)}) collective-permute-start(f32[16,1536]{1,0:T(8,128)S(1)} %collective-permute-done.27.refs_2_), channel_id=1, source_target_pairs={{0,1},{1,0},{2,3},{3,2},{4,5},{5,4},{6,7},{7,6},{8,9},{9,8},{10,11... | collective-permute-start | bytes 294920 | tf_op jit(solution)/shard_map/ppermute | solution.py:97
  218.1 42.2 %collective-permute-start.43 = (bf16[768,1024]{1,0:T(8,128)(2,1)S(1)}, bf16[768,1024]{1,0:T(8,128)(2,1)S(1)}, u32[]{:S(2)}, u32[]{:S(2)}) collective-permute-start(bf16[768,1024]{1,0:T(8,128)(2,1)S(1)} %get-tuple-element.183), channel_id=1, source_target_pairs={{0,32},{1,5},{2,34},{3,7},{4,36},{5,9},{6,38},{7,11},{8,40},{9,13}... | collective-permute-start | bytes 4718600 | tf_op jit(solution)/shard_map/ppermute | solution.py:86
  219.4 41.0 %collective-permute-start.44 = (bf16[768,1024]{1,0:T(8,128)(2,1)S(1)}, bf16[768,1024]{1,0:T(8,128)(2,1)S(1)}, u32[]{:S(2)}, u32[]{:S(2)}) collective-permute-start(bf16[768,1024]{1,0:T(8,128)(2,1)S(1)} %get-tuple-element.184), channel_id=1, source_target_pairs={{0,96},{1,13},{2,98},{3,15},{4,100},{5,1},{6,102},{7,3},{8,104},{9... | collective-permute-start | bytes 4718600 | tf_op jit(solution)/shard_map/ppermute | solution.py:86
  227.6 27.8 %collective-permute-start.37 = (bf16[416,1536]{1,0:T(8,128)(2,1)S(1)}, bf16[416,1536]{1,0:T(8,128)(2,1)S(1)}, u32[]{:S(2)}, u32[]{:S(2)}) collective-permute-start(bf16[416,1536]{1,0:T(8,128)(2,1)S(1)} %get-tuple-element.169), channel_id=1, source_target_pairs={{0,32},{1,5},{2,34},{3,7},{4,36},{5,9},{6,38},{7,11},{8,40},{9,13}... | collective-permute-start | bytes 3833864 | tf_op jit(solution)/shard_map/ppermute | solution.py:86
  228.2 27.2 %collective-permute-start.38 = (bf16[416,1536]{1,0:T(8,128)(2,1)S(1)}, bf16[416,1536]{1,0:T(8,128)(2,1)S(1)}, u32[]{:S(2)}, u32[]{:S(2)}) collective-permute-start(bf16[416,1536]{1,0:T(8,128)(2,1)S(1)} %get-tuple-element.170), channel_id=1, source_target_pairs={{0,96},{1,13},{2,98},{3,15},{4,100},{5,1},{6,102},{7,3},{8,104},{9... | collective-permute-start | bytes 3833864 | tf_op jit(solution)/shard_map/ppermute | solution.py:86
  230.8 24.6 %collective-permute-start.34 = (bf16[32,1536]{1,0:T(8,128)(2,1)S(1)}, bf16[32,1536]{1,0:T(8,128)(2,1)S(1)}, u32[]{:S(2)}, u32[]{:S(2)}) collective-permute-start(bf16[32,1536]{1,0:T(8,128)(2,1)S(1)} %merge.1.refs_20_.refs_1_), channel_id=1, source_target_pairs={{0,64},{1,9},{2,66},{3,11},{4,68},{5,13},{6,70},{7,15},{8,72},{9,1... | collective-permute-start | bytes 294920 | tf_op jit(solution)/shard_map/ppermute | solution.py:86
  266.6 12.0 %collective-permute-start.45 = (bf16[768,512]{1,0:T(8,128)(2,1)S(1)}, bf16[768,512]{1,0:T(8,128)(2,1)S(1)}, u32[]{:S(2)}, u32[]{:S(2)}) collective-permute-start(bf16[768,512]{1,0:T(8,128)(2,1)S(1)} %get-tuple-element.186), channel_id=1, source_target_pairs={{0,4},{1,33},{2,6},{3,35},{4,0},{5,37},{6,2},{7,39},{8,12},{9,41},... | collective-permute-start | bytes 2359304 | tf_op jit(solution)/shard_map/ppermute | solution.py:86
  267.5 16.9 %collective-permute-start.48 = (bf16[2,48,3072]{2,1,0:T(8,128)(2,1)S(1)}, bf16[2,48,3072]{2,1,0:T(8,128)(2,1)S(1)}, u32[]{:S(2)}, u32[]{:S(2)}) collective-permute-start(bf16[2,48,3072]{2,1,0:T(8,128)(2,1)S(1)} %get-tuple-element.166.refs_8_), channel_id=1, source_target_pairs={{0,12},{1,97},{2,14},{3,99},{4,8},{5,101},{6,10},{7,103},{8,4},{9,... | collective-permute-start | bytes 1769480 | tf_op jit(solution)/shard_map/ppermute | solution.py:86
  270.6 16.2 %collective-permute-start.39 = (bf16[160,1536]{1,0:T(8,128)(2,1)S(1)}, bf16[160,1536]{1,0:T(8,128)(2,1)S(1)}, u32[]{:S(2)}, u32[]{:S(2)}) collective-permute-start(bf16[160,1536]{1,0:T(8,128)(2,1)S(1)} %get-tuple-element.172), channel_id=1, source_target_pairs={{0,4},{1,33},{2,6},{3,35},{4,8},{5,37},{6,10},{7,39},{8,12},{9,41}... | collective-permute-start | bytes 1474568 | tf_op jit(solution)/shard_map/ppermute | solution.py:86
  270.8 20.6 %collective-permute-start.40 = (bf16[160,1536]{1,0:T(8,128)(2,1)S(1)}, bf16[160,1536]{1,0:T(8,128)(2,1)S(1)}, u32[]{:S(2)}, u32[]{:S(2)}) collective-permute-start(bf16[160,1536]{1,0:T(8,128)(2,1)S(1)} %get-tuple-element.173), channel_id=1, source_target_pairs={{0,8},{1,65},{2,10},{3,67},{4,12},{5,69},{6,14},{7,71},{8,0},{9,73... | collective-permute-start | bytes 1474568 | tf_op jit(solution)/shard_map/ppermute | solution.py:86
  272.2 19.2 %collective-permute-start.41 = (bf16[160,1536]{1,0:T(8,128)(2,1)S(1)}, bf16[160,1536]{1,0:T(8,128)(2,1)S(1)}, u32[]{:S(2)}, u32[]{:S(2)}) collective-permute-start(bf16[160,1536]{1,0:T(8,128)(2,1)S(1)} %get-tuple-element.174), channel_id=1, source_target_pairs={{0,12},{1,97},{2,14},{3,99},{4,0},{5,101},{6,2},{7,103},{8,4},{9,1... | collective-permute-start | bytes 1474568 | tf_op jit(solution)/shard_map/ppermute | solution.py:86
  281.6 18.4 %collective-permute-start.46 = (bf16[768,256]{1,0:T(8,128)(2,1)}, bf16[768,256]{1,0:T(8,128)(2,1)}, u32[]{:S(2)}, u32[]{:S(2)}) collective-permute-start(bf16[768,256]{1,0:T(8,128)(2,1)} %get-tuple-element.188), channel_id=1, source_target_pairs={{0,12},{1,97},{2,14},{3,99},{4,8},{5,101},{6,10},{7,103},{8,4},{9,... | collective-permute-start | bytes 1179656 | tf_op jit(solution)/shard_map/ppermute | solution.py:86
  (133 other events, 846.4 us)
